TPU v7x, 128 devices: a whole 4x4x4 slice. The times are simulated.
128 devices in a mesh: blk: 8 (over x_hi, z), grp: 16 (over y, x_lo, core).
Axes of the slice: x: 4 (x_hi: 2, x_lo: 2; x = x_hi * 2 + x_lo), y: 4, z: 4, core: 2. Of those that a mesh axis runs over, the one named last changes fastest.
Arguments:
- image_tokens: bfloat16 [512, 196, 256], P(('blk', 'grp')), may hold values from -0.375 to 0.375
- text_tokens: bfloat16 [256, 32, 256], P(('blk', 'grp')), may hold values from -0.375 to 0.375
- positives: int32 [512], P(('blk', 'grp')), may hold values from 0 to 255
Outputs:
- row_loss: float32 [512], P(('blk', 'grp'))
- grad_image: float32 [512, 196, 256], P(('blk', 'grp'))
- grad_text: float32 [256, 32, 256], P(('blk', 'grp'))
All inputs are finite; a program needn't handle non-finite values.
Results may differ from a plain program's by a relative error of at most 0.0029.
Values may be sent and summed in bfloat16 or wider, within the bound.
No kernel may reach another device: no remote copies, remote signals or barrier semaphores. Data moves between devices by JAX's collectives and lax.ppermute only.
A program may use at most 64 MiB of HBM per device.

v0:
```python
import functools
import jax
import jax.numpy as jnp
from jax import lax
from jax.experimental import pallas as pl
from jax.experimental.pallas import tpu as pltpu
from jax.sharding import PartitionSpec as P

SCORE_SCALE = 16.0
LOGIT_SCALE = 4.0
LOGIT_BIAS = -25.5
LOG2E = 1.4426950408889634
EXTRA = 16
CHUNK = 1024
AXES = ("blk", "grp")
CORE, X_LOW, X_HIGH = 1, 2, 64
NEIGHBOURS = (X_LOW, X_LOW | X_HIGH, X_HIGH)
CLASS = CORE | X_LOW | X_HIGH


def pair_kernel(*refs, count, chunk, img_tok, txt_tok, first, last):
    refs = list(refs)
    img_refs = [refs.pop(0) for _ in range(2 * count)]
    txt_in, ids_ref = refs.pop(0), refs.pop(0)
    gin_ref = None if first else refs.pop(0)
    gi_refs = [refs.pop(0) for _ in range(2 * count)]
    gt_ref = refs.pop(0)
    txt_ref = refs.pop(0) if first else txt_in
    acc_ref, lr_ref, lc_ref, turn_ref, *more = refs
    x_refs, xt_refs, e_refs, r_refs, c_refs = [more[count * i : count * (i + 1)] for i in range(5)]
    rows = img_refs[0].shape[0] - EXTRA
    cols, dim = txt_ref.shape
    texts = cols // txt_tok
    steps = cols // chunk
    groups = rows // 8
    every = range(0, cols, chunk)

    def lanes(x):
        return [x[:, 128 * i : 128 * (i + 1)] for i in range(x.shape[1] // 128)]

    def fold_rows(x, op):
        return op(x.reshape(2, groups, 8, x.shape[1]), axis=1)

    def spread(x):
        return jnp.broadcast_to(x[:, None], (2, groups) + x.shape[1:]).reshape(2 * rows, x.shape[2])

    def over_lanes(x, op):
        shift = 64
        while shift >= texts:
            x = op(x, pltpu.roll(x, shift, x.ndim - 1))
            shift //= 2
        return x

    def over_rows(x, op):
        return op(x, pltpu.roll(x, 4, 1))

    def over_tokens(x):
        return over_lanes(sum(x[:, :, 128 * i : 128 * (i + 1)] for i in range(cols // 128)), jnp.add)

    def scores(p, at):
        return lax.dot_general(
            x_refs[p][...], txt_ref[pl.ds(at, chunk), :], (((1,), (1,)), ((), ())), preferred_element_type=jnp.float32
        )

    def verdicts(p, row_lse_sum, col_lse_sum):
        logits = LOGIT_SCALE * (row_lse_sum * (0.5 / img_tok) + col_lse_sum * (0.5 / txt_tok)) + LOGIT_BIAS
        positives = jnp.stack([img_refs[2 * p + b][rows:, :128].astype(jnp.float32)[:8] for b in range(2)])
        sign = jnp.where(ids_ref[...][None] == positives, 1.0, -1.0).astype(jnp.float32)
        z = -sign * logits
        slope = -sign * (SCORE_SCALE * LOGIT_SCALE) / (1.0 + jnp.exp(-z))
        loss = jnp.maximum(z, 0.0) + jnp.log1p(jnp.exp(-jnp.abs(z)))
        loss = jnp.sum(loss, axis=2, keepdims=True) * (texts / 128)
        coarse = loss.astype(jnp.bfloat16).astype(jnp.float32)
        part = jnp.where(lax.broadcasted_iota(jnp.int32, (2, 8, 1), 1) < 4, coarse, loss - coarse)
        none = jnp.zeros_like(part[0])
        for b, found in enumerate(([part[0], none], [none, part[1]])):
            gi_ref = gi_refs[2 * p + b]
            gi_ref[rows:] = jnp.broadcast_to(jnp.concatenate(found, axis=0), (EXTRA, dim)).astype(gi_ref.dtype)
        return slope

    def weights(p, at, width):
        parts = []
        for i in range(width // 128):
            e = e_refs[p][:, pl.ds(at + 128 * i, 128)].reshape(2, groups, 8, 128)
            factor = r_refs[p][...].reshape(2, groups, 8, 128) + c_refs[p][:, :, pl.ds(at + 128 * i, 128)][:, None]
            parts.append((e * factor).reshape(2 * rows, 128).astype(jnp.bfloat16))
        return jnp.concatenate(parts, axis=1)

    def store_image_grad(p, grad):
        for b in range(2):
            gi_ref = gi_refs[2 * p + b]
            gi_ref[:rows] = grad[b * rows : (b + 1) * rows].astype(gi_ref.dtype)

    def fast_scores(p):
        for at in every:
            e = jnp.exp2(scores(p, at) * (SCORE_SCALE * LOG2E))
            e_refs[p][:, at : at + chunk] = e
            part = functools.reduce(jnp.add, lanes(e))
            r_refs[p][...] = part if at == 0 else r_refs[p][...] + part
            c_refs[p][:, :, at : at + chunk] = fold_rows(e, jnp.sum)

    def fast_factors(p):
        row_log = jnp.log2(over_lanes(r_refs[p][...], jnp.add))
        col_log = jnp.log2(over_rows(c_refs[p][...], jnp.add))
        low = jnp.minimum(jnp.min(fold_rows(row_log, jnp.min)), jnp.min(col_log))
        high = jnp.maximum(jnp.max(fold_rows(row_log, jnp.max)), jnp.max(col_log))
        row_lse = over_rows(fold_rows(row_log, jnp.sum), jnp.add)
        slope = verdicts(p, row_lse * (1.0 / LOG2E), over_tokens(col_log) * (1.0 / LOG2E))
        r_refs[p][...] = spread(slope * (0.5 / img_tok)) * jnp.exp2(-row_log)
        c_refs[p][...] = jnp.concatenate([slope * (0.5 / txt_tok)] * (cols // 128), axis=2) * jnp.exp2(-col_log)
        return jnp.logical_and(low > -100.0, high < 100.0)

    def fast_gradients(p):
        w = weights(p, 0, cols)
        store_image_grad(p, jnp.dot(w, txt_ref[...], preferred_element_type=jnp.float32))
        part = jnp.dot(xt_refs[p][...], w, preferred_element_type=jnp.float32)
        acc_ref[...] = part if p == 0 else acc_ref[...] + part

    def slow_pair(p):
        e_ref, r_ref, c_ref = e_refs[p], r_refs[p], c_refs[p]
        r_ref[...] = jnp.full_like(r_ref, -jnp.inf)

        def tops(j, carry):
            at = pl.multiple_of(j * chunk, chunk)
            s = SCORE_SCALE * scores(p, at)
            e_ref[:, pl.ds(at, chunk)] = s
            r_ref[...] = functools.reduce(jnp.maximum, lanes(s) + [r_ref[...]])
            c_ref[:, :, pl.ds(at, chunk)] = fold_rows(s, jnp.max)
            return carry

        lax.fori_loop(0, steps, tops, 0)
        r_ref[...] = over_lanes(r_ref[...], jnp.maximum)
        c_ref[...] = over_rows(c_ref[...], jnp.maximum)
        lr_ref[...] = jnp.zeros_like(lr_ref)

        def sums(j, carry):
            at = pl.multiple_of(j * 128, 128)
            s = e_ref[:, pl.ds(at, 128)]
            lr_ref[...] += jnp.exp(s - r_ref[...])
            lc_ref[:, :, pl.ds(at, 128)] = fold_rows(jnp.exp(s - spread(c_ref[:, :, pl.ds(at, 128)])), jnp.sum)
            return carry

        lax.fori_loop(0, cols // 128, sums, 0)
        lr_ref[...] = r_ref[...] + jnp.log(over_lanes(lr_ref[...], jnp.add))
        lc_ref[...] = c_ref[...] + jnp.log(over_rows(lc_ref[...], jnp.add))

        def mixtures(j, carry):
            at = pl.multiple_of(j * 128, 128)
            s = e_ref[:, pl.ds(at, 128)]
            by_col = jnp.exp(s - spread(lc_ref[:, :, pl.ds(at, 128)]))
            e_ref[:, pl.ds(at, 128)] = jnp.exp(s - lr_ref[...]) * (0.5 / img_tok) + by_col * (0.5 / txt_tok)
            return carry

        lax.fori_loop(0, cols // 128, mixtures, 0)
        slope = verdicts(p, over_rows(fold_rows(lr_ref[...], jnp.sum), jnp.add), over_tokens(lc_ref[...]))
        r_ref[...] = spread(slope)
        c_ref[...] = jnp.zeros_like(c_ref)

        def gradients(j, grad):
            at = pl.multiple_of(j * 256, 256)
            w = weights(p, at, 256)
            acc_ref[:, pl.ds(at, 256)] += jnp.dot(xt_refs[p][...], w, preferred_element_type=jnp.float32)
            return grad + jnp.dot(w, txt_ref[pl.ds(at, 256), :], preferred_element_type=jnp.float32)

        store_image_grad(p, lax.fori_loop(0, cols // 256, gradients, jnp.zeros((2 * rows, dim), jnp.float32)))

    if first:
        for h, part in enumerate(lanes(txt_in[...].astype(jnp.float32))):
            turn_ref[h] = part
        for q in range(txt_tok):
            picked = [turn_ref[h, pl.ds(q, texts, stride=txt_tok), :] for h in range(dim // 128)]
            txt_ref[q * texts : (q + 1) * texts, :] = jnp.concatenate(picked, axis=1).astype(jnp.bfloat16)
    for p in range(count):
        for b in range(2):
            x_refs[p][b * rows : (b + 1) * rows] = img_refs[2 * p + b][:rows]
        xt_refs[p][...] = x_refs[p][...].T
    safe = None
    for p in range(count + 1):
        if p < count:
            fast_scores(p)
        if p > 0:
            fine = fast_factors(p - 1)
            safe = fine if safe is None else jnp.logical_and(safe, fine)
            fast_gradients(p - 1)

    @pl.when(jnp.logical_not(safe))
    def _():
        acc_ref[...] = jnp.zeros_like(acc_ref)
        for p in range(count):
            slow_pair(p)

    total = acc_ref[...] if first else acc_ref[...] + gin_ref[...]
    if last:
        for j in range(cols // 128):
            turned = total[:, 128 * j : 128 * (j + 1)].T
            for i in range(128 // texts):
                for h, part in enumerate(lanes(turned[i * texts : (i + 1) * texts])):
                    turn_ref[h, pl.ds(j * (128 // texts) + i, texts, stride=txt_tok), :] = part
        gt_ref[...] = jnp.concatenate([turn_ref[h] for h in range(dim // 128)], axis=1).astype(gt_ref.dtype)
    else:
        gt_ref[...] = total


def pair_call(images, texts, ids, carried, img_tok, txt_tok, last, chunk=CHUNK):
    tall, dim = images[0].shape
    count = len(images) // 2
    rows = tall - EXTRA
    cols = texts.shape[0]
    first = carried is None
    out_shape = [jax.ShapeDtypeStruct((tall, dim), jnp.bfloat16 if b % 2 else jnp.float32) for b in range(2 * count)]
    out_shape.append(
        jax.ShapeDtypeStruct((cols, dim), jnp.bfloat16) if last else jax.ShapeDtypeStruct((dim, cols), jnp.float32)
    )
    if first:
        out_shape.append(jax.ShapeDtypeStruct((cols, dim), jnp.bfloat16))
    scratch = [
        pltpu.VMEM((dim, cols), jnp.float32),
        pltpu.VMEM((2 * rows, 128), jnp.float32),
        pltpu.VMEM((2, 8, cols), jnp.float32),
        pltpu.VMEM((dim // 128, cols, 128), jnp.float32),
    ]
    scratch += [pltpu.VMEM((2 * rows, dim), jnp.bfloat16)] * count
    scratch += [pltpu.VMEM((dim, 2 * rows), jnp.bfloat16)] * count
    scratch += [pltpu.VMEM((2 * rows, cols), jnp.float32)] * count
    scratch += [pltpu.VMEM((2 * rows, 128), jnp.float32)] * count
    scratch += [pltpu.VMEM((2, 8, cols), jnp.float32)] * count
    operands = [*images, texts, ids] + ([] if first else [carried])
    return pl.pallas_call(
        functools.partial(
            pair_kernel, count=count, chunk=chunk, img_tok=img_tok, txt_tok=txt_tok, first=first, last=last
        ),
        out_shape=out_shape,
        scratch_shapes=scratch,
        compiler_params=pltpu.CompilerParams(vmem_limit_bytes=40 * 2**20),
    )(*operands)


def body(image_tokens, text_tokens, positives):
    devices = lax.axis_size(AXES)
    own_images, img_tok, dim = image_tokens.shape
    own_texts, txt_tok, _ = text_tokens.shape
    rows = own_images * img_tok
    place = lax.axis_index("blk") * lax.axis_size("grp") + lax.axis_index("grp")
    classes = sorted({i & CLASS for i in range(devices)})
    across_texts = [[i for i in range(devices) if i & CLASS == k] for k in classes]
    peers = len(across_texts[0])

    def swapped(x, bits):
        return lax.ppermute(x, AXES, [(i, i ^ bits) for i in range(devices)])

    labels = jnp.broadcast_to(jnp.tile(positives.astype(jnp.bfloat16), EXTRA // own_images)[:, None], (EXTRA, dim))
    own = jnp.concatenate([image_tokens.transpose(1, 0, 2).reshape(rows, dim), labels], axis=0)
    text_tokens, own = lax.optimization_barrier((text_tokens, own))
    over = {bits: swapped(own, bits) for bits in NEIGHBOURS}

    sent = jnp.broadcast_to(text_tokens[None], (peers, own_texts, txt_tok, dim))
    texts = lax.all_to_all(sent, AXES, 0, 0, tiled=True, axis_index_groups=across_texts)
    X_BOTH = X_LOW | X_HIGH
    over[0] = own
    beside = {bits: swapped(x, CORE) for bits, x in over.items()}
    texts = texts.reshape(peers * own_texts * txt_tok, dim)
    lane = jnp.arange(128, dtype=jnp.int32) % (peers * own_texts)
    ids = ((lane // own_texts) * 4 + (place & CLASS)) * own_texts + lane % own_texts
    ids = jnp.broadcast_to(ids.astype(jnp.float32)[None], (8, 128))

    def summed(near, met):
        return (near + met.astype(jnp.float32)).astype(jnp.bfloat16)

    found, gathered = {}, None

    def work(pairs, last=False):
        nonlocal gathered, texts
        images = [x[bits] for bits in pairs for x in (over, beside)]
        out = pair_call(images, texts, ids, gathered, img_tok, txt_tok, last)
        texts = texts if gathered is not None else out[-1]
        gathered = out[len(images)]
        return out[: len(images)]

    near, far = work([X_LOW])
    found[X_LOW] = (near, swapped(far, CORE))
    near, far = work([X_BOTH])
    found[X_BOTH] = (near, swapped(far, CORE))
    *sent, gathered = lax.optimization_barrier((summed(*found[X_LOW]), summed(*found[X_BOTH]), gathered))
    back = [swapped(sent[0], X_LOW), swapped(sent[1], X_BOTH)]
    out = work([X_HIGH, 0], last=True)
    back, out, gathered = lax.optimization_barrier((back, out, gathered))
    found[X_HIGH] = (out[0], swapped(out[1], CORE))
    found[0] = (out[2], swapped(out[3], CORE))
    back.append(swapped(summed(*found[X_HIGH]), X_HIGH))

    grad = found[0][0] + found[0][1].astype(jnp.float32)
    for part in back:
        grad = grad + part.astype(jnp.float32)
    grad_image = grad[:rows].reshape(img_tok, own_images, dim).transpose(1, 0, 2)
    row_loss = jnp.sum(grad[rows:, 0].reshape(EXTRA // own_images, own_images), axis=0)

    sent = gathered.reshape(peers, own_texts, txt_tok, dim)
    parts = lax.all_to_all(sent, AXES, 0, 0, tiled=True, axis_index_groups=across_texts)
    grad_text = jnp.sum(parts.astype(jnp.float32), axis=0)
    return (row_loss, grad_image, grad_text)


def solution(mesh):
    placed = (P(AXES, None, None), P(AXES, None, None), P(AXES))
    return jax.shard_map(
        body,
        mesh=mesh,
        in_specs=placed,
        out_specs=(P(AXES), P(AXES, None, None), P(AXES, None, None)),
        check_vma=False,
    )
```

profile of v0, /device:TPU:1, one launch (start us, length us, event | category | flops | bytes accessed | tf_op | source)
XLA Modules:
  0.0 107.9 jit_solution(12846972352695165145)
XLA Ops:
  0.6 0.7 convert_element_type.43
  1.3 0.1 reshape.66
  1.4 1.1 %reshape.61 = bf16[784,256]{1,0:T(8,128)(2,1)S(1)} reshape(bf16[196,4,256]{2,1,0:T(4,128)(2,1)} %bitcast.6) | data formatting | bytes 802816 | tf_op jit(solution)/shard_map/reshape | solution.py:252
  2.5 0.1 pad.1.clone
  2.6 0.2 pad_maximum_fusion.refs_2_
  2.7 2.1 %collective-permute-start = (bf16[800,256]{1,0:T(8,128)(2,1)S(1)}, bf16[800,256]{1,0:T(8,128)(2,1)S(1)}, u32[]{:S(2)}, u32[]{:S(2)}) collective-permute-start(bf16[800,256]{1,0:T(8,128)(2,1)S(1)} %pad_maximum_fusion.refs_2_), channel_id=1, source_target_pairs={{0,2},{1,3},{2,0},{3,1},{4,6},{5,7},{6,4},{7,5},{8,10},{9,11},{10,... | collective-permute-start | bytes 1228808 | tf_op jit(solution)/shard_map/ppermute | solution.py:249
  4.9 1.8 %collective-permute-start.3 = (bf16[800,256]{1,0:T(8,128)(2,1)S(1)}, bf16[800,256]{1,0:T(8,128)(2,1)S(1)}, u32[]{:S(2)}, u32[]{:S(2)}) collective-permute-start(bf16[800,256]{1,0:T(8,128)(2,1)S(1)} %pad_maximum_fusion.refs_2_), channel_id=1, source_target_pairs={{0,66},{1,67},{2,64},{3,65},{4,70},{5,71},{6,68},{7,69},{8,74},{9,... | collective-permute-start | bytes 1228808 | tf_op jit(solution)/shard_map/ppermute | solution.py:249
  6.7 0.9 broadcast_in_dim.10
  7.5 7.8 %all-to-all-start = ((bf16[16,2,32,256]{3,2,1,0:T(8,128)(2,1)}), bf16[16,2,32,256]{3,2,1,0:T(8,128)(2,1)S(1)}, u32[]{:S(2)}, u32[]{:S(2)}) async-start(bf16[16,2,32,256]{3,2,1,0:T(8,128)(2,1)} %broadcast_in_dim.10), calls=%async_computation | async-start | bytes 1048576 | tf_op jit(solution)/shard_map/all_to_all | solution.py:257
  15.3 0.0 collective-permute-done.refs_0_
  15.3 1.6 %collective-permute-start.1 = (bf16[800,256]{1,0:T(8,128)(2,1)S(1)}, bf16[800,256]{1,0:T(8,128)(2,1)S(1)}, u32[]{:S(2)}, u32[]{:S(2)}) collective-permute-start(bf16[800,256]{1,0:T(8,128)(2,1)S(1)} %collective-permute-done.refs_0_), channel_id=1, source_target_pairs={{0,1},{1,0},{2,3},{3,2},{4,5},{5,4},{6,7},{7,6},{8,9},{9,8},{10,11... | collective-permute-start | bytes 1228808 | tf_op jit(solution)/shard_map/ppermute | solution.py:249
  16.9 0.0 collective-permute-done.3.refs_0_
  16.9 1.0 collective-permute-start.4
  18.0 1.2 %collective-permute-start.8 = (bf16[800,256]{1,0:T(8,128)(2,1)S(1)}, bf16[800,256]{1,0:T(8,128)(2,1)S(1)}, u32[]{:S(2)}, u32[]{:S(2)}) collective-permute-start(bf16[800,256]{1,0:T(8,128)(2,1)S(1)} %pad_maximum_fusion.refs_2_), channel_id=1, source_target_pairs={{0,64},{1,65},{2,66},{3,67},{4,68},{5,69},{6,70},{7,71},{8,72},{9,... | collective-permute-start | bytes 1228808 | tf_op jit(solution)/shard_map/ppermute | solution.py:249
  19.2 6.2 %all-to-all-done = bf16[16,2,32,256]{3,2,1,0:T(8,128)(2,1)S(1)} async-done(((bf16[16,2,32,256]{3,2,1,0:T(8,128)(2,1)}), bf16[16,2,32,256]{3,2,1,0:T(8,128)(2,1)S(1)}, u32[]{:S(2)}, u32[]{:S(2)}) %all-to-all-start) | async-done | bytes 524320 | tf_op jit(solution)/shard_map/all_to_all | solution.py:257
  25.4 0.0 collective-permute-done.1.refs_1_
  25.4 4.4 %shard_map.58 = (f32[800,256]{1,0:T(8,128)S(1)}, bf16[800,256]{1,0:T(8,128)(2,1)S(1)}, f32[256,1024]{1,0:T(8,128)S(1)}, bf16[1024,256]{1,0:T(8,128)(2,1)S(1)}) custom-call(bf16[800,256]{1,0:T(8,128)(2,1)S(1)} %collective-permute-done.refs_0_, bf16[800,256]{1,0:T(8,128)(2,1)S(1)} %collective-permute-done.1.refs_1_, bf16[1024,256]{1,0:T(8,128)(2,1)S(1)} %bitcast.4, ...), custom_call_target="tpu_custom_call" | custom-call | tf_op jit(solution)/shard_map/pallas_call | solution.py:228
  29.8 12.1 %collective-permute-start.2 = (bf16[800,256]{1,0:T(8,128)(2,1)S(1)}, bf16[800,256]{1,0:T(8,128)(2,1)S(1)}, u32[]{:S(2)}, u32[]{:S(2)}) collective-permute-start(bf16[800,256]{1,0:T(8,128)(2,1)S(1)} %get-tuple-element.30), channel_id=1, source_target_pairs={{0,1},{1,0},{2,3},{3,2},{4,5},{5,4},{6,7},{7,6},{8,9},{9,8},{10,11... | collective-permute-start | bytes 1228808 | tf_op jit(solution)/shard_map/ppermute | solution.py:249
  41.9 0.0 collective-permute-done.4.refs_1_
  41.9 3.8 %shard_map.59 = (f32[800,256]{1,0:T(8,128)S(1)}, bf16[800,256]{1,0:T(8,128)(2,1)S(1)}, f32[256,1024]{1,0:T(8,128)S(1)}) custom-call(bf16[800,256]{1,0:T(8,128)(2,1)S(1)} %collective-permute-done.3.refs_0_, bf16[800,256]{1,0:T(8,128)(2,1)S(1)} %collective-permute-done.4.refs_1_, bf16[1024,256]{1,0:T(8,128)(2,1)S(1)} %get-tuple-element.31.refs_2_.refs_4_, ...), custom_call_target="tpu_custom_call" | custom-call | tf_op jit(solution)/shard_map/pallas_call | solution.py:228
  45.7 9.5 %collective-permute-start.5 = (bf16[800,256]{1,0:T(8,128)(2,1)S(1)}, bf16[800,256]{1,0:T(8,128)(2,1)S(1)}, u32[]{:S(2)}, u32[]{:S(2)}) collective-permute-start(bf16[800,256]{1,0:T(8,128)(2,1)S(1)} %get-tuple-element.34), channel_id=1, source_target_pairs={{0,1},{1,0},{2,3},{3,2},{4,5},{5,4},{6,7},{7,6},{8,9},{9,8},{10,11... | collective-permute-start | bytes 1228808 | tf_op jit(solution)/shard_map/ppermute | solution.py:249
  55.2 0.1 collective-permute-start.10
  55.3 0.4 collective-permute-start.9
  55.7 0.0 collective-permute-done.2
  55.8 0.1 add_convert_fusion.2
  55.9 0.7 collective-permute-done.5
  56.6 0.1 add_convert_fusion.1
  56.7 0.1 collective-permute-start.6
  56.8 0.9 collective-permute-start.7
  57.7 0.0 collective-permute-done.10.refs_3_
  57.7 0.1 collective-permute-done.9.refs_1_
  57.8 8.9 %shard_map.60 = (f32[800,256]{1,0:T(8,128)S(1)}, bf16[800,256]{1,0:T(8,128)(2,1)S(1)}, f32[800,256]{1,0:T(8,128)S(1)}, bf16[800,256]{1,0:T(8,128)(2,1)S(1)}, bf16[1024,256]{1,0:T(8,128)(2,1)}) custom-call(bf16[800,256]{1,0:T(8,128)(2,1)S(1)} %collective-permute-done.8.refs_0_, bf16[800,256]{1,0:T(8,128)(2,1)S(1)} %collective-permute-done.9.refs_1_, ...), custom_call_target="tpu_custom_call" | custom-call | tf_op jit(solution)/shard_map/pallas_call | solution.py:228
  66.7 0.8 collective-permute-done.6
  67.5 1.5 %collective-permute-done.7 = bf16[800,256]{1,0:T(8,128)(2,1)S(1)} collective-permute-done((bf16[800,256]{1,0:T(8,128)(2,1)S(1)}, bf16[800,256]{1,0:T(8,128)(2,1)S(1)}, u32[]{:S(2)}, u32[]{:S(2)}) %collective-permute-start.7) | collective-permute-done | bytes 409632 | tf_op jit(solution)/shard_map/ppermute | solution.py:249
  69.0 17.5 %collective-permute-start.12 = (bf16[800,256]{1,0:T(8,128)(2,1)S(1)}, bf16[800,256]{1,0:T(8,128)(2,1)}, u32[]{:S(2)}, u32[]{:S(2)}) collective-permute-start(bf16[800,256]{1,0:T(8,128)(2,1)S(1)} %get-tuple-element.49), channel_id=1, source_target_pairs={{0,1},{1,0},{2,3},{3,2},{4,5},{5,4},{6,7},{7,6},{8,9},{9,8},{10,11... | collective-permute-start | bytes 1228808 | tf_op jit(solution)/shard_map/ppermute | solution.py:249
  86.5 3.6 %all-to-all-start.1 = ((bf16[16,2,32,256]{3,2,1,0:T(8,128)(2,1)}), bf16[16,2,32,256]{3,2,1,0:T(8,128)(2,1)S(1)}, u32[]{:S(2)}, u32[]{:S(2)}) async-start(bf16[16,2,32,256]{3,2,1,0:T(8,128)(2,1)} %bitcast.3), calls=%async_computation.1 | async-start | bytes 1048576 | tf_op jit(solution)/shard_map/all_to_all | solution.py:298
  90.1 0.9 collective-permute-start.11
  91.0 1.1 %add_convert_fusion = bf16[800,256]{1,0:T(8,128)(2,1)S(1)} fusion(f32[800,256]{1,0:T(8,128)S(1)} %get-tuple-element.48, bf16[800,256]{1,0:T(8,128)(2,1)} %collective-permute-done.12), kind=kLoop, calls=%fused_computation.2 | loop fusion | flops 614400 | bytes 1638400 | tf_op jit(solution)/shard_map/convert_element_type | solution.py:267
  92.2 2.4 %collective-permute-start.13 = (bf16[800,256]{1,0:T(8,128)(2,1)S(1)}, bf16[800,256]{1,0:T(8,128)(2,1)S(1)}, u32[]{:S(2)}, u32[]{:S(2)}) collective-permute-start(bf16[800,256]{1,0:T(8,128)(2,1)S(1)} %add_convert_fusion), channel_id=1, source_target_pairs={{0,64},{1,65},{2,66},{3,67},{4,68},{5,69},{6,70},{7,71},{8,72},{9,... | collective-permute-start | bytes 1228808 | tf_op jit(solution)/shard_map/ppermute | solution.py:249
  94.6 6.1 %all-to-all-done.1 = bf16[16,2,32,256]{3,2,1,0:T(8,128)(2,1)S(1)} async-done(((bf16[16,2,32,256]{3,2,1,0:T(8,128)(2,1)}), bf16[16,2,32,256]{3,2,1,0:T(8,128)(2,1)S(1)}, u32[]{:S(2)}, u32[]{:S(2)}) %all-to-all-start.1) | async-done | bytes 524320 | tf_op jit(solution)/shard_map/all_to_all | solution.py:298
  100.7 0.7 convert_reduce_fusion
  101.4 3.5 %collective-permute-done.13 = bf16[800,256]{1,0:T(8,128)(2,1)S(1)} collective-permute-done((bf16[800,256]{1,0:T(8,128)(2,1)S(1)}, bf16[800,256]{1,0:T(8,128)(2,1)S(1)}, u32[]{:S(2)}, u32[]{:S(2)}) %collective-permute-start.13) | collective-permute-done | bytes 409632 | tf_op jit(solution)/shard_map/ppermute | solution.py:249
  104.8 1.2 %convert_add_fusion = f32[800,256]{1,0:T(8,128)S(1)} fusion(bf16[800,256]{1,0:T(8,128)(2,1)S(1)} %collective-permute-done.13, bf16[800,256]{1,0:T(8,128)(2,1)S(1)} %copy-done.3, bf16[800,256]{1,0:T(8,128)(2,1)S(1)} %copy-done.1, f32[800,256]{1,0:T(8,128)S(1)} %get-tuple-element.44, bf16[800,256]{1,0:T(8,128)(2,1)} %collective-permute-done.11), kind=kLoop, calls=%fused_computation.1 | loop fusion | flops 1638400 | bytes 3276800 | tf_op jit(solution)/shard_map/add | solution.py:293
  106.0 0.1 slice_reduce_fusion
  106.2 0.1 slice.9
  106.2 1.1 %reshape.63 = f32[196,4,256]{2,1,0:T(4,128)} reshape(f32[784,256]{1,0:T(8,128)S(1)} %slice.9) | data formatting | bytes 1605632 | tf_op jit(solution)/shard_map/reshape | solution.py:294
  107.3 0.1 reshape_squeeze.3
  107.4 0.5 reduce_sum.18
  (16 shorter events, 0.0 us)
Async XLA Ops:
  2.6 4.1 %copy-start.4 = (bf16[2,32,256]{2,1,0:T(8,128)(2,1)S(1)}, bf16[2,32,256]{2,1,0:T(8,128)(2,1)}, u32[]{:S(2)}) copy-start(bf16[2,32,256]{2,1,0:T(8,128)(2,1)} %param.4) | copy-start | bytes 98308
  2.7 12.6 %collective-permute-start = (bf16[800,256]{1,0:T(8,128)(2,1)S(1)}, bf16[800,256]{1,0:T(8,128)(2,1)S(1)}, u32[]{:S(2)}, u32[]{:S(2)}) collective-permute-start(bf16[800,256]{1,0:T(8,128)(2,1)S(1)} %pad_maximum_fusion.refs_2_), channel_id=1, source_target_pairs={{0,2},{1,3},{2,0},{3,1},{4,6},{5,7},{6,4},{7,5},{8,10},{9,11},{10,... | collective-permute-start | bytes 1228808 | tf_op jit(solution)/shard_map/ppermute | solution.py:249
  4.9 12.1 %collective-permute-start.3 = (bf16[800,256]{1,0:T(8,128)(2,1)S(1)}, bf16[800,256]{1,0:T(8,128)(2,1)S(1)}, u32[]{:S(2)}, u32[]{:S(2)}) collective-permute-start(bf16[800,256]{1,0:T(8,128)(2,1)S(1)} %pad_maximum_fusion.refs_2_), channel_id=1, source_target_pairs={{0,66},{1,67},{2,64},{3,65},{4,70},{5,71},{6,68},{7,69},{8,74},{9,... | collective-permute-start | bytes 1228808 | tf_op jit(solution)/shard_map/ppermute | solution.py:249
  7.5 17.9 %all-to-all-start = ((bf16[16,2,32,256]{3,2,1,0:T(8,128)(2,1)}), bf16[16,2,32,256]{3,2,1,0:T(8,128)(2,1)S(1)}, u32[]{:S(2)}, u32[]{:S(2)}) async-start(bf16[16,2,32,256]{3,2,1,0:T(8,128)(2,1)} %broadcast_in_dim.10), calls=%async_computation | async-start | bytes 1048576 | tf_op jit(solution)/shard_map/all_to_all | solution.py:257
  15.3 10.1 %collective-permute-start.1 = (bf16[800,256]{1,0:T(8,128)(2,1)S(1)}, bf16[800,256]{1,0:T(8,128)(2,1)S(1)}, u32[]{:S(2)}, u32[]{:S(2)}) collective-permute-start(bf16[800,256]{1,0:T(8,128)(2,1)S(1)} %collective-permute-done.refs_0_), channel_id=1, source_target_pairs={{0,1},{1,0},{2,3},{3,2},{4,5},{5,4},{6,7},{7,6},{8,9},{9,8},{10,11... | collective-permute-start | bytes 1228808 | tf_op jit(solution)/shard_map/ppermute | solution.py:249
  16.9 25.0 %collective-permute-start.4 = (bf16[800,256]{1,0:T(8,128)(2,1)S(1)}, bf16[800,256]{1,0:T(8,128)(2,1)S(1)}, u32[]{:S(2)}, u32[]{:S(2)}) collective-permute-start(bf16[800,256]{1,0:T(8,128)(2,1)S(1)} %collective-permute-done.3.refs_0_), channel_id=1, source_target_pairs={{0,1},{1,0},{2,3},{3,2},{4,5},{5,4},{6,7},{7,6},{8,9},{9,8},{10,11... | collective-permute-start | bytes 1228808 | tf_op jit(solution)/shard_map/ppermute | solution.py:249
  18.0 37.4 %collective-permute-start.8 = (bf16[800,256]{1,0:T(8,128)(2,1)S(1)}, bf16[800,256]{1,0:T(8,128)(2,1)S(1)}, u32[]{:S(2)}, u32[]{:S(2)}) collective-permute-start(bf16[800,256]{1,0:T(8,128)(2,1)S(1)} %pad_maximum_fusion.refs_2_), channel_id=1, source_target_pairs={{0,64},{1,65},{2,66},{3,67},{4,68},{5,69},{6,70},{7,71},{8,72},{9,... | collective-permute-start | bytes 1228808 | tf_op jit(solution)/shard_map/ppermute | solution.py:249
  29.8 25.9 %collective-permute-start.2 = (bf16[800,256]{1,0:T(8,128)(2,1)S(1)}, bf16[800,256]{1,0:T(8,128)(2,1)S(1)}, u32[]{:S(2)}, u32[]{:S(2)}) collective-permute-start(bf16[800,256]{1,0:T(8,128)(2,1)S(1)} %get-tuple-element.30), channel_id=1, source_target_pairs={{0,1},{1,0},{2,3},{3,2},{4,5},{5,4},{6,7},{7,6},{8,9},{9,8},{10,11... | collective-permute-start | bytes 1228808 | tf_op jit(solution)/shard_map/ppermute | solution.py:249
  45.7 10.9 %collective-permute-start.5 = (bf16[800,256]{1,0:T(8,128)(2,1)S(1)}, bf16[800,256]{1,0:T(8,128)(2,1)S(1)}, u32[]{:S(2)}, u32[]{:S(2)}) collective-permute-start(bf16[800,256]{1,0:T(8,128)(2,1)S(1)} %get-tuple-element.34), channel_id=1, source_target_pairs={{0,1},{1,0},{2,3},{3,2},{4,5},{5,4},{6,7},{7,6},{8,9},{9,8},{10,11... | collective-permute-start | bytes 1228808 | tf_op jit(solution)/shard_map/ppermute | solution.py:249
  55.2 2.5 %collective-permute-start.10 = (bf16[800,256]{1,0:T(8,128)(2,1)S(1)}, bf16[800,256]{1,0:T(8,128)(2,1)S(1)}, u32[]{:S(2)}, u32[]{:S(2)}) collective-permute-start(bf16[800,256]{1,0:T(8,128)(2,1)S(1)} %pad_maximum_fusion.refs_2_), channel_id=1, source_target_pairs={{0,1},{1,0},{2,3},{3,2},{4,5},{5,4},{6,7},{7,6},{8,9},{9,8},{10,11... | collective-permute-start | bytes 1228808 | tf_op jit(solution)/shard_map/ppermute | solution.py:249
  55.3 2.4 %collective-permute-start.9 = (bf16[800,256]{1,0:T(8,128)(2,1)S(1)}, bf16[800,256]{1,0:T(8,128)(2,1)S(1)}, u32[]{:S(2)}, u32[]{:S(2)}) collective-permute-start(bf16[800,256]{1,0:T(8,128)(2,1)S(1)} %collective-permute-done.8.refs_0_), channel_id=1, source_target_pairs={{0,1},{1,0},{2,3},{3,2},{4,5},{5,4},{6,7},{7,6},{8,9},{9,8},{10,11... | collective-permute-start | bytes 1228808 | tf_op jit(solution)/shard_map/ppermute | solution.py:249
  56.7 10.8 %collective-permute-start.6 = (bf16[800,256]{1,0:T(8,128)(2,1)S(1)}, bf16[800,256]{1,0:T(8,128)(2,1)S(1)}, u32[]{:S(2)}, u32[]{:S(2)}) collective-permute-start(bf16[800,256]{1,0:T(8,128)(2,1)S(1)} %add_convert_fusion.2), channel_id=1, source_target_pairs={{0,2},{1,3},{2,0},{3,1},{4,6},{5,7},{6,4},{7,5},{8,10},{9,11},{10,... | collective-permute-start | bytes 1228808 | tf_op jit(solution)/shard_map/ppermute | solution.py:249
  56.8 12.2 %collective-permute-start.7 = (bf16[800,256]{1,0:T(8,128)(2,1)S(1)}, bf16[800,256]{1,0:T(8,128)(2,1)S(1)}, u32[]{:S(2)}, u32[]{:S(2)}) collective-permute-start(bf16[800,256]{1,0:T(8,128)(2,1)S(1)} %add_convert_fusion.1), channel_id=1, source_target_pairs={{0,66},{1,67},{2,64},{3,65},{4,70},{5,71},{6,68},{7,69},{8,74},{9,... | collective-permute-start | bytes 1228808 | tf_op jit(solution)/shard_map/ppermute | solution.py:249
  67.5 19.1 %copy-start = (bf16[800,256]{1,0:T(8,128)(2,1)}, bf16[800,256]{1,0:T(8,128)(2,1)S(1)}, u32[]{:S(2)}) copy-start(bf16[800,256]{1,0:T(8,128)(2,1)S(1)} %collective-permute-done.6) | copy-start | bytes 1228804
  69.0 17.6 %copy-start.2 = (bf16[800,256]{1,0:T(8,128)(2,1)}, bf16[800,256]{1,0:T(8,128)(2,1)S(1)}, u32[]{:S(2)}) copy-start(bf16[800,256]{1,0:T(8,128)(2,1)S(1)} %collective-permute-done.7) | copy-start | bytes 1228804
  69.0 22.0 %collective-permute-start.12 = (bf16[800,256]{1,0:T(8,128)(2,1)S(1)}, bf16[800,256]{1,0:T(8,128)(2,1)}, u32[]{:S(2)}, u32[]{:S(2)}) collective-permute-start(bf16[800,256]{1,0:T(8,128)(2,1)S(1)} %get-tuple-element.49), channel_id=1, source_target_pairs={{0,1},{1,0},{2,3},{3,2},{4,5},{5,4},{6,7},{7,6},{8,9},{9,8},{10,11... | collective-permute-start | bytes 1228808 | tf_op jit(solution)/shard_map/ppermute | solution.py:249
  86.5 14.1 %all-to-all-start.1 = ((bf16[16,2,32,256]{3,2,1,0:T(8,128)(2,1)}), bf16[16,2,32,256]{3,2,1,0:T(8,128)(2,1)S(1)}, u32[]{:S(2)}, u32[]{:S(2)}) async-start(bf16[16,2,32,256]{3,2,1,0:T(8,128)(2,1)} %bitcast.3), calls=%async_computation.1 | async-start | bytes 1048576 | tf_op jit(solution)/shard_map/all_to_all | solution.py:298
  90.1 11.2 %collective-permute-start.11 = (bf16[800,256]{1,0:T(8,128)(2,1)S(1)}, bf16[800,256]{1,0:T(8,128)(2,1)}, u32[]{:S(2)}, u32[]{:S(2)}) collective-permute-start(bf16[800,256]{1,0:T(8,128)(2,1)S(1)} %get-tuple-element.45), channel_id=1, source_target_pairs={{0,1},{1,0},{2,3},{3,2},{4,5},{5,4},{6,7},{7,6},{8,9},{9,8},{10,11... | collective-permute-start | bytes 1228808 | tf_op jit(solution)/shard_map/ppermute | solution.py:249
  91.0 13.8 %copy-start.3 = (bf16[800,256]{1,0:T(8,128)(2,1)S(1)}, bf16[800,256]{1,0:T(8,128)(2,1)}, u32[]{:S(2)}) copy-start(bf16[800,256]{1,0:T(8,128)(2,1)} %copy-done.2) | copy-start | bytes 1228804
  92.2 12.7 %copy-start.1 = (bf16[800,256]{1,0:T(8,128)(2,1)S(1)}, bf16[800,256]{1,0:T(8,128)(2,1)}, u32[]{:S(2)}) copy-start(bf16[800,256]{1,0:T(8,128)(2,1)} %copy-done) | copy-start | bytes 1228804
  92.2 12.6 %collective-permute-start.13 = (bf16[800,256]{1,0:T(8,128)(2,1)S(1)}, bf16[800,256]{1,0:T(8,128)(2,1)S(1)}, u32[]{:S(2)}, u32[]{:S(2)}) collective-permute-start(bf16[800,256]{1,0:T(8,128)(2,1)S(1)} %add_convert_fusion), channel_id=1, source_target_pairs={{0,64},{1,65},{2,66},{3,67},{4,68},{5,69},{6,70},{7,71},{8,72},{9,... | collective-permute-start | bytes 1228808 | tf_op jit(solution)/shard_map/ppermute | solution.py:249
where the time goes:
time: 108 us
  starting transfers between devices  63.1 us (58%)
  waiting for transfers between devices  18.9 us (17%)
  Pallas kernels  17 us (16%)
  other arithmetic  4.65 us (4%)
  local copies, waits for them, and re-layouts  3.5 us (3%)
    ppermute x14, starting transfers between devices, swapped(): return lax.ppermute(x, AXES, [(i, i ^ bits) for i in range(devices)])  51.7 us
    pallas_call x3, Pallas kernels, pair_call(): pl.pallas_call(functools.partial(pair_kernel, count=count, chunk=chunk, i...  17 us
    all_to_all x2, waiting for transfers between devices, body(): lax.all_to_all(sent, AXES, 0, 0, tiled=True, axis_index_groups=across_texts)  12.3 us
    all_to_all x2, starting transfers between devices, body(): lax.all_to_all(sent, AXES, 0, 0, tiled=True, axis_index_groups=across_texts)  11.3 us
    ppermute x14, waiting for transfers between devices, swapped(): return lax.ppermute(x, AXES, [(i, i ^ bits) for i in range(devices)])  6.62 us
  transfers between devices with their start and end apart: 16, of which 7 were waited for; matrix products, arithmetic and copies ran while one was open for 3% of the time, Pallas kernels for 16%

commit v1 on v0

--- a/solution.py
+++ b/solution.py
@@ -192,7 +192,7 @@
     total = acc_ref[...] if first else acc_ref[...] + gin_ref[...]
     if last:
         for j in range(cols // 128):
-            turned = total[:, 128 * j : 128 * (j + 1)].T
+            turned = total[:, 128 * j : 128 * (j + 1)].astype(gt_ref.dtype).T.astype(jnp.float32)
             for i in range(128 // texts):
                 for h, part in enumerate(lanes(turned[i * texts : (i + 1) * texts])):
                     turn_ref[h, pl.ds(j * (128 // texts) + i, texts, stride=txt_tok), :] = part
@@ -231,7 +231,7 @@
         ),
         out_shape=out_shape,
         scratch_shapes=scratch,
-        compiler_params=pltpu.CompilerParams(vmem_limit_bytes=40 * 2**20),
+        compiler_params=pltpu.CompilerParams(vmem_limit_bytes=(22 + 12 * (count - 1)) * 2**20),
     )(*operands)
 
 
@@ -250,7 +250,6 @@
 
     labels = jnp.broadcast_to(jnp.tile(positives.astype(jnp.bfloat16), EXTRA // own_images)[:, None], (EXTRA, dim))
     own = jnp.concatenate([image_tokens.transpose(1, 0, 2).reshape(rows, dim), labels], axis=0)
-    text_tokens, own = lax.optimization_barrier((text_tokens, own))
     over = {bits: swapped(own, bits) for bits in NEIGHBOURS}
 
     sent = jnp.broadcast_to(text_tokens[None], (peers, own_texts, txt_tok, dim))
@@ -282,17 +281,20 @@
     found[X_BOTH] = (near, swapped(far, CORE))
     *sent, gathered = lax.optimization_barrier((summed(*found[X_LOW]), summed(*found[X_BOTH]), gathered))
     back = [swapped(sent[0], X_LOW), swapped(sent[1], X_BOTH)]
-    out = work([X_HIGH, 0], last=True)
-    back, out, gathered = lax.optimization_barrier((back, out, gathered))
-    found[X_HIGH] = (out[0], swapped(out[1], CORE))
-    found[0] = (out[2], swapped(out[3], CORE))
+    near, far = work([X_HIGH])
+    met = swapped(far, CORE)
+    out = work([0], last=True)
+    back, met = lax.optimization_barrier((back, met))
+    found[X_HIGH] = (near, met)
+    met, gathered = lax.optimization_barrier((swapped(out[1], CORE), gathered))
+    found[0] = (out[0], met)
     back.append(swapped(summed(*found[X_HIGH]), X_HIGH))
 
     grad = found[0][0] + found[0][1].astype(jnp.float32)
     for part in back:
         grad = grad + part.astype(jnp.float32)
     grad_image = grad[:rows].reshape(img_tok, own_images, dim).transpose(1, 0, 2)
-    row_loss = jnp.sum(grad[rows:, 0].reshape(EXTRA // own_images, own_images), axis=0)
+    row_loss = sum(grad[rows + n : rows + n + own_images, 0] for n in range(0, EXTRA, own_images))
 
     sent = gathered.reshape(peers, own_texts, txt_tok, dim)
     parts = lax.all_to_all(sent, AXES, 0, 0, tiled=True, axis_index_groups=across_texts)

time: 108 us -> 105 us (0.972)
  waiting for transfers between devices: 18.9 us -> 15.1 us
  other arithmetic: 4.65 us -> 3.1 us
  starting transfers between devices: 63.1 us -> 64.6 us
    all_to_all x2, waiting for transfers between devices: 12.3 us -> 7.47 us  [body(): lax.all_to_all(sent, AXES, 0, 0, tiled=True, axis_index_groups=across_texts)]
    ppermute x14, starting transfers between devices: 51.7 us -> 53.2 us  [swapped(): return lax.ppermute(x, AXES, [(i, i ^ bits) for i in range(devices)])]
    pallas_call x3 -> x4, Pallas kernels: 17 us -> 17.8 us  [pair_call(): pl.pallas_call(functools.partial(pair_kernel, count=count, chunk=chunk, i...]
  transfers between devices with their start and end apart: 16 -> 16, of which waited for: 7 -> 4; matrix products, arithmetic and copies ran while one was open for 3% -> 4% of each run, Pallas kernels for 16% -> 17%
where the time goes in v1:
time: 105 us
  starting transfers between devices  64.6 us (62%)
  Pallas kernels  17.8 us (17%)
  waiting for transfers between devices  15.1 us (14%)
  local copies, waits for them, and re-layouts  3.3 us (3%)
  other arithmetic  3.1 us (3%)
    ppermute x14, starting transfers between devices, swapped(): return lax.ppermute(x, AXES, [(i, i ^ bits) for i in range(devices)])  53.2 us
    pallas_call x4, Pallas kernels, pair_call(): pl.pallas_call(functools.partial(pair_kernel, count=count, chunk=chunk, i...  17.8 us
    all_to_all x2, starting transfers between devices, body(): lax.all_to_all(sent, AXES, 0, 0, tiled=True, axis_index_groups=across_texts)  11.3 us
    ppermute x14, waiting for transfers between devices, swapped(): return lax.ppermute(x, AXES, [(i, i ^ bits) for i in range(devices)])  7.6 us
    all_to_all x2, waiting for transfers between devices, body(): lax.all_to_all(sent, AXES, 0, 0, tiled=True, axis_index_groups=across_texts)  7.47 us
  transfers between devices with their start and end apart: 16, of which 4 were waited for; matrix products, arithmetic and copies ran while one was open for 4% of the time, Pallas kernels for 17%

profile of v1, /device:TPU:1, one launch (start us, length us, event | category | flops | bytes accessed | tf_op | source)
XLA Modules:
  0.0 104.6 jit_solution(13811807786267271862)
XLA Ops:
  0.6 1.1 %reshape.64 = bf16[784,256]{1,0:T(8,128)(2,1)S(1)} reshape(bf16[196,4,256]{2,1,0:T(4,128)(2,1)} %bitcast.6) | data formatting | bytes 802816 | tf_op jit(solution)/shard_map/reshape | solution.py:252
  1.8 0.1 reshape.69
  1.9 0.1 pad.1.clone
  1.9 0.2 pad_maximum_fusion.refs_0_
  2.1 2.1 %collective-permute-start.1 = (bf16[800,256]{1,0:T(8,128)(2,1)S(1)}, bf16[800,256]{1,0:T(8,128)(2,1)S(1)}, u32[]{:S(2)}, u32[]{:S(2)}) collective-permute-start(bf16[800,256]{1,0:T(8,128)(2,1)S(1)} %pad_maximum_fusion.refs_0_), channel_id=1, source_target_pairs={{0,2},{1,3},{2,0},{3,1},{4,6},{5,7},{6,4},{7,5},{8,10},{9,11},{10,... | collective-permute-start | bytes 1228808 | tf_op jit(solution)/shard_map/ppermute | solution.py:249
  4.2 1.8 %collective-permute-start.6 = (bf16[800,256]{1,0:T(8,128)(2,1)S(1)}, bf16[800,256]{1,0:T(8,128)(2,1)S(1)}, u32[]{:S(2)}, u32[]{:S(2)}) collective-permute-start(bf16[800,256]{1,0:T(8,128)(2,1)S(1)} %pad_maximum_fusion.refs_0_), channel_id=1, source_target_pairs={{0,66},{1,67},{2,64},{3,65},{4,70},{5,71},{6,68},{7,69},{8,74},{9,... | collective-permute-start | bytes 1228808 | tf_op jit(solution)/shard_map/ppermute | solution.py:249
  6.1 0.9 broadcast_in_dim.10
  6.9 7.8 %all-to-all-start = ((bf16[16,2,32,256]{3,2,1,0:T(8,128)(2,1)}), bf16[16,2,32,256]{3,2,1,0:T(8,128)(2,1)S(1)}, u32[]{:S(2)}, u32[]{:S(2)}) async-start(bf16[16,2,32,256]{3,2,1,0:T(8,128)(2,1)} %broadcast_in_dim.10), calls=%async_computation | async-start | bytes 1048576 | tf_op jit(solution)/shard_map/all_to_all | solution.py:256
  14.7 0.0 collective-permute-done.1.refs_0_
  14.7 1.6 %collective-permute-start.2 = (bf16[800,256]{1,0:T(8,128)(2,1)S(1)}, bf16[800,256]{1,0:T(8,128)(2,1)S(1)}, u32[]{:S(2)}, u32[]{:S(2)}) collective-permute-start(bf16[800,256]{1,0:T(8,128)(2,1)S(1)} %collective-permute-done.1.refs_0_), channel_id=1, source_target_pairs={{0,1},{1,0},{2,3},{3,2},{4,5},{5,4},{6,7},{7,6},{8,9},{9,8},{10,11... | collective-permute-start | bytes 1228808 | tf_op jit(solution)/shard_map/ppermute | solution.py:249
  16.3 0.0 collective-permute-done.6.refs_0_
  16.3 1.0 collective-permute-start.7
  17.3 1.2 %collective-permute-start.3 = (bf16[800,256]{1,0:T(8,128)(2,1)S(1)}, bf16[800,256]{1,0:T(8,128)(2,1)S(1)}, u32[]{:S(2)}, u32[]{:S(2)}) collective-permute-start(bf16[800,256]{1,0:T(8,128)(2,1)S(1)} %pad_maximum_fusion.refs_0_), channel_id=1, source_target_pairs={{0,64},{1,65},{2,66},{3,67},{4,68},{5,69},{6,70},{7,71},{8,72},{9,... | collective-permute-start | bytes 1228808 | tf_op jit(solution)/shard_map/ppermute | solution.py:249
  18.6 6.2 %all-to-all-done = bf16[16,2,32,256]{3,2,1,0:T(8,128)(2,1)S(1)} async-done(((bf16[16,2,32,256]{3,2,1,0:T(8,128)(2,1)}), bf16[16,2,32,256]{3,2,1,0:T(8,128)(2,1)S(1)}, u32[]{:S(2)}, u32[]{:S(2)}) %all-to-all-start) | async-done | bytes 524320 | tf_op jit(solution)/shard_map/all_to_all | solution.py:256
  24.8 0.0 collective-permute-done.2.refs_1_
  24.8 4.4 %shard_map.58 = (f32[800,256]{1,0:T(8,128)S(1)}, bf16[800,256]{1,0:T(8,128)(2,1)S(1)}, f32[256,1024]{1,0:T(8,128)S(1)}, bf16[1024,256]{1,0:T(8,128)(2,1)S(1)}) custom-call(bf16[800,256]{1,0:T(8,128)(2,1)S(1)} %collective-permute-done.1.refs_0_, bf16[800,256]{1,0:T(8,128)(2,1)S(1)} %collective-permute-done.2.refs_1_, bf16[1024,256]{1,0:T(8,128)(2,1)S(1)} %bitcast.4, ...), custom_call_target="tpu_custom_call" | custom-call | tf_op jit(solution)/shard_map/pallas_call | solution.py:228
  29.2 12.1 %collective-permute-start.5 = (bf16[800,256]{1,0:T(8,128)(2,1)S(1)}, bf16[800,256]{1,0:T(8,128)(2,1)S(1)}, u32[]{:S(2)}, u32[]{:S(2)}) collective-permute-start(bf16[800,256]{1,0:T(8,128)(2,1)S(1)} %get-tuple-element.26), channel_id=1, source_target_pairs={{0,1},{1,0},{2,3},{3,2},{4,5},{5,4},{6,7},{7,6},{8,9},{9,8},{10,11... | collective-permute-start | bytes 1228808 | tf_op jit(solution)/shard_map/ppermute | solution.py:249
  41.3 0.0 collective-permute-done.7.refs_1_
  41.3 3.8 %shard_map.59 = (f32[800,256]{1,0:T(8,128)S(1)}, bf16[800,256]{1,0:T(8,128)(2,1)S(1)}, f32[256,1024]{1,0:T(8,128)S(1)}) custom-call(bf16[800,256]{1,0:T(8,128)(2,1)S(1)} %collective-permute-done.6.refs_0_, bf16[800,256]{1,0:T(8,128)(2,1)S(1)} %collective-permute-done.7.refs_1_, bf16[1024,256]{1,0:T(8,128)(2,1)S(1)} %get-tuple-element.24.refs_2_, ...), custom_call_target="tpu_custom_call" | custom-call | tf_op jit(solution)/shard_map/pallas_call | solution.py:228
  45.1 9.5 %collective-permute-start.8 = (bf16[800,256]{1,0:T(8,128)(2,1)S(1)}, bf16[800,256]{1,0:T(8,128)(2,1)S(1)}, u32[]{:S(2)}, u32[]{:S(2)}) collective-permute-start(bf16[800,256]{1,0:T(8,128)(2,1)S(1)} %get-tuple-element.29), channel_id=1, source_target_pairs={{0,1},{1,0},{2,3},{3,2},{4,5},{5,4},{6,7},{7,6},{8,9},{9,8},{10,11... | collective-permute-start | bytes 1228808 | tf_op jit(solution)/shard_map/ppermute | solution.py:249
  54.6 0.1 collective-permute-start
  54.7 0.0 collective-permute-done.3.refs_0_
  54.7 0.4 collective-permute-start.4
  55.1 0.0 collective-permute-done.5
  55.1 0.1 add_convert_fusion.2
  55.2 0.7 collective-permute-done.8
  56.0 0.1 add_convert_fusion.1
  56.1 0.1 collective-permute-start.10
  56.2 0.9 collective-permute-start.11
  57.1 0.0 collective-permute-done.4.refs_1_
  57.2 4.0 %shard_map.60 = (f32[800,256]{1,0:T(8,128)S(1)}, bf16[800,256]{1,0:T(8,128)(2,1)S(1)}, f32[256,1024]{1,0:T(8,128)S(1)}) custom-call(bf16[800,256]{1,0:T(8,128)(2,1)S(1)} %collective-permute-done.3.refs_0_, bf16[800,256]{1,0:T(8,128)(2,1)S(1)} %collective-permute-done.4.refs_1_, bf16[1024,256]{1,0:T(8,128)(2,1)S(1)} %get-tuple-element.24.refs_2_, ...), custom_call_target="tpu_custom_call" | custom-call | tf_op jit(solution)/shard_map/pallas_call | solution.py:228
  61.2 10.4 %collective-permute-start.12 = (bf16[800,256]{1,0:T(8,128)(2,1)S(1)}, bf16[800,256]{1,0:T(8,128)(2,1)S(1)}, u32[]{:S(2)}, u32[]{:S(2)}) collective-permute-start(bf16[800,256]{1,0:T(8,128)(2,1)S(1)} %get-tuple-element.39), channel_id=1, source_target_pairs={{0,1},{1,0},{2,3},{3,2},{4,5},{5,4},{6,7},{7,6},{8,9},{9,8},{10,11... | collective-permute-start | bytes 1228808 | tf_op jit(solution)/shard_map/ppermute | solution.py:249
  71.6 0.0 collective-permute-done.refs_1_
  71.6 5.7 %shard_map.61 = (f32[800,256]{1,0:T(8,128)S(1)}, bf16[800,256]{1,0:T(8,128)(2,1)S(1)}, bf16[1024,256]{1,0:T(8,128)(2,1)}) custom-call(bf16[800,256]{1,0:T(8,128)(2,1)S(1)} %pad_maximum_fusion.refs_0_, bf16[800,256]{1,0:T(8,128)(2,1)S(1)} %collective-permute-done.refs_1_, bf16[1024,256]{1,0:T(8,128)(2,1)S(1)} %get-tuple-element.24.refs_2_, ...), custom_call_target="tpu_custom_call" | custom-call | tf_op jit(solution)/shard_map/pallas_call | solution.py:228
  77.2 9.5 %collective-permute-start.9 = (bf16[800,256]{1,0:T(8,128)(2,1)S(1)}, bf16[800,256]{1,0:T(8,128)(2,1)S(1)}, u32[]{:S(2)}, u32[]{:S(2)}) collective-permute-start(bf16[800,256]{1,0:T(8,128)(2,1)S(1)} %get-tuple-element.34), channel_id=1, source_target_pairs={{0,1},{1,0},{2,3},{3,2},{4,5},{5,4},{6,7},{7,6},{8,9},{9,8},{10,11... | collective-permute-start | bytes 1228808 | tf_op jit(solution)/shard_map/ppermute | solution.py:249
  86.7 0.0 collective-permute-done.10
  86.7 0.0 collective-permute-done.11
  86.7 0.1 add_convert_fusion
  86.8 2.4 %collective-permute-start.13 = (bf16[800,256]{1,0:T(8,128)(2,1)S(1)}, bf16[800,256]{1,0:T(8,128)(2,1)}, u32[]{:S(2)}, u32[]{:S(2)}) collective-permute-start(bf16[800,256]{1,0:T(8,128)(2,1)S(1)} %add_convert_fusion), channel_id=1, source_target_pairs={{0,64},{1,65},{2,66},{3,67},{4,68},{5,69},{6,70},{7,71},{8,72},{9,... | collective-permute-start | bytes 1228808 | tf_op jit(solution)/shard_map/ppermute | solution.py:249
  89.3 0.0 collective-permute-done.9
  89.3 3.6 %all-to-all-start.1 = ((bf16[16,2,32,256]{3,2,1,0:T(8,128)(2,1)}), bf16[16,2,32,256]{3,2,1,0:T(8,128)(2,1)S(1)}, u32[]{:S(2)}, u32[]{:S(2)}) async-start(bf16[16,2,32,256]{3,2,1,0:T(8,128)(2,1)} %bitcast.3), calls=%async_computation.1 | async-start | bytes 1048576 | tf_op jit(solution)/shard_map/all_to_all | solution.py:300
  92.8 6.8 %collective-permute-done.13 = bf16[800,256]{1,0:T(8,128)(2,1)} collective-permute-done((bf16[800,256]{1,0:T(8,128)(2,1)S(1)}, bf16[800,256]{1,0:T(8,128)(2,1)}, u32[]{:S(2)}, u32[]{:S(2)}) %collective-permute-start.13) | collective-permute-done | bytes 409632 | tf_op jit(solution)/shard_map/ppermute | solution.py:249
  99.6 1.2 %convert_add_fusion = f32[800,256]{1,0:T(8,128)S(1)} fusion(bf16[800,256]{1,0:T(8,128)(2,1)} %collective-permute-done.13, bf16[800,256]{1,0:T(8,128)(2,1)S(1)} %collective-permute-done.11, bf16[800,256]{1,0:T(8,128)(2,1)S(1)} %collective-permute-done.10, f32[800,256]{1,0:T(8,128)S(1)} %get-tuple-element.33, bf16[800,256]{1,0:T(8,128)(2,1)S(1)} %collective-permute-done.9), kind=kLoop, calls=%fused_computation.1 | loop fusion | flops 1638400 | bytes 3276800 | tf_op jit(solution)/shard_map/add | solution.py:295
  100.8 0.1 slice.24
  100.9 1.1 %reshape.66 = f32[196,4,256]{2,1,0:T(4,128)} reshape(f32[784,256]{1,0:T(8,128)S(1)} %slice.24) | data formatting | bytes 1605632 | tf_op jit(solution)/shard_map/reshape | solution.py:296
  102.0 0.6 fusion
  102.6 1.2 %all-to-all-done.1 = bf16[16,2,32,256]{3,2,1,0:T(8,128)(2,1)S(1)} async-done(((bf16[16,2,32,256]{3,2,1,0:T(8,128)(2,1)}), bf16[16,2,32,256]{3,2,1,0:T(8,128)(2,1)S(1)}, u32[]{:S(2)}, u32[]{:S(2)}) %all-to-all-start.1) | async-done | bytes 524320 | tf_op jit(solution)/shard_map/all_to_all | solution.py:300
  103.9 0.7 convert_reduce_fusion
  (9 shorter events, 0.0 us)
Async XLA Ops:
  0.6 1.1 %copy-start.1 = (s32[4]{0:T(128)S(1)}, s32[4]{0:T(128)}, u32[]{:S(2)}) copy-start(s32[4]{0:T(128)} %param.5) | copy-start | bytes 52
  1.9 4.1 %copy-start = (bf16[2,32,256]{2,1,0:T(8,128)(2,1)S(1)}, bf16[2,32,256]{2,1,0:T(8,128)(2,1)}, u32[]{:S(2)}) copy-start(bf16[2,32,256]{2,1,0:T(8,128)(2,1)} %param.4) | copy-start | bytes 98308
  2.1 12.6 %collective-permute-start.1 = (bf16[800,256]{1,0:T(8,128)(2,1)S(1)}, bf16[800,256]{1,0:T(8,128)(2,1)S(1)}, u32[]{:S(2)}, u32[]{:S(2)}) collective-permute-start(bf16[800,256]{1,0:T(8,128)(2,1)S(1)} %pad_maximum_fusion.refs_0_), channel_id=1, source_target_pairs={{0,2},{1,3},{2,0},{3,1},{4,6},{5,7},{6,4},{7,5},{8,10},{9,11},{10,... | collective-permute-start | bytes 1228808 | tf_op jit(solution)/shard_map/ppermute | solution.py:249
  4.2 12.1 %collective-permute-start.6 = (bf16[800,256]{1,0:T(8,128)(2,1)S(1)}, bf16[800,256]{1,0:T(8,128)(2,1)S(1)}, u32[]{:S(2)}, u32[]{:S(2)}) collective-permute-start(bf16[800,256]{1,0:T(8,128)(2,1)S(1)} %pad_maximum_fusion.refs_0_), channel_id=1, source_target_pairs={{0,66},{1,67},{2,64},{3,65},{4,70},{5,71},{6,68},{7,69},{8,74},{9,... | collective-permute-start | bytes 1228808 | tf_op jit(solution)/shard_map/ppermute | solution.py:249
  6.9 17.9 %all-to-all-start = ((bf16[16,2,32,256]{3,2,1,0:T(8,128)(2,1)}), bf16[16,2,32,256]{3,2,1,0:T(8,128)(2,1)S(1)}, u32[]{:S(2)}, u32[]{:S(2)}) async-start(bf16[16,2,32,256]{3,2,1,0:T(8,128)(2,1)} %broadcast_in_dim.10), calls=%async_computation | async-start | bytes 1048576 | tf_op jit(solution)/shard_map/all_to_all | solution.py:256
  14.7 10.1 %collective-permute-start.2 = (bf16[800,256]{1,0:T(8,128)(2,1)S(1)}, bf16[800,256]{1,0:T(8,128)(2,1)S(1)}, u32[]{:S(2)}, u32[]{:S(2)}) collective-permute-start(bf16[800,256]{1,0:T(8,128)(2,1)S(1)} %collective-permute-done.1.refs_0_), channel_id=1, source_target_pairs={{0,1},{1,0},{2,3},{3,2},{4,5},{5,4},{6,7},{7,6},{8,9},{9,8},{10,11... | collective-permute-start | bytes 1228808 | tf_op jit(solution)/shard_map/ppermute | solution.py:249
  16.3 25.0 %collective-permute-start.7 = (bf16[800,256]{1,0:T(8,128)(2,1)S(1)}, bf16[800,256]{1,0:T(8,128)(2,1)S(1)}, u32[]{:S(2)}, u32[]{:S(2)}) collective-permute-start(bf16[800,256]{1,0:T(8,128)(2,1)S(1)} %collective-permute-done.6.refs_0_), channel_id=1, source_target_pairs={{0,1},{1,0},{2,3},{3,2},{4,5},{5,4},{6,7},{7,6},{8,9},{9,8},{10,11... | collective-permute-start | bytes 1228808 | tf_op jit(solution)/shard_map/ppermute | solution.py:249
  17.3 37.4 %collective-permute-start.3 = (bf16[800,256]{1,0:T(8,128)(2,1)S(1)}, bf16[800,256]{1,0:T(8,128)(2,1)S(1)}, u32[]{:S(2)}, u32[]{:S(2)}) collective-permute-start(bf16[800,256]{1,0:T(8,128)(2,1)S(1)} %pad_maximum_fusion.refs_0_), channel_id=1, source_target_pairs={{0,64},{1,65},{2,66},{3,67},{4,68},{5,69},{6,70},{7,71},{8,72},{9,... | collective-permute-start | bytes 1228808 | tf_op jit(solution)/shard_map/ppermute | solution.py:249
  29.2 25.9 %collective-permute-start.5 = (bf16[800,256]{1,0:T(8,128)(2,1)S(1)}, bf16[800,256]{1,0:T(8,128)(2,1)S(1)}, u32[]{:S(2)}, u32[]{:S(2)}) collective-permute-start(bf16[800,256]{1,0:T(8,128)(2,1)S(1)} %get-tuple-element.26), channel_id=1, source_target_pairs={{0,1},{1,0},{2,3},{3,2},{4,5},{5,4},{6,7},{7,6},{8,9},{9,8},{10,11... | collective-permute-start | bytes 1228808 | tf_op jit(solution)/shard_map/ppermute | solution.py:249
  45.1 10.9 %collective-permute-start.8 = (bf16[800,256]{1,0:T(8,128)(2,1)S(1)}, bf16[800,256]{1,0:T(8,128)(2,1)S(1)}, u32[]{:S(2)}, u32[]{:S(2)}) collective-permute-start(bf16[800,256]{1,0:T(8,128)(2,1)S(1)} %get-tuple-element.29), channel_id=1, source_target_pairs={{0,1},{1,0},{2,3},{3,2},{4,5},{5,4},{6,7},{7,6},{8,9},{9,8},{10,11... | collective-permute-start | bytes 1228808 | tf_op jit(solution)/shard_map/ppermute | solution.py:249
  54.6 17.0 %collective-permute-start = (bf16[800,256]{1,0:T(8,128)(2,1)S(1)}, bf16[800,256]{1,0:T(8,128)(2,1)S(1)}, u32[]{:S(2)}, u32[]{:S(2)}) collective-permute-start(bf16[800,256]{1,0:T(8,128)(2,1)S(1)} %pad_maximum_fusion.refs_0_), channel_id=1, source_target_pairs={{0,1},{1,0},{2,3},{3,2},{4,5},{5,4},{6,7},{7,6},{8,9},{9,8},{10,11... | collective-permute-start | bytes 1228808 | tf_op jit(solution)/shard_map/ppermute | solution.py:249
  54.7 2.4 %collective-permute-start.4 = (bf16[800,256]{1,0:T(8,128)(2,1)S(1)}, bf16[800,256]{1,0:T(8,128)(2,1)S(1)}, u32[]{:S(2)}, u32[]{:S(2)}) collective-permute-start(bf16[800,256]{1,0:T(8,128)(2,1)S(1)} %collective-permute-done.3.refs_0_), channel_id=1, source_target_pairs={{0,1},{1,0},{2,3},{3,2},{4,5},{5,4},{6,7},{7,6},{8,9},{9,8},{10,11... | collective-permute-start | bytes 1228808 | tf_op jit(solution)/shard_map/ppermute | solution.py:249
  56.1 30.6 %collective-permute-start.10 = (bf16[800,256]{1,0:T(8,128)(2,1)S(1)}, bf16[800,256]{1,0:T(8,128)(2,1)S(1)}, u32[]{:S(2)}, u32[]{:S(2)}) collective-permute-start(bf16[800,256]{1,0:T(8,128)(2,1)S(1)} %add_convert_fusion.2), channel_id=1, source_target_pairs={{0,2},{1,3},{2,0},{3,1},{4,6},{5,7},{6,4},{7,5},{8,10},{9,11},{10,... | collective-permute-start | bytes 1228808 | tf_op jit(solution)/shard_map/ppermute | solution.py:249
  56.2 30.5 %collective-permute-start.11 = (bf16[800,256]{1,0:T(8,128)(2,1)S(1)}, bf16[800,256]{1,0:T(8,128)(2,1)S(1)}, u32[]{:S(2)}, u32[]{:S(2)}) collective-permute-start(bf16[800,256]{1,0:T(8,128)(2,1)S(1)} %add_convert_fusion.1), channel_id=1, source_target_pairs={{0,66},{1,67},{2,64},{3,65},{4,70},{5,71},{6,68},{7,69},{8,74},{9,... | collective-permute-start | bytes 1228808 | tf_op jit(solution)/shard_map/ppermute | solution.py:249
  61.2 25.5 %collective-permute-start.12 = (bf16[800,256]{1,0:T(8,128)(2,1)S(1)}, bf16[800,256]{1,0:T(8,128)(2,1)S(1)}, u32[]{:S(2)}, u32[]{:S(2)}) collective-permute-start(bf16[800,256]{1,0:T(8,128)(2,1)S(1)} %get-tuple-element.39), channel_id=1, source_target_pairs={{0,1},{1,0},{2,3},{3,2},{4,5},{5,4},{6,7},{7,6},{8,9},{9,8},{10,11... | collective-permute-start | bytes 1228808 | tf_op jit(solution)/shard_map/ppermute | solution.py:249
  77.2 12.0 %collective-permute-start.9 = (bf16[800,256]{1,0:T(8,128)(2,1)S(1)}, bf16[800,256]{1,0:T(8,128)(2,1)S(1)}, u32[]{:S(2)}, u32[]{:S(2)}) collective-permute-start(bf16[800,256]{1,0:T(8,128)(2,1)S(1)} %get-tuple-element.34), channel_id=1, source_target_pairs={{0,1},{1,0},{2,3},{3,2},{4,5},{5,4},{6,7},{7,6},{8,9},{9,8},{10,11... | collective-permute-start | bytes 1228808 | tf_op jit(solution)/shard_map/ppermute | solution.py:249
  86.8 12.8 %collective-permute-start.13 = (bf16[800,256]{1,0:T(8,128)(2,1)S(1)}, bf16[800,256]{1,0:T(8,128)(2,1)}, u32[]{:S(2)}, u32[]{:S(2)}) collective-permute-start(bf16[800,256]{1,0:T(8,128)(2,1)S(1)} %add_convert_fusion), channel_id=1, source_target_pairs={{0,64},{1,65},{2,66},{3,67},{4,68},{5,69},{6,70},{7,71},{8,72},{9,... | collective-permute-start | bytes 1228808 | tf_op jit(solution)/shard_map/ppermute | solution.py:249
  89.3 14.6 %all-to-all-start.1 = ((bf16[16,2,32,256]{3,2,1,0:T(8,128)(2,1)}), bf16[16,2,32,256]{3,2,1,0:T(8,128)(2,1)S(1)}, u32[]{:S(2)}, u32[]{:S(2)}) async-start(bf16[16,2,32,256]{3,2,1,0:T(8,128)(2,1)} %bitcast.3), calls=%async_computation.1 | async-start | bytes 1048576 | tf_op jit(solution)/shard_map/all_to_all | solution.py:300

commit v2 on v1

--- a/solution.py
+++ b/solution.py
@@ -14,7 +14,7 @@
 CHUNK = 1024
 AXES = ("blk", "grp")
 CORE, X_LOW, X_HIGH = 1, 2, 64
-NEIGHBOURS = (X_LOW, X_LOW | X_HIGH, X_HIGH)
+X_BOTH = X_LOW | X_HIGH
 CLASS = CORE | X_LOW | X_HIGH
 
 
@@ -23,7 +23,9 @@
     img_refs = [refs.pop(0) for _ in range(2 * count)]
     txt_in, ids_ref = refs.pop(0), refs.pop(0)
     gin_ref = None if first else refs.pop(0)
-    gi_refs = [refs.pop(0) for _ in range(2 * count)]
+    gi_refs = [refs.pop(0) for _ in range(count)]
+    far_ref = refs.pop(0)
+    gi_refs = [gi_refs[b // 2] if b % 2 == 0 else far_ref.at[b // 2] for b in range(2 * count)]
     gt_ref = refs.pop(0)
     txt_ref = refs.pop(0) if first else txt_in
     acc_ref, lr_ref, lc_ref, turn_ref, *more = refs
@@ -191,12 +193,12 @@
 
     total = acc_ref[...] if first else acc_ref[...] + gin_ref[...]
     if last:
-        for j in range(cols // 128):
-            turned = total[:, 128 * j : 128 * (j + 1)].astype(gt_ref.dtype).T.astype(jnp.float32)
-            for i in range(128 // texts):
-                for h, part in enumerate(lanes(turned[i * texts : (i + 1) * texts])):
-                    turn_ref[h, pl.ds(j * (128 // texts) + i, texts, stride=txt_tok), :] = part
-        gt_ref[...] = jnp.concatenate([turn_ref[h] for h in range(dim // 128)], axis=1).astype(gt_ref.dtype)
+        row = lax.broadcasted_iota(jnp.int32, (cols, 1), 0)
+        source = (row % txt_tok) * texts + row // txt_tok
+        pick = jnp.where(lax.broadcasted_iota(jnp.int32, (cols, cols), 1) == source, 1.0, 0.0).astype(gt_ref.dtype)
+        gt_ref[...] = lax.dot_general(
+            pick, total.astype(gt_ref.dtype), (((1,), (1,)), ((), ())), preferred_element_type=jnp.float32
+        ).astype(gt_ref.dtype)
     else:
         gt_ref[...] = total
 
@@ -207,7 +209,8 @@
     rows = tall - EXTRA
     cols = texts.shape[0]
     first = carried is None
-    out_shape = [jax.ShapeDtypeStruct((tall, dim), jnp.bfloat16 if b % 2 else jnp.float32) for b in range(2 * count)]
+    out_shape = [jax.ShapeDtypeStruct((tall, dim), jnp.float32)] * count
+    out_shape.append(jax.ShapeDtypeStruct((count, tall, dim), jnp.bfloat16))
     out_shape.append(
         jax.ShapeDtypeStruct((cols, dim), jnp.bfloat16) if last else jax.ShapeDtypeStruct((dim, cols), jnp.float32)
     )
@@ -250,47 +253,44 @@
 
     labels = jnp.broadcast_to(jnp.tile(positives.astype(jnp.bfloat16), EXTRA // own_images)[:, None], (EXTRA, dim))
     own = jnp.concatenate([image_tokens.transpose(1, 0, 2).reshape(rows, dim), labels], axis=0)
-    over = {bits: swapped(own, bits) for bits in NEIGHBOURS}
+    over = {bits: swapped(own, bits) for bits in (X_LOW, X_BOTH)}
+    over[X_HIGH] = swapped(over[X_LOW], X_BOTH)
 
     sent = jnp.broadcast_to(text_tokens[None], (peers, own_texts, txt_tok, dim))
     texts = lax.all_to_all(sent, AXES, 0, 0, tiled=True, axis_index_groups=across_texts)
-    X_BOTH = X_LOW | X_HIGH
     over[0] = own
-    beside = {bits: swapped(x, CORE) for bits, x in over.items()}
+    beside = {bits: swapped(over[bits], CORE) for bits in (X_LOW, X_BOTH, 0)}
     texts = texts.reshape(peers * own_texts * txt_tok, dim)
     lane = jnp.arange(128, dtype=jnp.int32) % (peers * own_texts)
     ids = ((lane // own_texts) * 4 + (place & CLASS)) * own_texts + lane % own_texts
     ids = jnp.broadcast_to(ids.astype(jnp.float32)[None], (8, 128))
+    ids, beside[0] = lax.optimization_barrier((ids, beside[0]))
 
     def summed(near, met):
         return (near + met.astype(jnp.float32)).astype(jnp.bfloat16)
-
-    found, gathered = {}, None
 
     def work(pairs, last=False):
         nonlocal gathered, texts
         images = [x[bits] for bits in pairs for x in (over, beside)]
-        out = pair_call(images, texts, ids, gathered, img_tok, txt_tok, last)
-        texts = texts if gathered is not None else out[-1]
-        gathered = out[len(images)]
-        return out[: len(images)]
-
-    near, far = work([X_LOW])
-    found[X_LOW] = (near, swapped(far, CORE))
-    near, far = work([X_BOTH])
-    found[X_BOTH] = (near, swapped(far, CORE))
-    *sent, gathered = lax.optimization_barrier((summed(*found[X_LOW]), summed(*found[X_BOTH]), gathered))
+        *near, far, out = pair_call(images, texts, ids, gathered, img_tok, txt_tok, last)[: len(pairs) + 2]
+        gathered = out
+        return near, far
+
+    images = [x[bits] for bits in (X_LOW, X_BOTH) for x in (over, beside)]
+    *near, far, gathered, texts = pair_call(images, texts, ids, None, img_tok, txt_tok, False)
+    far, over[X_HIGH] = lax.optimization_barrier((far, over[X_HIGH]))
+    beside[X_HIGH] = swapped(over[X_HIGH], CORE)
+    met = swapped(far, CORE)
+    *sent, gathered = lax.optimization_barrier((summed(near[0], met[0]), summed(near[1], met[1]), gathered))
     back = [swapped(sent[0], X_LOW), swapped(sent[1], X_BOTH)]
-    near, far = work([X_HIGH])
+    (near,), far = work([X_HIGH])
     met = swapped(far, CORE)
-    out = work([0], last=True)
-    back, met = lax.optimization_barrier((back, met))
-    found[X_HIGH] = (near, met)
-    met, gathered = lax.optimization_barrier((swapped(out[1], CORE), gathered))
-    found[0] = (out[0], met)
-    back.append(swapped(summed(*found[X_HIGH]), X_HIGH))
-
-    grad = found[0][0] + found[0][1].astype(jnp.float32)
+    (own_near,), own_far = work([0], last=True)
+    back, near = lax.optimization_barrier((back, near))
+    own_met, gathered = lax.optimization_barrier((swapped(own_far, CORE), gathered))
+    back.append(swapped(summed(near, met[0]), X_HIGH))
+
+    grad = own_near + own_met[0].astype(jnp.float32)
     for part in back:
         grad = grad + part.astype(jnp.float32)
     grad_image = grad[:rows].reshape(img_tok, own_images, dim).transpose(1, 0, 2)

time: 105 us -> 104 us (level)
  Pallas kernels: 17.8 us -> 16.7 us
    pallas_call x4 -> x3, Pallas kernels: 17.8 us -> 16.7 us  [pair_call(): pl.pallas_call(functools.partial(pair_kernel, count=count, chunk=chunk, i...]
    ppermute x14 -> x13, waiting for transfers between devices: 7.6 us -> 8.68 us  [swapped(): return lax.ppermute(x, AXES, [(i, i ^ bits) for i in range(devices)])]
    ppermute x14 -> x13, starting transfers between devices: 53.2 us -> 53.1 us  [swapped(): return lax.ppermute(x, AXES, [(i, i ^ bits) for i in range(devices)])]
  transfers between devices with their start and end apart: 16 -> 15, of which waited for: 4 -> 4; matrix products, arithmetic and copies ran while one was open for 4% -> 4% of each run, Pallas kernels for 17% -> 16%
where the time goes in v2:
time: 104 us
  starting transfers between devices  64.4 us (62%)
  Pallas kernels  16.7 us (16%)
  waiting for transfers between devices  15.4 us (15%)
  local copies, waits for them, and re-layouts  3.3 us (3%)
  other arithmetic  3.2 us (3%)
    ppermute x13, starting transfers between devices, swapped(): return lax.ppermute(x, AXES, [(i, i ^ bits) for i in range(devices)])  53.1 us
    pallas_call x3, Pallas kernels, pair_call(): pl.pallas_call(functools.partial(pair_kernel, count=count, chunk=chunk, i...  16.7 us
    all_to_all x2, starting transfers between devices, body(): lax.all_to_all(sent, AXES, 0, 0, tiled=True, axis_index_groups=across_texts)  11.3 us
    ppermute x13, waiting for transfers between devices, swapped(): return lax.ppermute(x, AXES, [(i, i ^ bits) for i in range(devices)])  8.68 us
    all_to_all x2, waiting for transfers between devices, body(): lax.all_to_all(sent, AXES, 0, 0, tiled=True, axis_index_groups=across_texts)  6.75 us
  transfers between devices with their start and end apart: 15, of which 4 were waited for; matrix products, arithmetic and copies ran while one was open for 4% of the time, Pallas kernels for 16%

profile of v2, /device:TPU:1, one launch (start us, length us, event | category | flops | bytes accessed | tf_op | source)
XLA Modules:
  0.0 103.8 jit_solution(9878035245898197200)
XLA Ops:
  0.6 0.0 copy-start.1
  0.6 1.1 %reshape.72 = bf16[784,256]{1,0:T(8,128)(2,1)S(1)} reshape(bf16[196,4,256]{2,1,0:T(4,128)(2,1)} %bitcast.22) | data formatting | bytes 802816 | tf_op jit(solution)/shard_map/reshape | solution.py:255
  1.7 0.0 copy-done.1
  1.8 0.1 reshape.81
  1.9 0.1 pad.1.clone
  1.9 0.2 pad_maximum_fusion.refs_0_
  2.1 2.1 %collective-permute-start.1 = (bf16[800,256]{1,0:T(8,128)(2,1)S(1)}, bf16[800,256]{1,0:T(8,128)(2,1)S(1)}, u32[]{:S(2)}, u32[]{:S(2)}) collective-permute-start(bf16[800,256]{1,0:T(8,128)(2,1)S(1)} %pad_maximum_fusion.refs_0_), channel_id=1, source_target_pairs={{0,2},{1,3},{2,0},{3,1},{4,6},{5,7},{6,4},{7,5},{8,10},{9,11},{10,... | collective-permute-start | bytes 1228808 | tf_op jit(solution)/shard_map/ppermute | solution.py:252
  4.2 1.8 %collective-permute-start.3 = (bf16[800,256]{1,0:T(8,128)(2,1)S(1)}, bf16[800,256]{1,0:T(8,128)(2,1)S(1)}, u32[]{:S(2)}, u32[]{:S(2)}) collective-permute-start(bf16[800,256]{1,0:T(8,128)(2,1)S(1)} %pad_maximum_fusion.refs_0_), channel_id=1, source_target_pairs={{0,66},{1,67},{2,64},{3,65},{4,70},{5,71},{6,68},{7,69},{8,74},{9,... | collective-permute-start | bytes 1228808 | tf_op jit(solution)/shard_map/ppermute | solution.py:252
  6.1 0.0 copy-done
  6.1 0.9 broadcast_in_dim.22
  6.9 7.8 %all-to-all-start = ((bf16[16,2,32,256]{3,2,1,0:T(8,128)(2,1)}), bf16[16,2,32,256]{3,2,1,0:T(8,128)(2,1)S(1)}, u32[]{:S(2)}, u32[]{:S(2)}) async-start(bf16[16,2,32,256]{3,2,1,0:T(8,128)(2,1)} %broadcast_in_dim.22), calls=%async_computation | async-start | bytes 1048576 | tf_op jit(solution)/shard_map/all_to_all | solution.py:260
  14.7 1.6 %collective-permute-start = (bf16[800,256]{1,0:T(8,128)(2,1)S(1)}, bf16[800,256]{1,0:T(8,128)(2,1)S(1)}, u32[]{:S(2)}, u32[]{:S(2)}) collective-permute-start(bf16[800,256]{1,0:T(8,128)(2,1)S(1)} %pad_maximum_fusion.refs_0_), channel_id=1, source_target_pairs={{0,1},{1,0},{2,3},{3,2},{4,5},{5,4},{6,7},{7,6},{8,9},{9,8},{10,11... | collective-permute-start | bytes 1228808 | tf_op jit(solution)/shard_map/ppermute | solution.py:252
  16.3 0.0 collective-permute-done.1.refs_0_
  16.3 0.1 collective-permute-start.2
  16.4 0.0 collective-permute-done.3.refs_2_
  16.4 0.9 collective-permute-start.4
  17.3 1.8 %collective-permute-start.5 = (bf16[800,256]{1,0:T(8,128)(2,1)S(1)}, bf16[800,256]{1,0:T(8,128)(2,1)S(1)}, u32[]{:S(2)}, u32[]{:S(2)}) collective-permute-start(bf16[800,256]{1,0:T(8,128)(2,1)S(1)} %collective-permute-done.1.refs_0_), channel_id=1, source_target_pairs={{0,66},{1,67},{2,64},{3,65},{4,70},{5,71},{6,68},{7,69},{8,74},{9,... | collective-permute-start | bytes 1228808 | tf_op jit(solution)/shard_map/ppermute | solution.py:252
  19.2 0.0 collective-permute-done.refs_1_
  19.2 5.6 %all-to-all-done = bf16[16,2,32,256]{3,2,1,0:T(8,128)(2,1)S(1)} async-done(((bf16[16,2,32,256]{3,2,1,0:T(8,128)(2,1)}), bf16[16,2,32,256]{3,2,1,0:T(8,128)(2,1)S(1)}, u32[]{:S(2)}, u32[]{:S(2)}) %all-to-all-start) | async-done | bytes 524320 | tf_op jit(solution)/shard_map/all_to_all | solution.py:260
  24.8 0.0 collective-permute-done.2.refs_1_
  24.8 0.0 collective-permute-done.4.refs_3_
  24.8 7.5 %shard_map.58 = (f32[800,256]{1,0:T(8,128)S(1)}, f32[800,256]{1,0:T(8,128)S(1)}, bf16[2,800,256]{2,1,0:T(8,128)(2,1)S(1)}, f32[256,1024]{1,0:T(8,128)S(1)}, bf16[1024,256]{1,0:T(8,128)(2,1)S(1)}) custom-call(bf16[800,256]{1,0:T(8,128)(2,1)S(1)} %collective-permute-done.1.refs_0_, bf16[800,256]{1,0:T(8,128)(2,1)S(1)} %collective-permute-done.2.refs_1_, ...), custom_call_target="tpu_custom_call" | custom-call | tf_op jit(solution)/shard_map/pallas_call | solution.py:231
  32.4 0.0 collective-permute-done.5.refs_0_
  32.4 21.3 %collective-permute-start.7 = (bf16[2,800,256]{2,1,0:T(8,128)(2,1)S(1)}, bf16[2,800,256]{2,1,0:T(8,128)(2,1)S(1)}, u32[]{:S(2)}, u32[]{:S(2)}) collective-permute-start(bf16[2,800,256]{2,1,0:T(8,128)(2,1)S(1)} %get-tuple-element.32), channel_id=1, source_target_pairs={{0,1},{1,0},{2,3},{3,2},{4,5},{5,4},{6,7},{7,6},{8,9},{9,8},{10,11... | collective-permute-start | bytes 2457608 | tf_op jit(solution)/shard_map/ppermute | solution.py:252
  53.7 0.1 collective-permute-start.6
  53.8 1.9 %collective-permute-done.7 = bf16[2,800,256]{2,1,0:T(8,128)(2,1)S(1)} collective-permute-done((bf16[2,800,256]{2,1,0:T(8,128)(2,1)S(1)}, bf16[2,800,256]{2,1,0:T(8,128)(2,1)S(1)}, u32[]{:S(2)}, u32[]{:S(2)}) %collective-permute-start.7) | collective-permute-done | bytes 819232 | tf_op jit(solution)/shard_map/ppermute | solution.py:252
  55.6 0.2 fusion.4
  55.9 0.1 collective-permute-start.9
  56.0 0.9 collective-permute-start.10
  56.9 0.0 collective-permute-done.6.refs_1_
  56.9 4.0 %shard_map.59 = (f32[800,256]{1,0:T(8,128)S(1)}, bf16[1,800,256]{2,1,0:T(8,128)(2,1)S(1)}, f32[256,1024]{1,0:T(8,128)S(1)}) custom-call(bf16[800,256]{1,0:T(8,128)(2,1)S(1)} %collective-permute-done.5.refs_0_, bf16[800,256]{1,0:T(8,128)(2,1)S(1)} %collective-permute-done.6.refs_1_, bf16[1024,256]{1,0:T(8,128)(2,1)S(1)} %get-tuple-element.28.refs_2_, ...), custom_call_target="tpu_custom_call" | custom-call | tf_op jit(solution)/shard_map/pallas_call | solution.py:231
  60.9 10.4 %collective-permute-start.11 = (bf16[1,800,256]{2,1,0:T(8,128)(2,1)S(1)}, bf16[1,800,256]{2,1,0:T(8,128)(2,1)S(1)}, u32[]{:S(2)}, u32[]{:S(2)}) collective-permute-start(bf16[1,800,256]{2,1,0:T(8,128)(2,1)S(1)} %get-tuple-element.47), channel_id=1, source_target_pairs={{0,1},{1,0},{2,3},{3,2},{4,5},{5,4},{6,7},{7,6},{8,9},{9,8},{10,11... | collective-permute-start | bytes 1228808 | tf_op jit(solution)/shard_map/ppermute | solution.py:252
  71.3 5.2 %shard_map.60 = (f32[800,256]{1,0:T(8,128)S(1)}, bf16[1,800,256]{2,1,0:T(8,128)(2,1)S(1)}, bf16[1024,256]{1,0:T(8,128)(2,1)}) custom-call(bf16[800,256]{1,0:T(8,128)(2,1)S(1)} %pad_maximum_fusion.refs_0_, bf16[800,256]{1,0:T(8,128)(2,1)S(1)} %collective-permute-done.refs_1_, bf16[1024,256]{1,0:T(8,128)(2,1)S(1)} %get-tuple-element.28.refs_2_, ...), custom_call_target="tpu_custom_call" | custom-call | tf_op jit(solution)/shard_map/pallas_call | solution.py:231
  76.5 9.4 %collective-permute-start.8 = (bf16[1,800,256]{2,1,0:T(8,128)(2,1)S(1)}, bf16[1,800,256]{2,1,0:T(8,128)(2,1)}, u32[]{:S(2)}, u32[]{:S(2)}) collective-permute-start(bf16[1,800,256]{2,1,0:T(8,128)(2,1)S(1)} %get-tuple-element.38), channel_id=1, source_target_pairs={{0,1},{1,0},{2,3},{3,2},{4,5},{5,4},{6,7},{7,6},{8,9},{9,8},{10,11... | collective-permute-start | bytes 1228808 | tf_op jit(solution)/shard_map/ppermute | solution.py:252
  85.9 0.0 collective-permute-done.9
  85.9 0.0 collective-permute-done.10
  85.9 0.0 collective-permute-done.11
  85.9 0.1 fusion
  86.0 2.4 %collective-permute-start.12 = (bf16[800,256]{1,0:T(8,128)(2,1)S(1)}, bf16[800,256]{1,0:T(8,128)(2,1)}, u32[]{:S(2)}, u32[]{:S(2)}) collective-permute-start(bf16[800,256]{1,0:T(8,128)(2,1)S(1)} %fusion), channel_id=1, source_target_pairs={{0,64},{1,65},{2,66},{3,67},{4,68},{5,69},{6,70},{7,71},{8,72},{9,... | collective-permute-start | bytes 1228808 | tf_op jit(solution)/shard_map/ppermute | solution.py:252
  88.4 0.0 collective-permute-done.8
  88.4 3.6 %all-to-all-start.1 = ((bf16[16,2,32,256]{3,2,1,0:T(8,128)(2,1)}), bf16[16,2,32,256]{3,2,1,0:T(8,128)(2,1)S(1)}, u32[]{:S(2)}, u32[]{:S(2)}) async-start(bf16[16,2,32,256]{3,2,1,0:T(8,128)(2,1)} %bitcast.7), calls=%async_computation.1 | async-start | bytes 1048576 | tf_op jit(solution)/shard_map/all_to_all | solution.py:300
  92.0 6.8 %collective-permute-done.12 = bf16[800,256]{1,0:T(8,128)(2,1)} collective-permute-done((bf16[800,256]{1,0:T(8,128)(2,1)S(1)}, bf16[800,256]{1,0:T(8,128)(2,1)}, u32[]{:S(2)}, u32[]{:S(2)}) %collective-permute-start.12) | collective-permute-done | bytes 409632 | tf_op jit(solution)/shard_map/ppermute | solution.py:252
  98.8 1.3 %fusion.3 = f32[800,256]{1,0:T(8,128)S(1)} fusion(f32[800,256]{1,0:T(8,128)S(1)} %get-tuple-element.37, bf16[800,256]{1,0:T(8,128)(2,1)} %collective-permute-done.12, bf16[800,256]{1,0:T(8,128)(2,1)S(1)} %collective-permute-done.10, bf16[800,256]{1,0:T(8,128)(2,1)S(1)} %collective-permute-done.9, bf16[1,800,256]{2,1,0:T(8,128)(2,1)} %collective-permute-done.8), kind=kLoop, calls=%fused_computation.6 | loop fusion | flops 1638400 | bytes 3276800 | tf_op jit(solution)/shard_map/add | solution.py:295
  100.1 0.1 slice.34
  100.2 1.1 %reshape.74 = f32[196,4,256]{2,1,0:T(4,128)} reshape(f32[784,256]{1,0:T(8,128)S(1)} %slice.34) | data formatting | bytes 1605632 | tf_op jit(solution)/shard_map/reshape | solution.py:296
  101.3 0.6 fusion.6
  101.9 1.1 %all-to-all-done.1 = bf16[16,2,32,256]{3,2,1,0:T(8,128)(2,1)S(1)} async-done(((bf16[16,2,32,256]{3,2,1,0:T(8,128)(2,1)}), bf16[16,2,32,256]{3,2,1,0:T(8,128)(2,1)S(1)}, u32[]{:S(2)}, u32[]{:S(2)}) %all-to-all-start.1) | async-done | bytes 524320 | tf_op jit(solution)/shard_map/all_to_all | solution.py:300
  103.1 0.7 convert_reduce_fusion
  (5 shorter events, 0.0 us)
Async XLA Ops:
  0.6 1.1 %copy-start.1 = (s32[4]{0:T(128)S(1)}, s32[4]{0:T(128)}, u32[]{:S(2)}) copy-start(s32[4]{0:T(128)} %param.5) | copy-start | bytes 52
  1.9 4.1 %copy-start = (bf16[2,32,256]{2,1,0:T(8,128)(2,1)S(1)}, bf16[2,32,256]{2,1,0:T(8,128)(2,1)}, u32[]{:S(2)}) copy-start(bf16[2,32,256]{2,1,0:T(8,128)(2,1)} %param.4) | copy-start | bytes 98308
  2.1 14.2 %collective-permute-start.1 = (bf16[800,256]{1,0:T(8,128)(2,1)S(1)}, bf16[800,256]{1,0:T(8,128)(2,1)S(1)}, u32[]{:S(2)}, u32[]{:S(2)}) collective-permute-start(bf16[800,256]{1,0:T(8,128)(2,1)S(1)} %pad_maximum_fusion.refs_0_), channel_id=1, source_target_pairs={{0,2},{1,3},{2,0},{3,1},{4,6},{5,7},{6,4},{7,5},{8,10},{9,11},{10,... | collective-permute-start | bytes 1228808 | tf_op jit(solution)/shard_map/ppermute | solution.py:252
  4.2 12.2 %collective-permute-start.3 = (bf16[800,256]{1,0:T(8,128)(2,1)S(1)}, bf16[800,256]{1,0:T(8,128)(2,1)S(1)}, u32[]{:S(2)}, u32[]{:S(2)}) collective-permute-start(bf16[800,256]{1,0:T(8,128)(2,1)S(1)} %pad_maximum_fusion.refs_0_), channel_id=1, source_target_pairs={{0,66},{1,67},{2,64},{3,65},{4,70},{5,71},{6,68},{7,69},{8,74},{9,... | collective-permute-start | bytes 1228808 | tf_op jit(solution)/shard_map/ppermute | solution.py:252
  6.9 17.9 %all-to-all-start = ((bf16[16,2,32,256]{3,2,1,0:T(8,128)(2,1)}), bf16[16,2,32,256]{3,2,1,0:T(8,128)(2,1)S(1)}, u32[]{:S(2)}, u32[]{:S(2)}) async-start(bf16[16,2,32,256]{3,2,1,0:T(8,128)(2,1)} %broadcast_in_dim.22), calls=%async_computation | async-start | bytes 1048576 | tf_op jit(solution)/shard_map/all_to_all | solution.py:260
  14.7 4.5 %collective-permute-start = (bf16[800,256]{1,0:T(8,128)(2,1)S(1)}, bf16[800,256]{1,0:T(8,128)(2,1)S(1)}, u32[]{:S(2)}, u32[]{:S(2)}) collective-permute-start(bf16[800,256]{1,0:T(8,128)(2,1)S(1)} %pad_maximum_fusion.refs_0_), channel_id=1, source_target_pairs={{0,1},{1,0},{2,3},{3,2},{4,5},{5,4},{6,7},{7,6},{8,9},{9,8},{10,11... | collective-permute-start | bytes 1228808 | tf_op jit(solution)/shard_map/ppermute | solution.py:252
  16.3 8.5 %collective-permute-start.2 = (bf16[800,256]{1,0:T(8,128)(2,1)S(1)}, bf16[800,256]{1,0:T(8,128)(2,1)S(1)}, u32[]{:S(2)}, u32[]{:S(2)}) collective-permute-start(bf16[800,256]{1,0:T(8,128)(2,1)S(1)} %collective-permute-done.1.refs_0_), channel_id=1, source_target_pairs={{0,1},{1,0},{2,3},{3,2},{4,5},{5,4},{6,7},{7,6},{8,9},{9,8},{10,11... | collective-permute-start | bytes 1228808 | tf_op jit(solution)/shard_map/ppermute | solution.py:252
  16.4 8.4 %collective-permute-start.4 = (bf16[800,256]{1,0:T(8,128)(2,1)S(1)}, bf16[800,256]{1,0:T(8,128)(2,1)S(1)}, u32[]{:S(2)}, u32[]{:S(2)}) collective-permute-start(bf16[800,256]{1,0:T(8,128)(2,1)S(1)} %collective-permute-done.3.refs_2_), channel_id=1, source_target_pairs={{0,1},{1,0},{2,3},{3,2},{4,5},{5,4},{6,7},{7,6},{8,9},{9,8},{10,11... | collective-permute-start | bytes 1228808 | tf_op jit(solution)/shard_map/ppermute | solution.py:252
  17.3 15.0 %collective-permute-start.5 = (bf16[800,256]{1,0:T(8,128)(2,1)S(1)}, bf16[800,256]{1,0:T(8,128)(2,1)S(1)}, u32[]{:S(2)}, u32[]{:S(2)}) collective-permute-start(bf16[800,256]{1,0:T(8,128)(2,1)S(1)} %collective-permute-done.1.refs_0_), channel_id=1, source_target_pairs={{0,66},{1,67},{2,64},{3,65},{4,70},{5,71},{6,68},{7,69},{8,74},{9,... | collective-permute-start | bytes 1228808 | tf_op jit(solution)/shard_map/ppermute | solution.py:252
  32.4 23.3 %collective-permute-start.7 = (bf16[2,800,256]{2,1,0:T(8,128)(2,1)S(1)}, bf16[2,800,256]{2,1,0:T(8,128)(2,1)S(1)}, u32[]{:S(2)}, u32[]{:S(2)}) collective-permute-start(bf16[2,800,256]{2,1,0:T(8,128)(2,1)S(1)} %get-tuple-element.32), channel_id=1, source_target_pairs={{0,1},{1,0},{2,3},{3,2},{4,5},{5,4},{6,7},{7,6},{8,9},{9,8},{10,11... | collective-permute-start | bytes 2457608 | tf_op jit(solution)/shard_map/ppermute | solution.py:252
  53.7 3.2 %collective-permute-start.6 = (bf16[800,256]{1,0:T(8,128)(2,1)S(1)}, bf16[800,256]{1,0:T(8,128)(2,1)S(1)}, u32[]{:S(2)}, u32[]{:S(2)}) collective-permute-start(bf16[800,256]{1,0:T(8,128)(2,1)S(1)} %collective-permute-done.5.refs_0_), channel_id=1, source_target_pairs={{0,1},{1,0},{2,3},{3,2},{4,5},{5,4},{6,7},{7,6},{8,9},{9,8},{10,11... | collective-permute-start | bytes 1228808 | tf_op jit(solution)/shard_map/ppermute | solution.py:252
  55.9 30.0 %collective-permute-start.9 = (bf16[800,256]{1,0:T(8,128)(2,1)S(1)}, bf16[800,256]{1,0:T(8,128)(2,1)S(1)}, u32[]{:S(2)}, u32[]{:S(2)}) collective-permute-start(bf16[800,256]{1,0:T(8,128)(2,1)S(1)} %get-tuple-element.41), channel_id=1, source_target_pairs={{0,2},{1,3},{2,0},{3,1},{4,6},{5,7},{6,4},{7,5},{8,10},{9,11},{10,... | collective-permute-start | bytes 1228808 | tf_op jit(solution)/shard_map/ppermute | solution.py:252
  56.0 29.9 %collective-permute-start.10 = (bf16[800,256]{1,0:T(8,128)(2,1)S(1)}, bf16[800,256]{1,0:T(8,128)(2,1)S(1)}, u32[]{:S(2)}, u32[]{:S(2)}) collective-permute-start(bf16[800,256]{1,0:T(8,128)(2,1)S(1)} %get-tuple-element.42), channel_id=1, source_target_pairs={{0,66},{1,67},{2,64},{3,65},{4,70},{5,71},{6,68},{7,69},{8,74},{9,... | collective-permute-start | bytes 1228808 | tf_op jit(solution)/shard_map/ppermute | solution.py:252
  60.9 25.1 %collective-permute-start.11 = (bf16[1,800,256]{2,1,0:T(8,128)(2,1)S(1)}, bf16[1,800,256]{2,1,0:T(8,128)(2,1)S(1)}, u32[]{:S(2)}, u32[]{:S(2)}) collective-permute-start(bf16[1,800,256]{2,1,0:T(8,128)(2,1)S(1)} %get-tuple-element.47), channel_id=1, source_target_pairs={{0,1},{1,0},{2,3},{3,2},{4,5},{5,4},{6,7},{7,6},{8,9},{9,8},{10,11... | collective-permute-start | bytes 1228808 | tf_op jit(solution)/shard_map/ppermute | solution.py:252
  76.5 12.0 %collective-permute-start.8 = (bf16[1,800,256]{2,1,0:T(8,128)(2,1)S(1)}, bf16[1,800,256]{2,1,0:T(8,128)(2,1)}, u32[]{:S(2)}, u32[]{:S(2)}) collective-permute-start(bf16[1,800,256]{2,1,0:T(8,128)(2,1)S(1)} %get-tuple-element.38), channel_id=1, source_target_pairs={{0,1},{1,0},{2,3},{3,2},{4,5},{5,4},{6,7},{7,6},{8,9},{9,8},{10,11... | collective-permute-start | bytes 1228808 | tf_op jit(solution)/shard_map/ppermute | solution.py:252
  86.0 12.8 %collective-permute-start.12 = (bf16[800,256]{1,0:T(8,128)(2,1)S(1)}, bf16[800,256]{1,0:T(8,128)(2,1)}, u32[]{:S(2)}, u32[]{:S(2)}) collective-permute-start(bf16[800,256]{1,0:T(8,128)(2,1)S(1)} %fusion), channel_id=1, source_target_pairs={{0,64},{1,65},{2,66},{3,67},{4,68},{5,69},{6,70},{7,71},{8,72},{9,... | collective-permute-start | bytes 1228808 | tf_op jit(solution)/shard_map/ppermute | solution.py:252
  88.4 14.6 %all-to-all-start.1 = ((bf16[16,2,32,256]{3,2,1,0:T(8,128)(2,1)}), bf16[16,2,32,256]{3,2,1,0:T(8,128)(2,1)S(1)}, u32[]{:S(2)}, u32[]{:S(2)}) async-start(bf16[16,2,32,256]{3,2,1,0:T(8,128)(2,1)} %bitcast.7), calls=%async_computation.1 | async-start | bytes 1048576 | tf_op jit(solution)/shard_map/all_to_all | solution.py:300

commit v3 on v2

--- a/solution.py
+++ b/solution.py
@@ -23,9 +23,8 @@
     img_refs = [refs.pop(0) for _ in range(2 * count)]
     txt_in, ids_ref = refs.pop(0), refs.pop(0)
     gin_ref = None if first else refs.pop(0)
-    gi_refs = [refs.pop(0) for _ in range(count)]
-    far_ref = refs.pop(0)
-    gi_refs = [gi_refs[b // 2] if b % 2 == 0 else far_ref.at[b // 2] for b in range(2 * count)]
+    gi_refs = [refs.pop(0) for _ in range(2 * count)]
+    gi_refs = [gi_refs[b // 2 + count * (b % 2)] for b in range(2 * count)]
     gt_ref = refs.pop(0)
     txt_ref = refs.pop(0) if first else txt_in
     acc_ref, lr_ref, lc_ref, turn_ref, *more = refs
@@ -210,7 +209,7 @@
     cols = texts.shape[0]
     first = carried is None
     out_shape = [jax.ShapeDtypeStruct((tall, dim), jnp.float32)] * count
-    out_shape.append(jax.ShapeDtypeStruct((count, tall, dim), jnp.bfloat16))
+    out_shape += [jax.ShapeDtypeStruct((tall, dim), jnp.bfloat16)] * count
     out_shape.append(
         jax.ShapeDtypeStruct((cols, dim), jnp.bfloat16) if last else jax.ShapeDtypeStruct((dim, cols), jnp.float32)
     )
@@ -269,28 +268,27 @@
     def summed(near, met):
         return (near + met.astype(jnp.float32)).astype(jnp.bfloat16)
 
-    def work(pairs, last=False):
-        nonlocal gathered, texts
-        images = [x[bits] for bits in pairs for x in (over, beside)]
-        *near, far, out = pair_call(images, texts, ids, gathered, img_tok, txt_tok, last)[: len(pairs) + 2]
-        gathered = out
+    def work(bits, last=False):
+        nonlocal gathered
+        images = [over[bits], beside[bits]]
+        near, far, gathered = pair_call(images, texts, ids, gathered, img_tok, txt_tok, last)
         return near, far
 
     images = [x[bits] for bits in (X_LOW, X_BOTH) for x in (over, beside)]
-    *near, far, gathered, texts = pair_call(images, texts, ids, None, img_tok, txt_tok, False)
-    far, over[X_HIGH] = lax.optimization_barrier((far, over[X_HIGH]))
+    *both, gathered, texts = pair_call(images, texts, ids, None, img_tok, txt_tok, False)
+    near, far = both[:2], both[2:]
     beside[X_HIGH] = swapped(over[X_HIGH], CORE)
-    met = swapped(far, CORE)
+    met = [swapped(far[0], CORE), swapped(far[1], CORE)]
     *sent, gathered = lax.optimization_barrier((summed(near[0], met[0]), summed(near[1], met[1]), gathered))
     back = [swapped(sent[0], X_LOW), swapped(sent[1], X_BOTH)]
-    (near,), far = work([X_HIGH])
+    near, far = work(X_HIGH)
     met = swapped(far, CORE)
-    (own_near,), own_far = work([0], last=True)
+    own_near, own_far = work(0, last=True)
     back, near = lax.optimization_barrier((back, near))
     own_met, gathered = lax.optimization_barrier((swapped(own_far, CORE), gathered))
-    back.append(swapped(summed(near, met[0]), X_HIGH))
-
-    grad = own_near + own_met[0].astype(jnp.float32)
+    back.append(swapped(summed(near, met), X_HIGH))
+
+    grad = own_near + own_met.astype(jnp.float32)
     for part in back:
         grad = grad + part.astype(jnp.float32)
     grad_image = grad[:rows].reshape(img_tok, own_images, dim).transpose(1, 0, 2)

time: 104 us -> 105 us (level)
  local copies, waits for them, and re-layouts: 3.3 us -> 4.81 us
  waiting for transfers between devices: 15.4 us -> 14.3 us
    unnamed x4 -> x8, local copies, waits for them, and re-layouts: 0.01 us -> 1.52 us
    ppermute x13 -> x14, waiting for transfers between devices: 8.68 us -> 7.62 us  [swapped(): return lax.ppermute(x, AXES, [(i, i ^ bits) for i in range(devices)])]
    ppermute x13 -> x14, starting transfers between devices: 53.1 us -> 53.3 us  [swapped(): return lax.ppermute(x, AXES, [(i, i ^ bits) for i in range(devices)])]
  transfers between devices with their start and end apart: 15 -> 16, of which waited for: 4 -> 6; matrix products, arithmetic and copies ran while one was open for 4% -> 4% of each run, Pallas kernels for 16% -> 16%
where the time goes in v3:
time: 105 us; the launch traced here: 104 us
  starting transfers between devices  64.6 us (62%)
  Pallas kernels  16.6 us (16%)
  waiting for transfers between devices  14.3 us (14%)
  local copies, waits for them, and re-layouts  4.81 us (5%)
  other arithmetic  3.2 us (3%)
    ppermute x14, starting transfers between devices, swapped(): return lax.ppermute(x, AXES, [(i, i ^ bits) for i in range(devices)])  53.3 us
    pallas_call x3, Pallas kernels, pair_call(): pl.pallas_call(functools.partial(pair_kernel, count=count, chunk=chunk, i...  16.6 us
    all_to_all x2, starting transfers between devices, body(): lax.all_to_all(sent, AXES, 0, 0, tiled=True, axis_index_groups=across_texts)  11.3 us
    ppermute x14, waiting for transfers between devices, swapped(): return lax.ppermute(x, AXES, [(i, i ^ bits) for i in range(devices)])  7.62 us
    all_to_all x2, waiting for transfers between devices, body(): lax.all_to_all(sent, AXES, 0, 0, tiled=True, axis_index_groups=across_texts)  6.73 us
  transfers between devices with their start and end apart: 16, of which 6 were waited for; matrix products, arithmetic and copies ran while one was open for 4% of the time, Pallas kernels for 16%

profile of v3, /device:TPU:1, one launch (start us, length us, event | category | flops | bytes accessed | tf_op | source)
XLA Modules:
  0.0 104.4 jit_solution(15064606500451376387)
XLA Ops:
  0.6 1.1 %reshape.64 = bf16[784,256]{1,0:T(8,128)(2,1)S(1)} reshape(bf16[196,4,256]{2,1,0:T(4,128)(2,1)} %bitcast.6) | data formatting | bytes 802816 | tf_op jit(solution)/shard_map/reshape | solution.py:254
  1.8 0.1 reshape.69
  1.9 0.1 pad.1.clone
  1.9 0.2 pad_maximum_fusion.refs_0_
  2.1 2.1 %collective-permute-start.1 = (bf16[800,256]{1,0:T(8,128)(2,1)S(1)}, bf16[800,256]{1,0:T(8,128)(2,1)S(1)}, u32[]{:S(2)}, u32[]{:S(2)}) collective-permute-start(bf16[800,256]{1,0:T(8,128)(2,1)S(1)} %pad_maximum_fusion.refs_0_), channel_id=1, source_target_pairs={{0,2},{1,3},{2,0},{3,1},{4,6},{5,7},{6,4},{7,5},{8,10},{9,11},{10,... | collective-permute-start | bytes 1228808 | tf_op jit(solution)/shard_map/ppermute | solution.py:251
  4.2 1.8 %collective-permute-start.3 = (bf16[800,256]{1,0:T(8,128)(2,1)S(1)}, bf16[800,256]{1,0:T(8,128)(2,1)S(1)}, u32[]{:S(2)}, u32[]{:S(2)}) collective-permute-start(bf16[800,256]{1,0:T(8,128)(2,1)S(1)} %pad_maximum_fusion.refs_0_), channel_id=1, source_target_pairs={{0,66},{1,67},{2,64},{3,65},{4,70},{5,71},{6,68},{7,69},{8,74},{9,... | collective-permute-start | bytes 1228808 | tf_op jit(solution)/shard_map/ppermute | solution.py:251
  6.1 0.9 broadcast_in_dim.22
  6.9 7.8 %all-to-all-start = ((bf16[16,2,32,256]{3,2,1,0:T(8,128)(2,1)}), bf16[16,2,32,256]{3,2,1,0:T(8,128)(2,1)S(1)}, u32[]{:S(2)}, u32[]{:S(2)}) async-start(bf16[16,2,32,256]{3,2,1,0:T(8,128)(2,1)} %broadcast_in_dim.22), calls=%async_computation | async-start | bytes 1048576 | tf_op jit(solution)/shard_map/all_to_all | solution.py:259
  14.7 1.6 %collective-permute-start = (bf16[800,256]{1,0:T(8,128)(2,1)S(1)}, bf16[800,256]{1,0:T(8,128)(2,1)S(1)}, u32[]{:S(2)}, u32[]{:S(2)}) collective-permute-start(bf16[800,256]{1,0:T(8,128)(2,1)S(1)} %pad_maximum_fusion.refs_0_), channel_id=1, source_target_pairs={{0,1},{1,0},{2,3},{3,2},{4,5},{5,4},{6,7},{7,6},{8,9},{9,8},{10,11... | collective-permute-start | bytes 1228808 | tf_op jit(solution)/shard_map/ppermute | solution.py:251
  16.3 0.0 collective-permute-done.1.refs_0_
  16.3 0.1 collective-permute-start.2
  16.4 0.0 collective-permute-done.3.refs_2_
  16.4 0.9 collective-permute-start.4
  17.4 0.3 collective-permute-done.refs_1_
  17.7 1.6 %collective-permute-start.5 = (bf16[800,256]{1,0:T(8,128)(2,1)S(1)}, bf16[800,256]{1,0:T(8,128)(2,1)S(1)}, u32[]{:S(2)}, u32[]{:S(2)}) collective-permute-start(bf16[800,256]{1,0:T(8,128)(2,1)S(1)} %collective-permute-done.1.refs_0_), channel_id=1, source_target_pairs={{0,66},{1,67},{2,64},{3,65},{4,70},{5,71},{6,68},{7,69},{8,74},{9,... | collective-permute-start | bytes 1228808 | tf_op jit(solution)/shard_map/ppermute | solution.py:251
  19.3 5.6 %all-to-all-done = bf16[16,2,32,256]{3,2,1,0:T(8,128)(2,1)S(1)} async-done(((bf16[16,2,32,256]{3,2,1,0:T(8,128)(2,1)}), bf16[16,2,32,256]{3,2,1,0:T(8,128)(2,1)S(1)}, u32[]{:S(2)}, u32[]{:S(2)}) %all-to-all-start) | async-done | bytes 524320 | tf_op jit(solution)/shard_map/all_to_all | solution.py:259
  24.8 0.0 collective-permute-done.2.refs_1_
  24.8 0.0 collective-permute-done.4.refs_3_
  24.8 7.5 %shard_map.58 = (f32[800,256]{1,0:T(8,128)S(1)}, f32[800,256]{1,0:T(8,128)S(1)}, bf16[800,256]{1,0:T(8,128)(2,1)S(1)}, bf16[800,256]{1,0:T(8,128)(2,1)S(1)}, f32...) custom-call(bf16[800,256]{1,0:T(8,128)(2,1)S(1)} %collective-permute-done.1.refs_0_, ...), custom_call_target="tpu_custom_call" | custom-call | tf_op jit(solution)/shard_map/pallas_call | solution.py:230
  32.4 21.3 %collective-permute-start.8 = (bf16[800,256]{1,0:T(8,128)(2,1)S(1)}, bf16[800,256]{1,0:T(8,128)(2,1)S(1)}, u32[]{:S(2)}, u32[]{:S(2)}) collective-permute-start(bf16[800,256]{1,0:T(8,128)(2,1)S(1)} %get-tuple-element.31), channel_id=1, source_target_pairs={{0,1},{1,0},{2,3},{3,2},{4,5},{5,4},{6,7},{7,6},{8,9},{9,8},{10,11... | collective-permute-start | bytes 1228808 | tf_op jit(solution)/shard_map/ppermute | solution.py:251
  53.7 0.1 collective-permute-start.7
  53.8 0.0 collective-permute-done.5.refs_0_
  53.8 0.4 collective-permute-start.6
  54.2 0.9 collective-permute-done.8
  55.1 0.1 add_convert_fusion.1
  55.1 0.5 collective-permute-done.7
  55.6 0.1 add_convert_fusion.2
  55.8 0.1 collective-permute-start.10
  55.9 0.9 collective-permute-start.11
  56.8 0.0 collective-permute-done.6.refs_1_
  56.8 3.9 %shard_map.59 = (f32[800,256]{1,0:T(8,128)S(1)}, bf16[800,256]{1,0:T(8,128)(2,1)S(1)}, f32[256,1024]{1,0:T(8,128)S(1)}) custom-call(bf16[800,256]{1,0:T(8,128)(2,1)S(1)} %collective-permute-done.5.refs_0_, bf16[800,256]{1,0:T(8,128)(2,1)S(1)} %collective-permute-done.6.refs_1_, bf16[1024,256]{1,0:T(8,128)(2,1)S(1)} %get-tuple-element.27.refs_2_, ...), custom_call_target="tpu_custom_call" | custom-call | tf_op jit(solution)/shard_map/pallas_call | solution.py:230
  60.7 10.4 %collective-permute-start.12 = (bf16[800,256]{1,0:T(8,128)(2,1)S(1)}, bf16[800,256]{1,0:T(8,128)(2,1)S(1)}, u32[]{:S(2)}, u32[]{:S(2)}) collective-permute-start(bf16[800,256]{1,0:T(8,128)(2,1)S(1)} %get-tuple-element.45), channel_id=1, source_target_pairs={{0,1},{1,0},{2,3},{3,2},{4,5},{5,4},{6,7},{7,6},{8,9},{9,8},{10,11... | collective-permute-start | bytes 1228808 | tf_op jit(solution)/shard_map/ppermute | solution.py:251
  71.2 5.2 %shard_map.60 = (f32[800,256]{1,0:T(8,128)S(1)}, bf16[800,256]{1,0:T(8,128)(2,1)S(1)}, bf16[1024,256]{1,0:T(8,128)(2,1)}) custom-call(bf16[800,256]{1,0:T(8,128)(2,1)S(1)} %pad_maximum_fusion.refs_0_, bf16[800,256]{1,0:T(8,128)(2,1)S(1)} %collective-permute-done.refs_1_, bf16[1024,256]{1,0:T(8,128)(2,1)S(1)} %get-tuple-element.27.refs_2_, ...), custom_call_target="tpu_custom_call" | custom-call | tf_op jit(solution)/shard_map/pallas_call | solution.py:230
  76.3 9.5 %collective-permute-start.9 = (bf16[800,256]{1,0:T(8,128)(2,1)S(1)}, bf16[800,256]{1,0:T(8,128)(2,1)S(1)}, u32[]{:S(2)}, u32[]{:S(2)}) collective-permute-start(bf16[800,256]{1,0:T(8,128)(2,1)S(1)} %get-tuple-element.36), channel_id=1, source_target_pairs={{0,1},{1,0},{2,3},{3,2},{4,5},{5,4},{6,7},{7,6},{8,9},{9,8},{10,11... | collective-permute-start | bytes 1228808 | tf_op jit(solution)/shard_map/ppermute | solution.py:251
  85.8 0.0 collective-permute-done.10
  85.8 0.1 add_convert_fusion
  85.9 2.4 %collective-permute-start.13 = (bf16[800,256]{1,0:T(8,128)(2,1)S(1)}, bf16[800,256]{1,0:T(8,128)(2,1)S(1)}, u32[]{:S(2)}, u32[]{:S(2)}) collective-permute-start(bf16[800,256]{1,0:T(8,128)(2,1)S(1)} %add_convert_fusion), channel_id=1, source_target_pairs={{0,64},{1,65},{2,66},{3,67},{4,68},{5,69},{6,70},{7,71},{8,72},{9,... | collective-permute-start | bytes 1228808 | tf_op jit(solution)/shard_map/ppermute | solution.py:251
  88.3 0.0 collective-permute-done.9
  88.3 0.8 copy-done
  89.0 3.6 %all-to-all-start.1 = ((bf16[16,2,32,256]{3,2,1,0:T(8,128)(2,1)}), bf16[16,2,32,256]{3,2,1,0:T(8,128)(2,1)S(1)}, u32[]{:S(2)}, u32[]{:S(2)}) async-start(bf16[16,2,32,256]{3,2,1,0:T(8,128)(2,1)} %bitcast.3), calls=%async_computation.1 | async-start | bytes 1048576 | tf_op jit(solution)/shard_map/all_to_all | solution.py:298
  92.6 5.9 %collective-permute-done.13 = bf16[800,256]{1,0:T(8,128)(2,1)S(1)} collective-permute-done((bf16[800,256]{1,0:T(8,128)(2,1)S(1)}, bf16[800,256]{1,0:T(8,128)(2,1)S(1)}, u32[]{:S(2)}, u32[]{:S(2)}) %collective-permute-start.13) | collective-permute-done | bytes 409632 | tf_op jit(solution)/shard_map/ppermute | solution.py:251
  98.6 0.7 copy-done.1
  99.3 1.4 %convert_add_fusion = f32[800,256]{1,0:T(8,128)S(1)} fusion(bf16[800,256]{1,0:T(8,128)(2,1)} %copy-done.1, bf16[800,256]{1,0:T(8,128)(2,1)S(1)} %collective-permute-done.11, bf16[800,256]{1,0:T(8,128)(2,1)S(1)} %collective-permute-done.10, f32[800,256]{1,0:T(8,128)S(1)} %get-tuple-element.35, bf16[800,256]{1,0:T(8,128)(2,1)} %copy-done), kind=kLoop, calls=%fused_computation.1 | loop fusion | flops 1638400 | bytes 3276800 | tf_op jit(solution)/shard_map/add | solution.py:293
  100.7 0.1 slice.24
  100.8 1.1 %reshape.66 = f32[196,4,256]{2,1,0:T(4,128)} reshape(f32[784,256]{1,0:T(8,128)S(1)} %slice.24) | data formatting | bytes 1605632 | tf_op jit(solution)/shard_map/reshape | solution.py:294
  101.9 0.6 fusion
  102.5 1.2 %all-to-all-done.1 = bf16[16,2,32,256]{3,2,1,0:T(8,128)(2,1)S(1)} async-done(((bf16[16,2,32,256]{3,2,1,0:T(8,128)(2,1)}), bf16[16,2,32,256]{3,2,1,0:T(8,128)(2,1)S(1)}, u32[]{:S(2)}, u32[]{:S(2)}) %all-to-all-start.1) | async-done | bytes 524320 | tf_op jit(solution)/shard_map/all_to_all | solution.py:298
  103.7 0.7 convert_reduce_fusion
  (12 shorter events, 0.0 us)
Async XLA Ops:
  0.6 1.1 %copy-start.3 = (s32[4]{0:T(128)S(1)}, s32[4]{0:T(128)}, u32[]{:S(2)}) copy-start(s32[4]{0:T(128)} %param.5) | copy-start | bytes 52
  1.9 4.1 %copy-start.2 = (bf16[2,32,256]{2,1,0:T(8,128)(2,1)S(1)}, bf16[2,32,256]{2,1,0:T(8,128)(2,1)}, u32[]{:S(2)}) copy-start(bf16[2,32,256]{2,1,0:T(8,128)(2,1)} %param.4) | copy-start | bytes 98308
  2.1 14.2 %collective-permute-start.1 = (bf16[800,256]{1,0:T(8,128)(2,1)S(1)}, bf16[800,256]{1,0:T(8,128)(2,1)S(1)}, u32[]{:S(2)}, u32[]{:S(2)}) collective-permute-start(bf16[800,256]{1,0:T(8,128)(2,1)S(1)} %pad_maximum_fusion.refs_0_), channel_id=1, source_target_pairs={{0,2},{1,3},{2,0},{3,1},{4,6},{5,7},{6,4},{7,5},{8,10},{9,11},{10,... | collective-permute-start | bytes 1228808 | tf_op jit(solution)/shard_map/ppermute | solution.py:251
  4.2 12.2 %collective-permute-start.3 = (bf16[800,256]{1,0:T(8,128)(2,1)S(1)}, bf16[800,256]{1,0:T(8,128)(2,1)S(1)}, u32[]{:S(2)}, u32[]{:S(2)}) collective-permute-start(bf16[800,256]{1,0:T(8,128)(2,1)S(1)} %pad_maximum_fusion.refs_0_), channel_id=1, source_target_pairs={{0,66},{1,67},{2,64},{3,65},{4,70},{5,71},{6,68},{7,69},{8,74},{9,... | collective-permute-start | bytes 1228808 | tf_op jit(solution)/shard_map/ppermute | solution.py:251
  6.9 17.9 %all-to-all-start = ((bf16[16,2,32,256]{3,2,1,0:T(8,128)(2,1)}), bf16[16,2,32,256]{3,2,1,0:T(8,128)(2,1)S(1)}, u32[]{:S(2)}, u32[]{:S(2)}) async-start(bf16[16,2,32,256]{3,2,1,0:T(8,128)(2,1)} %broadcast_in_dim.22), calls=%async_computation | async-start | bytes 1048576 | tf_op jit(solution)/shard_map/all_to_all | solution.py:259
  14.7 3.0 %collective-permute-start = (bf16[800,256]{1,0:T(8,128)(2,1)S(1)}, bf16[800,256]{1,0:T(8,128)(2,1)S(1)}, u32[]{:S(2)}, u32[]{:S(2)}) collective-permute-start(bf16[800,256]{1,0:T(8,128)(2,1)S(1)} %pad_maximum_fusion.refs_0_), channel_id=1, source_target_pairs={{0,1},{1,0},{2,3},{3,2},{4,5},{5,4},{6,7},{7,6},{8,9},{9,8},{10,11... | collective-permute-start | bytes 1228808 | tf_op jit(solution)/shard_map/ppermute | solution.py:251
  16.3 8.5 %collective-permute-start.2 = (bf16[800,256]{1,0:T(8,128)(2,1)S(1)}, bf16[800,256]{1,0:T(8,128)(2,1)S(1)}, u32[]{:S(2)}, u32[]{:S(2)}) collective-permute-start(bf16[800,256]{1,0:T(8,128)(2,1)S(1)} %collective-permute-done.1.refs_0_), channel_id=1, source_target_pairs={{0,1},{1,0},{2,3},{3,2},{4,5},{5,4},{6,7},{7,6},{8,9},{9,8},{10,11... | collective-permute-start | bytes 1228808 | tf_op jit(solution)/shard_map/ppermute | solution.py:251
  16.4 8.4 %collective-permute-start.4 = (bf16[800,256]{1,0:T(8,128)(2,1)S(1)}, bf16[800,256]{1,0:T(8,128)(2,1)S(1)}, u32[]{:S(2)}, u32[]{:S(2)}) collective-permute-start(bf16[800,256]{1,0:T(8,128)(2,1)S(1)} %collective-permute-done.3.refs_2_), channel_id=1, source_target_pairs={{0,1},{1,0},{2,3},{3,2},{4,5},{5,4},{6,7},{7,6},{8,9},{9,8},{10,11... | collective-permute-start | bytes 1228808 | tf_op jit(solution)/shard_map/ppermute | solution.py:251
  17.7 36.1 %collective-permute-start.5 = (bf16[800,256]{1,0:T(8,128)(2,1)S(1)}, bf16[800,256]{1,0:T(8,128)(2,1)S(1)}, u32[]{:S(2)}, u32[]{:S(2)}) collective-permute-start(bf16[800,256]{1,0:T(8,128)(2,1)S(1)} %collective-permute-done.1.refs_0_), channel_id=1, source_target_pairs={{0,66},{1,67},{2,64},{3,65},{4,70},{5,71},{6,68},{7,69},{8,74},{9,... | collective-permute-start | bytes 1228808 | tf_op jit(solution)/shard_map/ppermute | solution.py:251
  32.4 22.7 %collective-permute-start.8 = (bf16[800,256]{1,0:T(8,128)(2,1)S(1)}, bf16[800,256]{1,0:T(8,128)(2,1)S(1)}, u32[]{:S(2)}, u32[]{:S(2)}) collective-permute-start(bf16[800,256]{1,0:T(8,128)(2,1)S(1)} %get-tuple-element.31), channel_id=1, source_target_pairs={{0,1},{1,0},{2,3},{3,2},{4,5},{5,4},{6,7},{7,6},{8,9},{9,8},{10,11... | collective-permute-start | bytes 1228808 | tf_op jit(solution)/shard_map/ppermute | solution.py:251
  53.7 2.0 %collective-permute-start.7 = (bf16[800,256]{1,0:T(8,128)(2,1)S(1)}, bf16[800,256]{1,0:T(8,128)(2,1)S(1)}, u32[]{:S(2)}, u32[]{:S(2)}) collective-permute-start(bf16[800,256]{1,0:T(8,128)(2,1)S(1)} %get-tuple-element.29), channel_id=1, source_target_pairs={{0,1},{1,0},{2,3},{3,2},{4,5},{5,4},{6,7},{7,6},{8,9},{9,8},{10,11... | collective-permute-start | bytes 1228808 | tf_op jit(solution)/shard_map/ppermute | solution.py:251
  53.8 3.0 %collective-permute-start.6 = (bf16[800,256]{1,0:T(8,128)(2,1)S(1)}, bf16[800,256]{1,0:T(8,128)(2,1)S(1)}, u32[]{:S(2)}, u32[]{:S(2)}) collective-permute-start(bf16[800,256]{1,0:T(8,128)(2,1)S(1)} %collective-permute-done.5.refs_0_), channel_id=1, source_target_pairs={{0,1},{1,0},{2,3},{3,2},{4,5},{5,4},{6,7},{7,6},{8,9},{9,8},{10,11... | collective-permute-start | bytes 1228808 | tf_op jit(solution)/shard_map/ppermute | solution.py:251
  55.8 30.0 %collective-permute-start.10 = (bf16[800,256]{1,0:T(8,128)(2,1)S(1)}, bf16[800,256]{1,0:T(8,128)(2,1)S(1)}, u32[]{:S(2)}, u32[]{:S(2)}) collective-permute-start(bf16[800,256]{1,0:T(8,128)(2,1)S(1)} %add_convert_fusion.2), channel_id=1, source_target_pairs={{0,2},{1,3},{2,0},{3,1},{4,6},{5,7},{6,4},{7,5},{8,10},{9,11},{10,... | collective-permute-start | bytes 1228808 | tf_op jit(solution)/shard_map/ppermute | solution.py:251
  55.9 29.9 %collective-permute-start.11 = (bf16[800,256]{1,0:T(8,128)(2,1)S(1)}, bf16[800,256]{1,0:T(8,128)(2,1)S(1)}, u32[]{:S(2)}, u32[]{:S(2)}) collective-permute-start(bf16[800,256]{1,0:T(8,128)(2,1)S(1)} %add_convert_fusion.1), channel_id=1, source_target_pairs={{0,66},{1,67},{2,64},{3,65},{4,70},{5,71},{6,68},{7,69},{8,74},{9,... | collective-permute-start | bytes 1228808 | tf_op jit(solution)/shard_map/ppermute | solution.py:251
  60.7 25.1 %collective-permute-start.12 = (bf16[800,256]{1,0:T(8,128)(2,1)S(1)}, bf16[800,256]{1,0:T(8,128)(2,1)S(1)}, u32[]{:S(2)}, u32[]{:S(2)}) collective-permute-start(bf16[800,256]{1,0:T(8,128)(2,1)S(1)} %get-tuple-element.45), channel_id=1, source_target_pairs={{0,1},{1,0},{2,3},{3,2},{4,5},{5,4},{6,7},{7,6},{8,9},{9,8},{10,11... | collective-permute-start | bytes 1228808 | tf_op jit(solution)/shard_map/ppermute | solution.py:251
  76.3 12.0 %collective-permute-start.9 = (bf16[800,256]{1,0:T(8,128)(2,1)S(1)}, bf16[800,256]{1,0:T(8,128)(2,1)S(1)}, u32[]{:S(2)}, u32[]{:S(2)}) collective-permute-start(bf16[800,256]{1,0:T(8,128)(2,1)S(1)} %get-tuple-element.36), channel_id=1, source_target_pairs={{0,1},{1,0},{2,3},{3,2},{4,5},{5,4},{6,7},{7,6},{8,9},{9,8},{10,11... | collective-permute-start | bytes 1228808 | tf_op jit(solution)/shard_map/ppermute | solution.py:251
  85.9 12.7 %collective-permute-start.13 = (bf16[800,256]{1,0:T(8,128)(2,1)S(1)}, bf16[800,256]{1,0:T(8,128)(2,1)S(1)}, u32[]{:S(2)}, u32[]{:S(2)}) collective-permute-start(bf16[800,256]{1,0:T(8,128)(2,1)S(1)} %add_convert_fusion), channel_id=1, source_target_pairs={{0,64},{1,65},{2,66},{3,67},{4,68},{5,69},{6,70},{7,71},{8,72},{9,... | collective-permute-start | bytes 1228808 | tf_op jit(solution)/shard_map/ppermute | solution.py:251
  88.3 0.8 copy-start
  89.0 14.6 %all-to-all-start.1 = ((bf16[16,2,32,256]{3,2,1,0:T(8,128)(2,1)}), bf16[16,2,32,256]{3,2,1,0:T(8,128)(2,1)S(1)}, u32[]{:S(2)}, u32[]{:S(2)}) async-start(bf16[16,2,32,256]{3,2,1,0:T(8,128)(2,1)} %bitcast.3), calls=%async_computation.1 | async-start | bytes 1048576 | tf_op jit(solution)/shard_map/all_to_all | solution.py:298
  98.6 0.8 copy-start.1

commit v4 on v2

--- a/solution.py
+++ b/solution.py
@@ -113,10 +113,14 @@
         return jnp.logical_and(low > -100.0, high < 100.0)
 
     def fast_gradients(p):
-        w = weights(p, 0, cols)
-        store_image_grad(p, jnp.dot(w, txt_ref[...], preferred_element_type=jnp.float32))
-        part = jnp.dot(xt_refs[p][...], w, preferred_element_type=jnp.float32)
-        acc_ref[...] = part if p == 0 else acc_ref[...] + part
+        grad = None
+        for at in range(0, cols, 256):
+            w = weights(p, at, 256)
+            part = jnp.dot(w, txt_ref[at : at + 256, :], preferred_element_type=jnp.float32)
+            grad = part if grad is None else grad + part
+            part = jnp.dot(xt_refs[p][...], w, preferred_element_type=jnp.float32)
+            acc_ref[:, at : at + 256] = part if p == 0 else acc_ref[:, at : at + 256] + part
+        store_image_grad(p, grad)
 
     def slow_pair(p):
         e_ref, r_ref, c_ref = e_refs[p], r_refs[p], c_refs[p]

time: 104 us -> 104 us (level)
  no operation moved by 1% of the time
where the time goes in v4:
time: 104 us
  starting transfers between devices  64.4 us (62%)
  Pallas kernels  16.7 us (16%)
  waiting for transfers between devices  15.4 us (15%)
  local copies, waits for them, and re-layouts  3.3 us (3%)
  other arithmetic  3.2 us (3%)
    ppermute x13, starting transfers between devices, swapped(): return lax.ppermute(x, AXES, [(i, i ^ bits) for i in range(devices)])  53.1 us
    pallas_call x3, Pallas kernels, pair_call(): pl.pallas_call(functools.partial(pair_kernel, count=count, chunk=chunk, i...  16.7 us
    all_to_all x2, starting transfers between devices, body(): lax.all_to_all(sent, AXES, 0, 0, tiled=True, axis_index_groups=across_texts)  11.3 us
    ppermute x13, waiting for transfers between devices, swapped(): return lax.ppermute(x, AXES, [(i, i ^ bits) for i in range(devices)])  8.68 us
    all_to_all x2, waiting for transfers between devices, body(): lax.all_to_all(sent, AXES, 0, 0, tiled=True, axis_index_groups=across_texts)  6.74 us
  transfers between devices with their start and end apart: 15, of which 4 were waited for; matrix products, arithmetic and copies ran while one was open for 4% of the time, Pallas kernels for 16%

profile of v4, /device:TPU:1, one launch (start us, length us, event | category | flops | bytes accessed | tf_op | source)
XLA Modules:
  0.0 103.8 jit_solution(11960071136904486125)
XLA Ops:
  0.6 0.0 copy-start.1
  0.6 1.1 %reshape.72 = bf16[784,256]{1,0:T(8,128)(2,1)S(1)} reshape(bf16[196,4,256]{2,1,0:T(4,128)(2,1)} %bitcast.22) | data formatting | bytes 802816 | tf_op jit(solution)/shard_map/reshape | solution.py:259
  1.7 0.0 copy-done.1
  1.8 0.1 reshape.81
  1.9 0.1 pad.1.clone
  1.9 0.2 pad_maximum_fusion.refs_0_
  2.1 2.1 %collective-permute-start.1 = (bf16[800,256]{1,0:T(8,128)(2,1)S(1)}, bf16[800,256]{1,0:T(8,128)(2,1)S(1)}, u32[]{:S(2)}, u32[]{:S(2)}) collective-permute-start(bf16[800,256]{1,0:T(8,128)(2,1)S(1)} %pad_maximum_fusion.refs_0_), channel_id=1, source_target_pairs={{0,2},{1,3},{2,0},{3,1},{4,6},{5,7},{6,4},{7,5},{8,10},{9,11},{10,... | collective-permute-start | bytes 1228808 | tf_op jit(solution)/shard_map/ppermute | solution.py:256
  4.2 1.8 %collective-permute-start.3 = (bf16[800,256]{1,0:T(8,128)(2,1)S(1)}, bf16[800,256]{1,0:T(8,128)(2,1)S(1)}, u32[]{:S(2)}, u32[]{:S(2)}) collective-permute-start(bf16[800,256]{1,0:T(8,128)(2,1)S(1)} %pad_maximum_fusion.refs_0_), channel_id=1, source_target_pairs={{0,66},{1,67},{2,64},{3,65},{4,70},{5,71},{6,68},{7,69},{8,74},{9,... | collective-permute-start | bytes 1228808 | tf_op jit(solution)/shard_map/ppermute | solution.py:256
  6.1 0.0 copy-done
  6.1 0.9 broadcast_in_dim.22
  6.9 7.8 %all-to-all-start = ((bf16[16,2,32,256]{3,2,1,0:T(8,128)(2,1)}), bf16[16,2,32,256]{3,2,1,0:T(8,128)(2,1)S(1)}, u32[]{:S(2)}, u32[]{:S(2)}) async-start(bf16[16,2,32,256]{3,2,1,0:T(8,128)(2,1)} %broadcast_in_dim.22), calls=%async_computation | async-start | bytes 1048576 | tf_op jit(solution)/shard_map/all_to_all | solution.py:264
  14.7 1.6 %collective-permute-start = (bf16[800,256]{1,0:T(8,128)(2,1)S(1)}, bf16[800,256]{1,0:T(8,128)(2,1)S(1)}, u32[]{:S(2)}, u32[]{:S(2)}) collective-permute-start(bf16[800,256]{1,0:T(8,128)(2,1)S(1)} %pad_maximum_fusion.refs_0_), channel_id=1, source_target_pairs={{0,1},{1,0},{2,3},{3,2},{4,5},{5,4},{6,7},{7,6},{8,9},{9,8},{10,11... | collective-permute-start | bytes 1228808 | tf_op jit(solution)/shard_map/ppermute | solution.py:256
  16.3 0.0 collective-permute-done.1.refs_0_
  16.3 0.1 collective-permute-start.2
  16.4 0.0 collective-permute-done.3.refs_2_
  16.4 0.9 collective-permute-start.4
  17.3 1.8 %collective-permute-start.5 = (bf16[800,256]{1,0:T(8,128)(2,1)S(1)}, bf16[800,256]{1,0:T(8,128)(2,1)S(1)}, u32[]{:S(2)}, u32[]{:S(2)}) collective-permute-start(bf16[800,256]{1,0:T(8,128)(2,1)S(1)} %collective-permute-done.1.refs_0_), channel_id=1, source_target_pairs={{0,66},{1,67},{2,64},{3,65},{4,70},{5,71},{6,68},{7,69},{8,74},{9,... | collective-permute-start | bytes 1228808 | tf_op jit(solution)/shard_map/ppermute | solution.py:256
  19.2 0.0 collective-permute-done.refs_1_
  19.2 5.6 %all-to-all-done = bf16[16,2,32,256]{3,2,1,0:T(8,128)(2,1)S(1)} async-done(((bf16[16,2,32,256]{3,2,1,0:T(8,128)(2,1)}), bf16[16,2,32,256]{3,2,1,0:T(8,128)(2,1)S(1)}, u32[]{:S(2)}, u32[]{:S(2)}) %all-to-all-start) | async-done | bytes 524320 | tf_op jit(solution)/shard_map/all_to_all | solution.py:264
  24.8 0.0 collective-permute-done.2.refs_1_
  24.8 0.0 collective-permute-done.4.refs_3_
  24.8 7.4 %shard_map.58 = (f32[800,256]{1,0:T(8,128)S(1)}, f32[800,256]{1,0:T(8,128)S(1)}, bf16[2,800,256]{2,1,0:T(8,128)(2,1)S(1)}, f32[256,1024]{1,0:T(8,128)S(1)}, bf16[1024,256]{1,0:T(8,128)(2,1)S(1)}) custom-call(bf16[800,256]{1,0:T(8,128)(2,1)S(1)} %collective-permute-done.1.refs_0_, bf16[800,256]{1,0:T(8,128)(2,1)S(1)} %collective-permute-done.2.refs_1_, ...), custom_call_target="tpu_custom_call" | custom-call | tf_op jit(solution)/shard_map/pallas_call | solution.py:235
  32.2 0.0 collective-permute-done.5.refs_0_
  32.3 21.3 %collective-permute-start.7 = (bf16[2,800,256]{2,1,0:T(8,128)(2,1)S(1)}, bf16[2,800,256]{2,1,0:T(8,128)(2,1)S(1)}, u32[]{:S(2)}, u32[]{:S(2)}) collective-permute-start(bf16[2,800,256]{2,1,0:T(8,128)(2,1)S(1)} %get-tuple-element.32), channel_id=1, source_target_pairs={{0,1},{1,0},{2,3},{3,2},{4,5},{5,4},{6,7},{7,6},{8,9},{9,8},{10,11... | collective-permute-start | bytes 2457608 | tf_op jit(solution)/shard_map/ppermute | solution.py:256
  53.6 0.1 collective-permute-start.6
  53.7 1.9 %collective-permute-done.7 = bf16[2,800,256]{2,1,0:T(8,128)(2,1)S(1)} collective-permute-done((bf16[2,800,256]{2,1,0:T(8,128)(2,1)S(1)}, bf16[2,800,256]{2,1,0:T(8,128)(2,1)S(1)}, u32[]{:S(2)}, u32[]{:S(2)}) %collective-permute-start.7) | collective-permute-done | bytes 819232 | tf_op jit(solution)/shard_map/ppermute | solution.py:256
  55.5 0.2 fusion.4
  55.8 0.1 collective-permute-start.9
  55.9 0.9 collective-permute-start.10
  56.8 0.0 collective-permute-done.6.refs_1_
  56.8 4.0 %shard_map.59 = (f32[800,256]{1,0:T(8,128)S(1)}, bf16[1,800,256]{2,1,0:T(8,128)(2,1)S(1)}, f32[256,1024]{1,0:T(8,128)S(1)}) custom-call(bf16[800,256]{1,0:T(8,128)(2,1)S(1)} %collective-permute-done.5.refs_0_, bf16[800,256]{1,0:T(8,128)(2,1)S(1)} %collective-permute-done.6.refs_1_, bf16[1024,256]{1,0:T(8,128)(2,1)S(1)} %get-tuple-element.28.refs_2_, ...), custom_call_target="tpu_custom_call" | custom-call | tf_op jit(solution)/shard_map/pallas_call | solution.py:235
  60.8 10.4 %collective-permute-start.11 = (bf16[1,800,256]{2,1,0:T(8,128)(2,1)S(1)}, bf16[1,800,256]{2,1,0:T(8,128)(2,1)S(1)}, u32[]{:S(2)}, u32[]{:S(2)}) collective-permute-start(bf16[1,800,256]{2,1,0:T(8,128)(2,1)S(1)} %get-tuple-element.47), channel_id=1, source_target_pairs={{0,1},{1,0},{2,3},{3,2},{4,5},{5,4},{6,7},{7,6},{8,9},{9,8},{10,11... | collective-permute-start | bytes 1228808 | tf_op jit(solution)/shard_map/ppermute | solution.py:256
  71.3 5.2 %shard_map.60 = (f32[800,256]{1,0:T(8,128)S(1)}, bf16[1,800,256]{2,1,0:T(8,128)(2,1)S(1)}, bf16[1024,256]{1,0:T(8,128)(2,1)}) custom-call(bf16[800,256]{1,0:T(8,128)(2,1)S(1)} %pad_maximum_fusion.refs_0_, bf16[800,256]{1,0:T(8,128)(2,1)S(1)} %collective-permute-done.refs_1_, bf16[1024,256]{1,0:T(8,128)(2,1)S(1)} %get-tuple-element.28.refs_2_, ...), custom_call_target="tpu_custom_call" | custom-call | tf_op jit(solution)/shard_map/pallas_call | solution.py:235
  76.5 9.4 %collective-permute-start.8 = (bf16[1,800,256]{2,1,0:T(8,128)(2,1)S(1)}, bf16[1,800,256]{2,1,0:T(8,128)(2,1)}, u32[]{:S(2)}, u32[]{:S(2)}) collective-permute-start(bf16[1,800,256]{2,1,0:T(8,128)(2,1)S(1)} %get-tuple-element.38), channel_id=1, source_target_pairs={{0,1},{1,0},{2,3},{3,2},{4,5},{5,4},{6,7},{7,6},{8,9},{9,8},{10,11... | collective-permute-start | bytes 1228808 | tf_op jit(solution)/shard_map/ppermute | solution.py:256
  86.0 0.0 collective-permute-done.9
  86.0 0.0 collective-permute-done.10
  86.0 0.0 collective-permute-done.11
  86.0 0.1 fusion
  86.1 2.4 %collective-permute-start.12 = (bf16[800,256]{1,0:T(8,128)(2,1)S(1)}, bf16[800,256]{1,0:T(8,128)(2,1)}, u32[]{:S(2)}, u32[]{:S(2)}) collective-permute-start(bf16[800,256]{1,0:T(8,128)(2,1)S(1)} %fusion), channel_id=1, source_target_pairs={{0,64},{1,65},{2,66},{3,67},{4,68},{5,69},{6,70},{7,71},{8,72},{9,... | collective-permute-start | bytes 1228808 | tf_op jit(solution)/shard_map/ppermute | solution.py:256
  88.5 0.0 collective-permute-done.8
  88.5 3.6 %all-to-all-start.1 = ((bf16[16,2,32,256]{3,2,1,0:T(8,128)(2,1)}), bf16[16,2,32,256]{3,2,1,0:T(8,128)(2,1)S(1)}, u32[]{:S(2)}, u32[]{:S(2)}) async-start(bf16[16,2,32,256]{3,2,1,0:T(8,128)(2,1)} %bitcast.7), calls=%async_computation.1 | async-start | bytes 1048576 | tf_op jit(solution)/shard_map/all_to_all | solution.py:304
  92.1 6.8 %collective-permute-done.12 = bf16[800,256]{1,0:T(8,128)(2,1)} collective-permute-done((bf16[800,256]{1,0:T(8,128)(2,1)S(1)}, bf16[800,256]{1,0:T(8,128)(2,1)}, u32[]{:S(2)}, u32[]{:S(2)}) %collective-permute-start.12) | collective-permute-done | bytes 409632 | tf_op jit(solution)/shard_map/ppermute | solution.py:256
  98.8 1.3 %fusion.3 = f32[800,256]{1,0:T(8,128)S(1)} fusion(f32[800,256]{1,0:T(8,128)S(1)} %get-tuple-element.37, bf16[800,256]{1,0:T(8,128)(2,1)} %collective-permute-done.12, bf16[800,256]{1,0:T(8,128)(2,1)S(1)} %collective-permute-done.10, bf16[800,256]{1,0:T(8,128)(2,1)S(1)} %collective-permute-done.9, bf16[1,800,256]{2,1,0:T(8,128)(2,1)} %collective-permute-done.8), kind=kLoop, calls=%fused_computation.6 | loop fusion | flops 1638400 | bytes 3276800 | tf_op jit(solution)/shard_map/add | solution.py:299
  100.2 0.1 slice.34
  100.3 1.1 %reshape.74 = f32[196,4,256]{2,1,0:T(4,128)} reshape(f32[784,256]{1,0:T(8,128)S(1)} %slice.34) | data formatting | bytes 1605632 | tf_op jit(solution)/shard_map/reshape | solution.py:300
  101.4 0.6 fusion.6
  102.0 1.1 %all-to-all-done.1 = bf16[16,2,32,256]{3,2,1,0:T(8,128)(2,1)S(1)} async-done(((bf16[16,2,32,256]{3,2,1,0:T(8,128)(2,1)}), bf16[16,2,32,256]{3,2,1,0:T(8,128)(2,1)S(1)}, u32[]{:S(2)}, u32[]{:S(2)}) %all-to-all-start.1) | async-done | bytes 524320 | tf_op jit(solution)/shard_map/all_to_all | solution.py:304
  103.1 0.7 convert_reduce_fusion
  (5 shorter events, 0.0 us)
Async XLA Ops:
  0.6 1.1 %copy-start.1 = (s32[4]{0:T(128)S(1)}, s32[4]{0:T(128)}, u32[]{:S(2)}) copy-start(s32[4]{0:T(128)} %param.5) | copy-start | bytes 52
  1.9 4.1 %copy-start = (bf16[2,32,256]{2,1,0:T(8,128)(2,1)S(1)}, bf16[2,32,256]{2,1,0:T(8,128)(2,1)}, u32[]{:S(2)}) copy-start(bf16[2,32,256]{2,1,0:T(8,128)(2,1)} %param.4) | copy-start | bytes 98308
  2.1 14.2 %collective-permute-start.1 = (bf16[800,256]{1,0:T(8,128)(2,1)S(1)}, bf16[800,256]{1,0:T(8,128)(2,1)S(1)}, u32[]{:S(2)}, u32[]{:S(2)}) collective-permute-start(bf16[800,256]{1,0:T(8,128)(2,1)S(1)} %pad_maximum_fusion.refs_0_), channel_id=1, source_target_pairs={{0,2},{1,3},{2,0},{3,1},{4,6},{5,7},{6,4},{7,5},{8,10},{9,11},{10,... | collective-permute-start | bytes 1228808 | tf_op jit(solution)/shard_map/ppermute | solution.py:256
  4.2 12.2 %collective-permute-start.3 = (bf16[800,256]{1,0:T(8,128)(2,1)S(1)}, bf16[800,256]{1,0:T(8,128)(2,1)S(1)}, u32[]{:S(2)}, u32[]{:S(2)}) collective-permute-start(bf16[800,256]{1,0:T(8,128)(2,1)S(1)} %pad_maximum_fusion.refs_0_), channel_id=1, source_target_pairs={{0,66},{1,67},{2,64},{3,65},{4,70},{5,71},{6,68},{7,69},{8,74},{9,... | collective-permute-start | bytes 1228808 | tf_op jit(solution)/shard_map/ppermute | solution.py:256
  6.9 17.9 %all-to-all-start = ((bf16[16,2,32,256]{3,2,1,0:T(8,128)(2,1)}), bf16[16,2,32,256]{3,2,1,0:T(8,128)(2,1)S(1)}, u32[]{:S(2)}, u32[]{:S(2)}) async-start(bf16[16,2,32,256]{3,2,1,0:T(8,128)(2,1)} %broadcast_in_dim.22), calls=%async_computation | async-start | bytes 1048576 | tf_op jit(solution)/shard_map/all_to_all | solution.py:264
  14.7 4.5 %collective-permute-start = (bf16[800,256]{1,0:T(8,128)(2,1)S(1)}, bf16[800,256]{1,0:T(8,128)(2,1)S(1)}, u32[]{:S(2)}, u32[]{:S(2)}) collective-permute-start(bf16[800,256]{1,0:T(8,128)(2,1)S(1)} %pad_maximum_fusion.refs_0_), channel_id=1, source_target_pairs={{0,1},{1,0},{2,3},{3,2},{4,5},{5,4},{6,7},{7,6},{8,9},{9,8},{10,11... | collective-permute-start | bytes 1228808 | tf_op jit(solution)/shard_map/ppermute | solution.py:256
  16.3 8.5 %collective-permute-start.2 = (bf16[800,256]{1,0:T(8,128)(2,1)S(1)}, bf16[800,256]{1,0:T(8,128)(2,1)S(1)}, u32[]{:S(2)}, u32[]{:S(2)}) collective-permute-start(bf16[800,256]{1,0:T(8,128)(2,1)S(1)} %collective-permute-done.1.refs_0_), channel_id=1, source_target_pairs={{0,1},{1,0},{2,3},{3,2},{4,5},{5,4},{6,7},{7,6},{8,9},{9,8},{10,11... | collective-permute-start | bytes 1228808 | tf_op jit(solution)/shard_map/ppermute | solution.py:256
  16.4 8.4 %collective-permute-start.4 = (bf16[800,256]{1,0:T(8,128)(2,1)S(1)}, bf16[800,256]{1,0:T(8,128)(2,1)S(1)}, u32[]{:S(2)}, u32[]{:S(2)}) collective-permute-start(bf16[800,256]{1,0:T(8,128)(2,1)S(1)} %collective-permute-done.3.refs_2_), channel_id=1, source_target_pairs={{0,1},{1,0},{2,3},{3,2},{4,5},{5,4},{6,7},{7,6},{8,9},{9,8},{10,11... | collective-permute-start | bytes 1228808 | tf_op jit(solution)/shard_map/ppermute | solution.py:256
  17.3 14.9 %collective-permute-start.5 = (bf16[800,256]{1,0:T(8,128)(2,1)S(1)}, bf16[800,256]{1,0:T(8,128)(2,1)S(1)}, u32[]{:S(2)}, u32[]{:S(2)}) collective-permute-start(bf16[800,256]{1,0:T(8,128)(2,1)S(1)} %collective-permute-done.1.refs_0_), channel_id=1, source_target_pairs={{0,66},{1,67},{2,64},{3,65},{4,70},{5,71},{6,68},{7,69},{8,74},{9,... | collective-permute-start | bytes 1228808 | tf_op jit(solution)/shard_map/ppermute | solution.py:256
  32.3 23.3 %collective-permute-start.7 = (bf16[2,800,256]{2,1,0:T(8,128)(2,1)S(1)}, bf16[2,800,256]{2,1,0:T(8,128)(2,1)S(1)}, u32[]{:S(2)}, u32[]{:S(2)}) collective-permute-start(bf16[2,800,256]{2,1,0:T(8,128)(2,1)S(1)} %get-tuple-element.32), channel_id=1, source_target_pairs={{0,1},{1,0},{2,3},{3,2},{4,5},{5,4},{6,7},{7,6},{8,9},{9,8},{10,11... | collective-permute-start | bytes 2457608 | tf_op jit(solution)/shard_map/ppermute | solution.py:256
  53.6 3.2 %collective-permute-start.6 = (bf16[800,256]{1,0:T(8,128)(2,1)S(1)}, bf16[800,256]{1,0:T(8,128)(2,1)S(1)}, u32[]{:S(2)}, u32[]{:S(2)}) collective-permute-start(bf16[800,256]{1,0:T(8,128)(2,1)S(1)} %collective-permute-done.5.refs_0_), channel_id=1, source_target_pairs={{0,1},{1,0},{2,3},{3,2},{4,5},{5,4},{6,7},{7,6},{8,9},{9,8},{10,11... | collective-permute-start | bytes 1228808 | tf_op jit(solution)/shard_map/ppermute | solution.py:256
  55.8 30.2 %collective-permute-start.9 = (bf16[800,256]{1,0:T(8,128)(2,1)S(1)}, bf16[800,256]{1,0:T(8,128)(2,1)S(1)}, u32[]{:S(2)}, u32[]{:S(2)}) collective-permute-start(bf16[800,256]{1,0:T(8,128)(2,1)S(1)} %get-tuple-element.41), channel_id=1, source_target_pairs={{0,2},{1,3},{2,0},{3,1},{4,6},{5,7},{6,4},{7,5},{8,10},{9,11},{10,... | collective-permute-start | bytes 1228808 | tf_op jit(solution)/shard_map/ppermute | solution.py:256
  55.9 30.1 %collective-permute-start.10 = (bf16[800,256]{1,0:T(8,128)(2,1)S(1)}, bf16[800,256]{1,0:T(8,128)(2,1)S(1)}, u32[]{:S(2)}, u32[]{:S(2)}) collective-permute-start(bf16[800,256]{1,0:T(8,128)(2,1)S(1)} %get-tuple-element.42), channel_id=1, source_target_pairs={{0,66},{1,67},{2,64},{3,65},{4,70},{5,71},{6,68},{7,69},{8,74},{9,... | collective-permute-start | bytes 1228808 | tf_op jit(solution)/shard_map/ppermute | solution.py:256
  60.8 25.1 %collective-permute-start.11 = (bf16[1,800,256]{2,1,0:T(8,128)(2,1)S(1)}, bf16[1,800,256]{2,1,0:T(8,128)(2,1)S(1)}, u32[]{:S(2)}, u32[]{:S(2)}) collective-permute-start(bf16[1,800,256]{2,1,0:T(8,128)(2,1)S(1)} %get-tuple-element.47), channel_id=1, source_target_pairs={{0,1},{1,0},{2,3},{3,2},{4,5},{5,4},{6,7},{7,6},{8,9},{9,8},{10,11... | collective-permute-start | bytes 1228808 | tf_op jit(solution)/shard_map/ppermute | solution.py:256
  76.5 12.0 %collective-permute-start.8 = (bf16[1,800,256]{2,1,0:T(8,128)(2,1)S(1)}, bf16[1,800,256]{2,1,0:T(8,128)(2,1)}, u32[]{:S(2)}, u32[]{:S(2)}) collective-permute-start(bf16[1,800,256]{2,1,0:T(8,128)(2,1)S(1)} %get-tuple-element.38), channel_id=1, source_target_pairs={{0,1},{1,0},{2,3},{3,2},{4,5},{5,4},{6,7},{7,6},{8,9},{9,8},{10,11... | collective-permute-start | bytes 1228808 | tf_op jit(solution)/shard_map/ppermute | solution.py:256
  86.1 12.8 %collective-permute-start.12 = (bf16[800,256]{1,0:T(8,128)(2,1)S(1)}, bf16[800,256]{1,0:T(8,128)(2,1)}, u32[]{:S(2)}, u32[]{:S(2)}) collective-permute-start(bf16[800,256]{1,0:T(8,128)(2,1)S(1)} %fusion), channel_id=1, source_target_pairs={{0,64},{1,65},{2,66},{3,67},{4,68},{5,69},{6,70},{7,71},{8,72},{9,... | collective-permute-start | bytes 1228808 | tf_op jit(solution)/shard_map/ppermute | solution.py:256
  88.5 14.6 %all-to-all-start.1 = ((bf16[16,2,32,256]{3,2,1,0:T(8,128)(2,1)}), bf16[16,2,32,256]{3,2,1,0:T(8,128)(2,1)S(1)}, u32[]{:S(2)}, u32[]{:S(2)}) async-start(bf16[16,2,32,256]{3,2,1,0:T(8,128)(2,1)} %bitcast.7), calls=%async_computation.1 | async-start | bytes 1048576 | tf_op jit(solution)/shard_map/all_to_all | solution.py:304

commit v5 on v1

--- a/solution.py
+++ b/solution.py
@@ -14,7 +14,6 @@
 CHUNK = 1024
 AXES = ("blk", "grp")
 CORE, X_LOW, X_HIGH = 1, 2, 64
-NEIGHBOURS = (X_LOW, X_LOW | X_HIGH, X_HIGH)
 CLASS = CORE | X_LOW | X_HIGH
 
 
@@ -111,10 +110,14 @@
         return jnp.logical_and(low > -100.0, high < 100.0)
 
     def fast_gradients(p):
-        w = weights(p, 0, cols)
-        store_image_grad(p, jnp.dot(w, txt_ref[...], preferred_element_type=jnp.float32))
-        part = jnp.dot(xt_refs[p][...], w, preferred_element_type=jnp.float32)
-        acc_ref[...] = part if p == 0 else acc_ref[...] + part
+        grad = None
+        for at in range(0, cols, 256):
+            w = weights(p, at, 256)
+            part = jnp.dot(w, txt_ref[at : at + 256, :], preferred_element_type=jnp.float32)
+            grad = part if grad is None else grad + part
+            part = jnp.dot(xt_refs[p][...], w, preferred_element_type=jnp.float32)
+            acc_ref[:, at : at + 256] = part if p == 0 else acc_ref[:, at : at + 256] + part
+        store_image_grad(p, grad)
 
     def slow_pair(p):
         e_ref, r_ref, c_ref = e_refs[p], r_refs[p], c_refs[p]
@@ -191,12 +194,12 @@
 
     total = acc_ref[...] if first else acc_ref[...] + gin_ref[...]
     if last:
-        for j in range(cols // 128):
-            turned = total[:, 128 * j : 128 * (j + 1)].astype(gt_ref.dtype).T.astype(jnp.float32)
-            for i in range(128 // texts):
-                for h, part in enumerate(lanes(turned[i * texts : (i + 1) * texts])):
-                    turn_ref[h, pl.ds(j * (128 // texts) + i, texts, stride=txt_tok), :] = part
-        gt_ref[...] = jnp.concatenate([turn_ref[h] for h in range(dim // 128)], axis=1).astype(gt_ref.dtype)
+        row = lax.broadcasted_iota(jnp.int32, (cols, 1), 0)
+        source = (row % txt_tok) * texts + row // txt_tok
+        pick = jnp.where(lax.broadcasted_iota(jnp.int32, (cols, cols), 1) == source, 1.0, 0.0).astype(gt_ref.dtype)
+        gt_ref[...] = lax.dot_general(
+            pick, total.astype(gt_ref.dtype), (((1,), (1,)), ((), ())), preferred_element_type=jnp.float32
+        ).astype(gt_ref.dtype)
     else:
         gt_ref[...] = total
 
@@ -250,7 +253,8 @@
 
     labels = jnp.broadcast_to(jnp.tile(positives.astype(jnp.bfloat16), EXTRA // own_images)[:, None], (EXTRA, dim))
     own = jnp.concatenate([image_tokens.transpose(1, 0, 2).reshape(rows, dim), labels], axis=0)
-    over = {bits: swapped(own, bits) for bits in NEIGHBOURS}
+    over = {bits: swapped(own, bits) for bits in (X_LOW, X_LOW | X_HIGH)}
+    over[X_HIGH] = swapped(over[X_LOW], X_LOW | X_HIGH)
 
     sent = jnp.broadcast_to(text_tokens[None], (peers, own_texts, txt_tok, dim))
     texts = lax.all_to_all(sent, AXES, 0, 0, tiled=True, axis_index_groups=across_texts)
@@ -275,16 +279,15 @@
         gathered = out[len(images)]
         return out[: len(images)]
 
-    near, far = work([X_LOW])
-    found[X_LOW] = (near, swapped(far, CORE))
-    near, far = work([X_BOTH])
-    found[X_BOTH] = (near, swapped(far, CORE))
+    out = work([X_LOW, X_BOTH])
+    found[X_LOW] = (out[0], swapped(out[1], CORE))
+    found[X_BOTH] = (out[2], swapped(out[3], CORE))
     *sent, gathered = lax.optimization_barrier((summed(*found[X_LOW]), summed(*found[X_BOTH]), gathered))
     back = [swapped(sent[0], X_LOW), swapped(sent[1], X_BOTH)]
     near, far = work([X_HIGH])
     met = swapped(far, CORE)
     out = work([0], last=True)
-    back, met = lax.optimization_barrier((back, met))
+    back, near = lax.optimization_barrier((back, near))
     found[X_HIGH] = (near, met)
     met, gathered = lax.optimization_barrier((swapped(out[1], CORE), gathered))
     found[0] = (out[0], met)

time: 105 us -> 104 us (level)
  Pallas kernels: 17.8 us -> 16.7 us
    pallas_call x4 -> x3, Pallas kernels: 17.8 us -> 16.7 us  [pair_call(): pl.pallas_call(functools.partial(pair_kernel, count=count, chunk=chunk, i...]
  transfers between devices with their start and end apart: 16 -> 16, of which waited for: 4 -> 6; matrix products, arithmetic and copies ran while one was open for 4% -> 4% of each run, Pallas kernels for 17% -> 16%
where the time goes in v5:
time: 104 us
  starting transfers between devices  65 us (62%)
  Pallas kernels  16.7 us (16%)
  waiting for transfers between devices  14.9 us (14%)
  local copies, waits for them, and re-layouts  3.3 us (3%)
  other arithmetic  3.05 us (3%)
    ppermute x14, starting transfers between devices, swapped(): return lax.ppermute(x, AXES, [(i, i ^ bits) for i in range(devices)])  53.6 us
    pallas_call x3, Pallas kernels, pair_call(): pl.pallas_call(functools.partial(pair_kernel, count=count, chunk=chunk, i...  16.7 us
    all_to_all x2, starting transfers between devices, body(): lax.all_to_all(sent, AXES, 0, 0, tiled=True, axis_index_groups=across_texts)  11.3 us
    ppermute x14, waiting for transfers between devices, swapped(): return lax.ppermute(x, AXES, [(i, i ^ bits) for i in range(devices)])  8.12 us
    all_to_all x2, waiting for transfers between devices, body(): lax.all_to_all(sent, AXES, 0, 0, tiled=True, axis_index_groups=across_texts)  6.81 us
  transfers between devices with their start and end apart: 16, of which 6 were waited for; matrix products, arithmetic and copies ran while one was open for 4% of the time, Pallas kernels for 16%

profile of v5, /device:TPU:1, one launch (start us, length us, event | category | flops | bytes accessed | tf_op | source)
XLA Modules:
  0.0 103.7 jit_solution(445054281429507935)
XLA Ops:
  0.6 1.1 %reshape.64 = bf16[784,256]{1,0:T(8,128)(2,1)S(1)} reshape(bf16[196,4,256]{2,1,0:T(4,128)(2,1)} %bitcast.6) | data formatting | bytes 802816 | tf_op jit(solution)/shard_map/reshape | solution.py:255
  1.8 0.1 reshape.69
  1.9 0.1 pad.1.clone
  1.9 0.2 pad_maximum_fusion.refs_0_
  2.1 2.1 %collective-permute-start.1 = (bf16[800,256]{1,0:T(8,128)(2,1)S(1)}, bf16[800,256]{1,0:T(8,128)(2,1)S(1)}, u32[]{:S(2)}, u32[]{:S(2)}) collective-permute-start(bf16[800,256]{1,0:T(8,128)(2,1)S(1)} %pad_maximum_fusion.refs_0_), channel_id=1, source_target_pairs={{0,2},{1,3},{2,0},{3,1},{4,6},{5,7},{6,4},{7,5},{8,10},{9,11},{10,... | collective-permute-start | bytes 1228808 | tf_op jit(solution)/shard_map/ppermute | solution.py:252
  4.2 1.8 %collective-permute-start.3 = (bf16[800,256]{1,0:T(8,128)(2,1)S(1)}, bf16[800,256]{1,0:T(8,128)(2,1)S(1)}, u32[]{:S(2)}, u32[]{:S(2)}) collective-permute-start(bf16[800,256]{1,0:T(8,128)(2,1)S(1)} %pad_maximum_fusion.refs_0_), channel_id=1, source_target_pairs={{0,66},{1,67},{2,64},{3,65},{4,70},{5,71},{6,68},{7,69},{8,74},{9,... | collective-permute-start | bytes 1228808 | tf_op jit(solution)/shard_map/ppermute | solution.py:252
  6.1 0.9 broadcast_in_dim.10
  6.9 7.8 %all-to-all-start = ((bf16[16,2,32,256]{3,2,1,0:T(8,128)(2,1)}), bf16[16,2,32,256]{3,2,1,0:T(8,128)(2,1)S(1)}, u32[]{:S(2)}, u32[]{:S(2)}) async-start(bf16[16,2,32,256]{3,2,1,0:T(8,128)(2,1)} %broadcast_in_dim.10), calls=%async_computation | async-start | bytes 1048576 | tf_op jit(solution)/shard_map/all_to_all | solution.py:260
  14.7 0.0 collective-permute-done.1.refs_0_
  14.7 1.6 %collective-permute-start.2 = (bf16[800,256]{1,0:T(8,128)(2,1)S(1)}, bf16[800,256]{1,0:T(8,128)(2,1)S(1)}, u32[]{:S(2)}, u32[]{:S(2)}) collective-permute-start(bf16[800,256]{1,0:T(8,128)(2,1)S(1)} %collective-permute-done.1.refs_0_), channel_id=1, source_target_pairs={{0,1},{1,0},{2,3},{3,2},{4,5},{5,4},{6,7},{7,6},{8,9},{9,8},{10,11... | collective-permute-start | bytes 1228808 | tf_op jit(solution)/shard_map/ppermute | solution.py:252
  16.3 0.0 collective-permute-done.3.refs_2_
  16.3 1.0 collective-permute-start.4
  17.4 1.9 %collective-permute-start.5 = (bf16[800,256]{1,0:T(8,128)(2,1)S(1)}, bf16[800,256]{1,0:T(8,128)(2,1)S(1)}, u32[]{:S(2)}, u32[]{:S(2)}) collective-permute-start(bf16[800,256]{1,0:T(8,128)(2,1)S(1)} %collective-permute-done.1.refs_0_), channel_id=1, source_target_pairs={{0,66},{1,67},{2,64},{3,65},{4,70},{5,71},{6,68},{7,69},{8,74},{9,... | collective-permute-start | bytes 1228808 | tf_op jit(solution)/shard_map/ppermute | solution.py:252
  19.2 5.6 %all-to-all-done = bf16[16,2,32,256]{3,2,1,0:T(8,128)(2,1)S(1)} async-done(((bf16[16,2,32,256]{3,2,1,0:T(8,128)(2,1)}), bf16[16,2,32,256]{3,2,1,0:T(8,128)(2,1)S(1)}, u32[]{:S(2)}, u32[]{:S(2)}) %all-to-all-start) | async-done | bytes 524320 | tf_op jit(solution)/shard_map/all_to_all | solution.py:260
  24.8 0.0 collective-permute-done.2.refs_1_
  24.8 0.0 collective-permute-done.4.refs_3_
  24.8 7.4 %shard_map.58 = (f32[800,256]{1,0:T(8,128)S(1)}, bf16[800,256]{1,0:T(8,128)(2,1)S(1)}, f32[800,256]{1,0:T(8,128)S(1)}, bf16[800,256]{1,0:T(8,128)(2,1)S(1)}, f32...) custom-call(bf16[800,256]{1,0:T(8,128)(2,1)S(1)} %collective-permute-done.1.refs_0_, ...), custom_call_target="tpu_custom_call" | custom-call | tf_op jit(solution)/shard_map/pallas_call | solution.py:231
  32.3 21.3 %collective-permute-start.8 = (bf16[800,256]{1,0:T(8,128)(2,1)S(1)}, bf16[800,256]{1,0:T(8,128)(2,1)S(1)}, u32[]{:S(2)}, u32[]{:S(2)}) collective-permute-start(bf16[800,256]{1,0:T(8,128)(2,1)S(1)} %get-tuple-element.27), channel_id=1, source_target_pairs={{0,1},{1,0},{2,3},{3,2},{4,5},{5,4},{6,7},{7,6},{8,9},{9,8},{10,11... | collective-permute-start | bytes 1228808 | tf_op jit(solution)/shard_map/ppermute | solution.py:252
  53.6 0.1 collective-permute-start.7
  53.7 0.4 collective-permute-start
  54.1 0.0 collective-permute-done.5.refs_0_
  54.1 0.1 collective-permute-start.6
  54.2 0.8 collective-permute-done.8
  54.9 0.1 add_convert_fusion.1
  55.0 0.5 collective-permute-done.7
  55.5 0.1 add_convert_fusion.2
  55.6 0.1 collective-permute-start.10
  55.7 0.9 collective-permute-start.11
  56.6 0.1 collective-permute-done.6.refs_1_
  56.7 4.0 %shard_map.59 = (f32[800,256]{1,0:T(8,128)S(1)}, bf16[800,256]{1,0:T(8,128)(2,1)S(1)}, f32[256,1024]{1,0:T(8,128)S(1)}) custom-call(bf16[800,256]{1,0:T(8,128)(2,1)S(1)} %collective-permute-done.5.refs_0_, bf16[800,256]{1,0:T(8,128)(2,1)S(1)} %collective-permute-done.6.refs_1_, bf16[1024,256]{1,0:T(8,128)(2,1)S(1)} %get-tuple-element.23.refs_2_, ...), custom_call_target="tpu_custom_call" | custom-call | tf_op jit(solution)/shard_map/pallas_call | solution.py:231
  60.7 10.4 %collective-permute-start.12 = (bf16[800,256]{1,0:T(8,128)(2,1)S(1)}, bf16[800,256]{1,0:T(8,128)(2,1)S(1)}, u32[]{:S(2)}, u32[]{:S(2)}) collective-permute-start(bf16[800,256]{1,0:T(8,128)(2,1)S(1)} %get-tuple-element.41), channel_id=1, source_target_pairs={{0,1},{1,0},{2,3},{3,2},{4,5},{5,4},{6,7},{7,6},{8,9},{9,8},{10,11... | collective-permute-start | bytes 1228808 | tf_op jit(solution)/shard_map/ppermute | solution.py:252
  71.1 0.0 collective-permute-done.refs_1_
  71.1 5.2 %shard_map.60 = (f32[800,256]{1,0:T(8,128)S(1)}, bf16[800,256]{1,0:T(8,128)(2,1)S(1)}, bf16[1024,256]{1,0:T(8,128)(2,1)}) custom-call(bf16[800,256]{1,0:T(8,128)(2,1)S(1)} %pad_maximum_fusion.refs_0_, bf16[800,256]{1,0:T(8,128)(2,1)S(1)} %collective-permute-done.refs_1_, bf16[1024,256]{1,0:T(8,128)(2,1)S(1)} %get-tuple-element.23.refs_2_, ...), custom_call_target="tpu_custom_call" | custom-call | tf_op jit(solution)/shard_map/pallas_call | solution.py:231
  76.4 9.5 %collective-permute-start.9 = (bf16[800,256]{1,0:T(8,128)(2,1)S(1)}, bf16[800,256]{1,0:T(8,128)(2,1)S(1)}, u32[]{:S(2)}, u32[]{:S(2)}) collective-permute-start(bf16[800,256]{1,0:T(8,128)(2,1)S(1)} %get-tuple-element.32), channel_id=1, source_target_pairs={{0,1},{1,0},{2,3},{3,2},{4,5},{5,4},{6,7},{7,6},{8,9},{9,8},{10,11... | collective-permute-start | bytes 1228808 | tf_op jit(solution)/shard_map/ppermute | solution.py:252
  85.8 0.0 collective-permute-done.10
  85.8 0.0 collective-permute-done.11
  85.8 0.0 collective-permute-done.12
  85.8 0.1 add_convert_fusion
  85.9 2.4 %collective-permute-start.13 = (bf16[800,256]{1,0:T(8,128)(2,1)S(1)}, bf16[800,256]{1,0:T(8,128)(2,1)}, u32[]{:S(2)}, u32[]{:S(2)}) collective-permute-start(bf16[800,256]{1,0:T(8,128)(2,1)S(1)} %add_convert_fusion), channel_id=1, source_target_pairs={{0,64},{1,65},{2,66},{3,67},{4,68},{5,69},{6,70},{7,71},{8,72},{9,... | collective-permute-start | bytes 1228808 | tf_op jit(solution)/shard_map/ppermute | solution.py:252
  88.4 0.0 collective-permute-done.9
  88.4 3.6 %all-to-all-start.1 = ((bf16[16,2,32,256]{3,2,1,0:T(8,128)(2,1)}), bf16[16,2,32,256]{3,2,1,0:T(8,128)(2,1)S(1)}, u32[]{:S(2)}, u32[]{:S(2)}) async-start(bf16[16,2,32,256]{3,2,1,0:T(8,128)(2,1)} %bitcast.3), calls=%async_computation.1 | async-start | bytes 1048576 | tf_op jit(solution)/shard_map/all_to_all | solution.py:303
  91.9 6.8 %collective-permute-done.13 = bf16[800,256]{1,0:T(8,128)(2,1)} collective-permute-done((bf16[800,256]{1,0:T(8,128)(2,1)S(1)}, bf16[800,256]{1,0:T(8,128)(2,1)}, u32[]{:S(2)}, u32[]{:S(2)}) %collective-permute-start.13) | collective-permute-done | bytes 409632 | tf_op jit(solution)/shard_map/ppermute | solution.py:252
  98.7 1.2 %convert_add_fusion = f32[800,256]{1,0:T(8,128)S(1)} fusion(bf16[800,256]{1,0:T(8,128)(2,1)} %collective-permute-done.13, bf16[800,256]{1,0:T(8,128)(2,1)S(1)} %collective-permute-done.11, bf16[800,256]{1,0:T(8,128)(2,1)S(1)} %collective-permute-done.10, f32[800,256]{1,0:T(8,128)S(1)} %get-tuple-element.31, bf16[800,256]{1,0:T(8,128)(2,1)S(1)} %collective-permute-done.9), kind=kLoop, calls=%fused_computation.1 | loop fusion | flops 1638400 | bytes 3276800 | tf_op jit(solution)/shard_map/add | solution.py:298
  99.9 0.1 slice.24
  100.0 1.1 %reshape.66 = f32[196,4,256]{2,1,0:T(4,128)} reshape(f32[784,256]{1,0:T(8,128)S(1)} %slice.24) | data formatting | bytes 1605632 | tf_op jit(solution)/shard_map/reshape | solution.py:299
  101.1 0.6 fusion
  101.8 1.2 %all-to-all-done.1 = bf16[16,2,32,256]{3,2,1,0:T(8,128)(2,1)S(1)} async-done(((bf16[16,2,32,256]{3,2,1,0:T(8,128)(2,1)}), bf16[16,2,32,256]{3,2,1,0:T(8,128)(2,1)S(1)}, u32[]{:S(2)}, u32[]{:S(2)}) %all-to-all-start.1) | async-done | bytes 524320 | tf_op jit(solution)/shard_map/all_to_all | solution.py:303
  103.0 0.7 convert_reduce_fusion
  (8 shorter events, 0.0 us)
Async XLA Ops:
  0.6 1.1 %copy-start.1 = (s32[4]{0:T(128)S(1)}, s32[4]{0:T(128)}, u32[]{:S(2)}) copy-start(s32[4]{0:T(128)} %param.5) | copy-start | bytes 52
  1.9 4.1 %copy-start = (bf16[2,32,256]{2,1,0:T(8,128)(2,1)S(1)}, bf16[2,32,256]{2,1,0:T(8,128)(2,1)}, u32[]{:S(2)}) copy-start(bf16[2,32,256]{2,1,0:T(8,128)(2,1)} %param.4) | copy-start | bytes 98308
  2.1 12.6 %collective-permute-start.1 = (bf16[800,256]{1,0:T(8,128)(2,1)S(1)}, bf16[800,256]{1,0:T(8,128)(2,1)S(1)}, u32[]{:S(2)}, u32[]{:S(2)}) collective-permute-start(bf16[800,256]{1,0:T(8,128)(2,1)S(1)} %pad_maximum_fusion.refs_0_), channel_id=1, source_target_pairs={{0,2},{1,3},{2,0},{3,1},{4,6},{5,7},{6,4},{7,5},{8,10},{9,11},{10,... | collective-permute-start | bytes 1228808 | tf_op jit(solution)/shard_map/ppermute | solution.py:252
  4.2 12.1 %collective-permute-start.3 = (bf16[800,256]{1,0:T(8,128)(2,1)S(1)}, bf16[800,256]{1,0:T(8,128)(2,1)S(1)}, u32[]{:S(2)}, u32[]{:S(2)}) collective-permute-start(bf16[800,256]{1,0:T(8,128)(2,1)S(1)} %pad_maximum_fusion.refs_0_), channel_id=1, source_target_pairs={{0,66},{1,67},{2,64},{3,65},{4,70},{5,71},{6,68},{7,69},{8,74},{9,... | collective-permute-start | bytes 1228808 | tf_op jit(solution)/shard_map/ppermute | solution.py:252
  6.9 17.9 %all-to-all-start = ((bf16[16,2,32,256]{3,2,1,0:T(8,128)(2,1)}), bf16[16,2,32,256]{3,2,1,0:T(8,128)(2,1)S(1)}, u32[]{:S(2)}, u32[]{:S(2)}) async-start(bf16[16,2,32,256]{3,2,1,0:T(8,128)(2,1)} %broadcast_in_dim.10), calls=%async_computation | async-start | bytes 1048576 | tf_op jit(solution)/shard_map/all_to_all | solution.py:260
  14.7 10.1 %collective-permute-start.2 = (bf16[800,256]{1,0:T(8,128)(2,1)S(1)}, bf16[800,256]{1,0:T(8,128)(2,1)S(1)}, u32[]{:S(2)}, u32[]{:S(2)}) collective-permute-start(bf16[800,256]{1,0:T(8,128)(2,1)S(1)} %collective-permute-done.1.refs_0_), channel_id=1, source_target_pairs={{0,1},{1,0},{2,3},{3,2},{4,5},{5,4},{6,7},{7,6},{8,9},{9,8},{10,11... | collective-permute-start | bytes 1228808 | tf_op jit(solution)/shard_map/ppermute | solution.py:252
  16.3 8.5 %collective-permute-start.4 = (bf16[800,256]{1,0:T(8,128)(2,1)S(1)}, bf16[800,256]{1,0:T(8,128)(2,1)S(1)}, u32[]{:S(2)}, u32[]{:S(2)}) collective-permute-start(bf16[800,256]{1,0:T(8,128)(2,1)S(1)} %collective-permute-done.3.refs_2_), channel_id=1, source_target_pairs={{0,1},{1,0},{2,3},{3,2},{4,5},{5,4},{6,7},{7,6},{8,9},{9,8},{10,11... | collective-permute-start | bytes 1228808 | tf_op jit(solution)/shard_map/ppermute | solution.py:252
  17.4 36.7 %collective-permute-start.5 = (bf16[800,256]{1,0:T(8,128)(2,1)S(1)}, bf16[800,256]{1,0:T(8,128)(2,1)S(1)}, u32[]{:S(2)}, u32[]{:S(2)}) collective-permute-start(bf16[800,256]{1,0:T(8,128)(2,1)S(1)} %collective-permute-done.1.refs_0_), channel_id=1, source_target_pairs={{0,66},{1,67},{2,64},{3,65},{4,70},{5,71},{6,68},{7,69},{8,74},{9,... | collective-permute-start | bytes 1228808 | tf_op jit(solution)/shard_map/ppermute | solution.py:252
  32.3 22.7 %collective-permute-start.8 = (bf16[800,256]{1,0:T(8,128)(2,1)S(1)}, bf16[800,256]{1,0:T(8,128)(2,1)S(1)}, u32[]{:S(2)}, u32[]{:S(2)}) collective-permute-start(bf16[800,256]{1,0:T(8,128)(2,1)S(1)} %get-tuple-element.27), channel_id=1, source_target_pairs={{0,1},{1,0},{2,3},{3,2},{4,5},{5,4},{6,7},{7,6},{8,9},{9,8},{10,11... | collective-permute-start | bytes 1228808 | tf_op jit(solution)/shard_map/ppermute | solution.py:252
  53.6 2.0 %collective-permute-start.7 = (bf16[800,256]{1,0:T(8,128)(2,1)S(1)}, bf16[800,256]{1,0:T(8,128)(2,1)S(1)}, u32[]{:S(2)}, u32[]{:S(2)}) collective-permute-start(bf16[800,256]{1,0:T(8,128)(2,1)S(1)} %get-tuple-element.25), channel_id=1, source_target_pairs={{0,1},{1,0},{2,3},{3,2},{4,5},{5,4},{6,7},{7,6},{8,9},{9,8},{10,11... | collective-permute-start | bytes 1228808 | tf_op jit(solution)/shard_map/ppermute | solution.py:252
  53.7 17.5 %collective-permute-start = (bf16[800,256]{1,0:T(8,128)(2,1)S(1)}, bf16[800,256]{1,0:T(8,128)(2,1)S(1)}, u32[]{:S(2)}, u32[]{:S(2)}) collective-permute-start(bf16[800,256]{1,0:T(8,128)(2,1)S(1)} %pad_maximum_fusion.refs_0_), channel_id=1, source_target_pairs={{0,1},{1,0},{2,3},{3,2},{4,5},{5,4},{6,7},{7,6},{8,9},{9,8},{10,11... | collective-permute-start | bytes 1228808 | tf_op jit(solution)/shard_map/ppermute | solution.py:252
  54.1 2.6 %collective-permute-start.6 = (bf16[800,256]{1,0:T(8,128)(2,1)S(1)}, bf16[800,256]{1,0:T(8,128)(2,1)S(1)}, u32[]{:S(2)}, u32[]{:S(2)}) collective-permute-start(bf16[800,256]{1,0:T(8,128)(2,1)S(1)} %collective-permute-done.5.refs_0_), channel_id=1, source_target_pairs={{0,1},{1,0},{2,3},{3,2},{4,5},{5,4},{6,7},{7,6},{8,9},{9,8},{10,11... | collective-permute-start | bytes 1228808 | tf_op jit(solution)/shard_map/ppermute | solution.py:252
  55.6 30.2 %collective-permute-start.10 = (bf16[800,256]{1,0:T(8,128)(2,1)S(1)}, bf16[800,256]{1,0:T(8,128)(2,1)S(1)}, u32[]{:S(2)}, u32[]{:S(2)}) collective-permute-start(bf16[800,256]{1,0:T(8,128)(2,1)S(1)} %add_convert_fusion.2), channel_id=1, source_target_pairs={{0,2},{1,3},{2,0},{3,1},{4,6},{5,7},{6,4},{7,5},{8,10},{9,11},{10,... | collective-permute-start | bytes 1228808 | tf_op jit(solution)/shard_map/ppermute | solution.py:252
  55.7 30.1 %collective-permute-start.11 = (bf16[800,256]{1,0:T(8,128)(2,1)S(1)}, bf16[800,256]{1,0:T(8,128)(2,1)S(1)}, u32[]{:S(2)}, u32[]{:S(2)}) collective-permute-start(bf16[800,256]{1,0:T(8,128)(2,1)S(1)} %add_convert_fusion.1), channel_id=1, source_target_pairs={{0,66},{1,67},{2,64},{3,65},{4,70},{5,71},{6,68},{7,69},{8,74},{9,... | collective-permute-start | bytes 1228808 | tf_op jit(solution)/shard_map/ppermute | solution.py:252
  60.7 25.1 %collective-permute-start.12 = (bf16[800,256]{1,0:T(8,128)(2,1)S(1)}, bf16[800,256]{1,0:T(8,128)(2,1)S(1)}, u32[]{:S(2)}, u32[]{:S(2)}) collective-permute-start(bf16[800,256]{1,0:T(8,128)(2,1)S(1)} %get-tuple-element.41), channel_id=1, source_target_pairs={{0,1},{1,0},{2,3},{3,2},{4,5},{5,4},{6,7},{7,6},{8,9},{9,8},{10,11... | collective-permute-start | bytes 1228808 | tf_op jit(solution)/shard_map/ppermute | solution.py:252
  76.4 12.0 %collective-permute-start.9 = (bf16[800,256]{1,0:T(8,128)(2,1)S(1)}, bf16[800,256]{1,0:T(8,128)(2,1)S(1)}, u32[]{:S(2)}, u32[]{:S(2)}) collective-permute-start(bf16[800,256]{1,0:T(8,128)(2,1)S(1)} %get-tuple-element.32), channel_id=1, source_target_pairs={{0,1},{1,0},{2,3},{3,2},{4,5},{5,4},{6,7},{7,6},{8,9},{9,8},{10,11... | collective-permute-start | bytes 1228808 | tf_op jit(solution)/shard_map/ppermute | solution.py:252
  85.9 12.8 %collective-permute-start.13 = (bf16[800,256]{1,0:T(8,128)(2,1)S(1)}, bf16[800,256]{1,0:T(8,128)(2,1)}, u32[]{:S(2)}, u32[]{:S(2)}) collective-permute-start(bf16[800,256]{1,0:T(8,128)(2,1)S(1)} %add_convert_fusion), channel_id=1, source_target_pairs={{0,64},{1,65},{2,66},{3,67},{4,68},{5,69},{6,70},{7,71},{8,72},{9,... | collective-permute-start | bytes 1228808 | tf_op jit(solution)/shard_map/ppermute | solution.py:252
  88.4 14.6 %all-to-all-start.1 = ((bf16[16,2,32,256]{3,2,1,0:T(8,128)(2,1)}), bf16[16,2,32,256]{3,2,1,0:T(8,128)(2,1)S(1)}, u32[]{:S(2)}, u32[]{:S(2)}) async-start(bf16[16,2,32,256]{3,2,1,0:T(8,128)(2,1)} %bitcast.3), calls=%async_computation.1 | async-start | bytes 1048576 | tf_op jit(solution)/shard_map/all_to_all | solution.py:303

commit v6 on v5

--- a/solution.py
+++ b/solution.py
@@ -11,7 +11,7 @@
 LOGIT_BIAS = -25.5
 LOG2E = 1.4426950408889634
 EXTRA = 16
-CHUNK = 1024
+CHUNK = 256
 AXES = ("blk", "grp")
 CORE, X_LOW, X_HIGH = 1, 2, 64
 CLASS = CORE | X_LOW | X_HIGH
@@ -234,7 +234,7 @@
         ),
         out_shape=out_shape,
         scratch_shapes=scratch,
-        compiler_params=pltpu.CompilerParams(vmem_limit_bytes=(22 + 12 * (count - 1)) * 2**20),
+        compiler_params=pltpu.CompilerParams(vmem_limit_bytes=(17 + 11 * (count - 1)) * 2**20),
     )(*operands)
 
 

time: 104 us -> 108 us (1.038)
  starting transfers between devices: 65 us -> 69 us
    ppermute x14, starting transfers between devices: 53.6 us -> 57.7 us  [swapped(): return lax.ppermute(x, AXES, [(i, i ^ bits) for i in range(devices)])]
where the time goes in v6:
time: 108 us
  starting transfers between devices  69 us (64%)
  Pallas kernels  16.7 us (15%)
  waiting for transfers between devices  14.9 us (14%)
  local copies, waits for them, and re-layouts  3.3 us (3%)
  other arithmetic  3.05 us (3%)
    ppermute x14, starting transfers between devices, swapped(): return lax.ppermute(x, AXES, [(i, i ^ bits) for i in range(devices)])  57.7 us
    pallas_call x3, Pallas kernels, pair_call(): pl.pallas_call(functools.partial(pair_kernel, count=count, chunk=chunk, i...  16.7 us
    all_to_all x2, starting transfers between devices, body(): lax.all_to_all(sent, AXES, 0, 0, tiled=True, axis_index_groups=across_texts)  11.3 us
    ppermute x14, waiting for transfers between devices, swapped(): return lax.ppermute(x, AXES, [(i, i ^ bits) for i in range(devices)])  8.1 us
    all_to_all x2, waiting for transfers between devices, body(): lax.all_to_all(sent, AXES, 0, 0, tiled=True, axis_index_groups=across_texts)  6.84 us
  transfers between devices with their start and end apart: 16, of which 6 were waited for; matrix products, arithmetic and copies ran while one was open for 4% of the time, Pallas kernels for 16%

profile of v6, /device:TPU:1, one launch (start us, length us, event | category | flops | bytes accessed | tf_op | source)
XLA Modules:
  0.0 107.8 jit_solution(18124914818314808384)
XLA Ops:
  0.6 1.1 %reshape.64 = bf16[784,256]{1,0:T(8,128)(2,1)S(1)} reshape(bf16[196,4,256]{2,1,0:T(4,128)(2,1)} %bitcast.6) | data formatting | bytes 802816 | tf_op jit(solution)/shard_map/reshape | solution.py:255
  1.8 0.1 reshape.69
  1.9 0.1 pad.1.clone
  1.9 0.2 pad_maximum_fusion.refs_0_
  2.1 2.1 %collective-permute-start.1 = (bf16[800,256]{1,0:T(8,128)(2,1)S(1)}, bf16[800,256]{1,0:T(8,128)(2,1)S(1)}, u32[]{:S(2)}, u32[]{:S(2)}) collective-permute-start(bf16[800,256]{1,0:T(8,128)(2,1)S(1)} %pad_maximum_fusion.refs_0_), channel_id=1, source_target_pairs={{0,2},{1,3},{2,0},{3,1},{4,6},{5,7},{6,4},{7,5},{8,10},{9,11},{10,... | collective-permute-start | bytes 1228808 | tf_op jit(solution)/shard_map/ppermute | solution.py:252
  4.2 1.8 %collective-permute-start.3 = (bf16[800,256]{1,0:T(8,128)(2,1)S(1)}, bf16[800,256]{1,0:T(8,128)(2,1)S(1)}, u32[]{:S(2)}, u32[]{:S(2)}) collective-permute-start(bf16[800,256]{1,0:T(8,128)(2,1)S(1)} %pad_maximum_fusion.refs_0_), channel_id=1, source_target_pairs={{0,66},{1,67},{2,64},{3,65},{4,70},{5,71},{6,68},{7,69},{8,74},{9,... | collective-permute-start | bytes 1228808 | tf_op jit(solution)/shard_map/ppermute | solution.py:252
  6.1 0.9 broadcast_in_dim.10
  6.9 7.8 %all-to-all-start = ((bf16[16,2,32,256]{3,2,1,0:T(8,128)(2,1)}), bf16[16,2,32,256]{3,2,1,0:T(8,128)(2,1)S(1)}, u32[]{:S(2)}, u32[]{:S(2)}) async-start(bf16[16,2,32,256]{3,2,1,0:T(8,128)(2,1)} %broadcast_in_dim.10), calls=%async_computation | async-start | bytes 1048576 | tf_op jit(solution)/shard_map/all_to_all | solution.py:260
  14.7 0.0 collective-permute-done.1.refs_0_
  14.7 1.6 %collective-permute-start.2 = (bf16[800,256]{1,0:T(8,128)(2,1)S(1)}, bf16[800,256]{1,0:T(8,128)(2,1)S(1)}, u32[]{:S(2)}, u32[]{:S(2)}) collective-permute-start(bf16[800,256]{1,0:T(8,128)(2,1)S(1)} %collective-permute-done.1.refs_0_), channel_id=1, source_target_pairs={{0,1},{1,0},{2,3},{3,2},{4,5},{5,4},{6,7},{7,6},{8,9},{9,8},{10,11... | collective-permute-start | bytes 1228808 | tf_op jit(solution)/shard_map/ppermute | solution.py:252
  16.3 0.0 collective-permute-done.3.refs_2_
  16.3 1.0 collective-permute-start.4
  17.4 1.9 %collective-permute-start.5 = (bf16[800,256]{1,0:T(8,128)(2,1)S(1)}, bf16[800,256]{1,0:T(8,128)(2,1)S(1)}, u32[]{:S(2)}, u32[]{:S(2)}) collective-permute-start(bf16[800,256]{1,0:T(8,128)(2,1)S(1)} %collective-permute-done.1.refs_0_), channel_id=1, source_target_pairs={{0,66},{1,67},{2,64},{3,65},{4,70},{5,71},{6,68},{7,69},{8,74},{9,... | collective-permute-start | bytes 1228808 | tf_op jit(solution)/shard_map/ppermute | solution.py:252
  19.2 5.6 %all-to-all-done = bf16[16,2,32,256]{3,2,1,0:T(8,128)(2,1)S(1)} async-done(((bf16[16,2,32,256]{3,2,1,0:T(8,128)(2,1)}), bf16[16,2,32,256]{3,2,1,0:T(8,128)(2,1)S(1)}, u32[]{:S(2)}, u32[]{:S(2)}) %all-to-all-start) | async-done | bytes 524320 | tf_op jit(solution)/shard_map/all_to_all | solution.py:260
  24.8 0.0 collective-permute-done.2.refs_1_
  24.8 0.0 collective-permute-done.4.refs_3_
  24.8 7.3 %shard_map.58 = (f32[800,256]{1,0:T(8,128)S(1)}, bf16[800,256]{1,0:T(8,128)(2,1)S(1)}, f32[800,256]{1,0:T(8,128)S(1)}, bf16[800,256]{1,0:T(8,128)(2,1)S(1)}, f32...) custom-call(bf16[800,256]{1,0:T(8,128)(2,1)S(1)} %collective-permute-done.1.refs_0_, ...), custom_call_target="tpu_custom_call" | custom-call | tf_op jit(solution)/shard_map/pallas_call | solution.py:231
  32.2 23.3 %collective-permute-start.8 = (bf16[800,256]{1,0:T(8,128)(2,1)S(1)}, bf16[800,256]{1,0:T(8,128)(2,1)S(1)}, u32[]{:S(2)}, u32[]{:S(2)}) collective-permute-start(bf16[800,256]{1,0:T(8,128)(2,1)S(1)} %get-tuple-element.27), channel_id=1, source_target_pairs={{0,1},{1,0},{2,3},{3,2},{4,5},{5,4},{6,7},{7,6},{8,9},{9,8},{10,11... | collective-permute-start | bytes 1228808 | tf_op jit(solution)/shard_map/ppermute | solution.py:252
  55.5 0.1 collective-permute-start.7
  55.6 0.4 collective-permute-start
  56.0 0.0 collective-permute-done.5.refs_0_
  56.0 0.1 collective-permute-start.6
  56.1 0.8 collective-permute-done.8
  56.8 0.1 add_convert_fusion.1
  56.9 0.5 collective-permute-done.7
  57.4 0.1 add_convert_fusion.2
  57.5 0.1 collective-permute-start.10
  57.6 0.9 collective-permute-start.11
  58.5 0.1 collective-permute-done.6.refs_1_
  58.6 4.1 %shard_map.59 = (f32[800,256]{1,0:T(8,128)S(1)}, bf16[800,256]{1,0:T(8,128)(2,1)S(1)}, f32[256,1024]{1,0:T(8,128)S(1)}) custom-call(bf16[800,256]{1,0:T(8,128)(2,1)S(1)} %collective-permute-done.5.refs_0_, bf16[800,256]{1,0:T(8,128)(2,1)S(1)} %collective-permute-done.6.refs_1_, bf16[1024,256]{1,0:T(8,128)(2,1)S(1)} %get-tuple-element.23.refs_2_, ...), custom_call_target="tpu_custom_call" | custom-call | tf_op jit(solution)/shard_map/pallas_call | solution.py:231
  62.7 11.4 %collective-permute-start.12 = (bf16[800,256]{1,0:T(8,128)(2,1)S(1)}, bf16[800,256]{1,0:T(8,128)(2,1)S(1)}, u32[]{:S(2)}, u32[]{:S(2)}) collective-permute-start(bf16[800,256]{1,0:T(8,128)(2,1)S(1)} %get-tuple-element.41), channel_id=1, source_target_pairs={{0,1},{1,0},{2,3},{3,2},{4,5},{5,4},{6,7},{7,6},{8,9},{9,8},{10,11... | collective-permute-start | bytes 1228808 | tf_op jit(solution)/shard_map/ppermute | solution.py:252
  74.1 0.0 collective-permute-done.refs_1_
  74.1 5.3 %shard_map.60 = (f32[800,256]{1,0:T(8,128)S(1)}, bf16[800,256]{1,0:T(8,128)(2,1)S(1)}, bf16[1024,256]{1,0:T(8,128)(2,1)}) custom-call(bf16[800,256]{1,0:T(8,128)(2,1)S(1)} %pad_maximum_fusion.refs_0_, bf16[800,256]{1,0:T(8,128)(2,1)S(1)} %collective-permute-done.refs_1_, bf16[1024,256]{1,0:T(8,128)(2,1)S(1)} %get-tuple-element.23.refs_2_, ...), custom_call_target="tpu_custom_call" | custom-call | tf_op jit(solution)/shard_map/pallas_call | solution.py:231
  79.4 10.5 %collective-permute-start.9 = (bf16[800,256]{1,0:T(8,128)(2,1)S(1)}, bf16[800,256]{1,0:T(8,128)(2,1)S(1)}, u32[]{:S(2)}, u32[]{:S(2)}) collective-permute-start(bf16[800,256]{1,0:T(8,128)(2,1)S(1)} %get-tuple-element.32), channel_id=1, source_target_pairs={{0,1},{1,0},{2,3},{3,2},{4,5},{5,4},{6,7},{7,6},{8,9},{9,8},{10,11... | collective-permute-start | bytes 1228808 | tf_op jit(solution)/shard_map/ppermute | solution.py:252
  89.9 0.0 collective-permute-done.10
  89.9 0.0 collective-permute-done.11
  89.9 0.0 collective-permute-done.12
  89.9 0.1 add_convert_fusion
  90.0 2.4 %collective-permute-start.13 = (bf16[800,256]{1,0:T(8,128)(2,1)S(1)}, bf16[800,256]{1,0:T(8,128)(2,1)}, u32[]{:S(2)}, u32[]{:S(2)}) collective-permute-start(bf16[800,256]{1,0:T(8,128)(2,1)S(1)} %add_convert_fusion), channel_id=1, source_target_pairs={{0,64},{1,65},{2,66},{3,67},{4,68},{5,69},{6,70},{7,71},{8,72},{9,... | collective-permute-start | bytes 1228808 | tf_op jit(solution)/shard_map/ppermute | solution.py:252
  92.4 0.0 collective-permute-done.9
  92.4 3.6 %all-to-all-start.1 = ((bf16[16,2,32,256]{3,2,1,0:T(8,128)(2,1)}), bf16[16,2,32,256]{3,2,1,0:T(8,128)(2,1)S(1)}, u32[]{:S(2)}, u32[]{:S(2)}) async-start(bf16[16,2,32,256]{3,2,1,0:T(8,128)(2,1)} %bitcast.3), calls=%async_computation.1 | async-start | bytes 1048576 | tf_op jit(solution)/shard_map/all_to_all | solution.py:303
  96.0 6.8 %collective-permute-done.13 = bf16[800,256]{1,0:T(8,128)(2,1)} collective-permute-done((bf16[800,256]{1,0:T(8,128)(2,1)S(1)}, bf16[800,256]{1,0:T(8,128)(2,1)}, u32[]{:S(2)}, u32[]{:S(2)}) %collective-permute-start.13) | collective-permute-done | bytes 409632 | tf_op jit(solution)/shard_map/ppermute | solution.py:252
  102.8 1.2 %convert_add_fusion = f32[800,256]{1,0:T(8,128)S(1)} fusion(bf16[800,256]{1,0:T(8,128)(2,1)} %collective-permute-done.13, bf16[800,256]{1,0:T(8,128)(2,1)S(1)} %collective-permute-done.11, bf16[800,256]{1,0:T(8,128)(2,1)S(1)} %collective-permute-done.10, f32[800,256]{1,0:T(8,128)S(1)} %get-tuple-element.31, bf16[800,256]{1,0:T(8,128)(2,1)S(1)} %collective-permute-done.9), kind=kLoop, calls=%fused_computation.1 | loop fusion | flops 1638400 | bytes 3276800 | tf_op jit(solution)/shard_map/add | solution.py:298
  104.0 0.1 slice.24
  104.1 1.1 %reshape.66 = f32[196,4,256]{2,1,0:T(4,128)} reshape(f32[784,256]{1,0:T(8,128)S(1)} %slice.24) | data formatting | bytes 1605632 | tf_op jit(solution)/shard_map/reshape | solution.py:299
  105.2 0.6 fusion
  105.8 1.3 %all-to-all-done.1 = bf16[16,2,32,256]{3,2,1,0:T(8,128)(2,1)S(1)} async-done(((bf16[16,2,32,256]{3,2,1,0:T(8,128)(2,1)}), bf16[16,2,32,256]{3,2,1,0:T(8,128)(2,1)S(1)}, u32[]{:S(2)}, u32[]{:S(2)}) %all-to-all-start.1) | async-done | bytes 524320 | tf_op jit(solution)/shard_map/all_to_all | solution.py:303
  107.1 0.7 convert_reduce_fusion
  (8 shorter events, 0.0 us)
Async XLA Ops:
  0.6 1.1 %copy-start.1 = (s32[4]{0:T(128)S(1)}, s32[4]{0:T(128)}, u32[]{:S(2)}) copy-start(s32[4]{0:T(128)} %param.5) | copy-start | bytes 52
  1.9 4.1 %copy-start = (bf16[2,32,256]{2,1,0:T(8,128)(2,1)S(1)}, bf16[2,32,256]{2,1,0:T(8,128)(2,1)}, u32[]{:S(2)}) copy-start(bf16[2,32,256]{2,1,0:T(8,128)(2,1)} %param.4) | copy-start | bytes 98308
  2.1 12.6 %collective-permute-start.1 = (bf16[800,256]{1,0:T(8,128)(2,1)S(1)}, bf16[800,256]{1,0:T(8,128)(2,1)S(1)}, u32[]{:S(2)}, u32[]{:S(2)}) collective-permute-start(bf16[800,256]{1,0:T(8,128)(2,1)S(1)} %pad_maximum_fusion.refs_0_), channel_id=1, source_target_pairs={{0,2},{1,3},{2,0},{3,1},{4,6},{5,7},{6,4},{7,5},{8,10},{9,11},{10,... | collective-permute-start | bytes 1228808 | tf_op jit(solution)/shard_map/ppermute | solution.py:252
  4.2 12.1 %collective-permute-start.3 = (bf16[800,256]{1,0:T(8,128)(2,1)S(1)}, bf16[800,256]{1,0:T(8,128)(2,1)S(1)}, u32[]{:S(2)}, u32[]{:S(2)}) collective-permute-start(bf16[800,256]{1,0:T(8,128)(2,1)S(1)} %pad_maximum_fusion.refs_0_), channel_id=1, source_target_pairs={{0,66},{1,67},{2,64},{3,65},{4,70},{5,71},{6,68},{7,69},{8,74},{9,... | collective-permute-start | bytes 1228808 | tf_op jit(solution)/shard_map/ppermute | solution.py:252
  6.9 17.9 %all-to-all-start = ((bf16[16,2,32,256]{3,2,1,0:T(8,128)(2,1)}), bf16[16,2,32,256]{3,2,1,0:T(8,128)(2,1)S(1)}, u32[]{:S(2)}, u32[]{:S(2)}) async-start(bf16[16,2,32,256]{3,2,1,0:T(8,128)(2,1)} %broadcast_in_dim.10), calls=%async_computation | async-start | bytes 1048576 | tf_op jit(solution)/shard_map/all_to_all | solution.py:260
  14.7 10.1 %collective-permute-start.2 = (bf16[800,256]{1,0:T(8,128)(2,1)S(1)}, bf16[800,256]{1,0:T(8,128)(2,1)S(1)}, u32[]{:S(2)}, u32[]{:S(2)}) collective-permute-start(bf16[800,256]{1,0:T(8,128)(2,1)S(1)} %collective-permute-done.1.refs_0_), channel_id=1, source_target_pairs={{0,1},{1,0},{2,3},{3,2},{4,5},{5,4},{6,7},{7,6},{8,9},{9,8},{10,11... | collective-permute-start | bytes 1228808 | tf_op jit(solution)/shard_map/ppermute | solution.py:252
  16.3 8.5 %collective-permute-start.4 = (bf16[800,256]{1,0:T(8,128)(2,1)S(1)}, bf16[800,256]{1,0:T(8,128)(2,1)S(1)}, u32[]{:S(2)}, u32[]{:S(2)}) collective-permute-start(bf16[800,256]{1,0:T(8,128)(2,1)S(1)} %collective-permute-done.3.refs_2_), channel_id=1, source_target_pairs={{0,1},{1,0},{2,3},{3,2},{4,5},{5,4},{6,7},{7,6},{8,9},{9,8},{10,11... | collective-permute-start | bytes 1228808 | tf_op jit(solution)/shard_map/ppermute | solution.py:252
  17.4 38.6 %collective-permute-start.5 = (bf16[800,256]{1,0:T(8,128)(2,1)S(1)}, bf16[800,256]{1,0:T(8,128)(2,1)S(1)}, u32[]{:S(2)}, u32[]{:S(2)}) collective-permute-start(bf16[800,256]{1,0:T(8,128)(2,1)S(1)} %collective-permute-done.1.refs_0_), channel_id=1, source_target_pairs={{0,66},{1,67},{2,64},{3,65},{4,70},{5,71},{6,68},{7,69},{8,74},{9,... | collective-permute-start | bytes 1228808 | tf_op jit(solution)/shard_map/ppermute | solution.py:252
  32.2 24.7 %collective-permute-start.8 = (bf16[800,256]{1,0:T(8,128)(2,1)S(1)}, bf16[800,256]{1,0:T(8,128)(2,1)S(1)}, u32[]{:S(2)}, u32[]{:S(2)}) collective-permute-start(bf16[800,256]{1,0:T(8,128)(2,1)S(1)} %get-tuple-element.27), channel_id=1, source_target_pairs={{0,1},{1,0},{2,3},{3,2},{4,5},{5,4},{6,7},{7,6},{8,9},{9,8},{10,11... | collective-permute-start | bytes 1228808 | tf_op jit(solution)/shard_map/ppermute | solution.py:252
  55.5 2.0 %collective-permute-start.7 = (bf16[800,256]{1,0:T(8,128)(2,1)S(1)}, bf16[800,256]{1,0:T(8,128)(2,1)S(1)}, u32[]{:S(2)}, u32[]{:S(2)}) collective-permute-start(bf16[800,256]{1,0:T(8,128)(2,1)S(1)} %get-tuple-element.25), channel_id=1, source_target_pairs={{0,1},{1,0},{2,3},{3,2},{4,5},{5,4},{6,7},{7,6},{8,9},{9,8},{10,11... | collective-permute-start | bytes 1228808 | tf_op jit(solution)/shard_map/ppermute | solution.py:252
  55.6 18.5 %collective-permute-start = (bf16[800,256]{1,0:T(8,128)(2,1)S(1)}, bf16[800,256]{1,0:T(8,128)(2,1)S(1)}, u32[]{:S(2)}, u32[]{:S(2)}) collective-permute-start(bf16[800,256]{1,0:T(8,128)(2,1)S(1)} %pad_maximum_fusion.refs_0_), channel_id=1, source_target_pairs={{0,1},{1,0},{2,3},{3,2},{4,5},{5,4},{6,7},{7,6},{8,9},{9,8},{10,11... | collective-permute-start | bytes 1228808 | tf_op jit(solution)/shard_map/ppermute | solution.py:252
  56.0 2.6 %collective-permute-start.6 = (bf16[800,256]{1,0:T(8,128)(2,1)S(1)}, bf16[800,256]{1,0:T(8,128)(2,1)S(1)}, u32[]{:S(2)}, u32[]{:S(2)}) collective-permute-start(bf16[800,256]{1,0:T(8,128)(2,1)S(1)} %collective-permute-done.5.refs_0_), channel_id=1, source_target_pairs={{0,1},{1,0},{2,3},{3,2},{4,5},{5,4},{6,7},{7,6},{8,9},{9,8},{10,11... | collective-permute-start | bytes 1228808 | tf_op jit(solution)/shard_map/ppermute | solution.py:252
  57.5 32.3 %collective-permute-start.10 = (bf16[800,256]{1,0:T(8,128)(2,1)S(1)}, bf16[800,256]{1,0:T(8,128)(2,1)S(1)}, u32[]{:S(2)}, u32[]{:S(2)}) collective-permute-start(bf16[800,256]{1,0:T(8,128)(2,1)S(1)} %add_convert_fusion.2), channel_id=1, source_target_pairs={{0,2},{1,3},{2,0},{3,1},{4,6},{5,7},{6,4},{7,5},{8,10},{9,11},{10,... | collective-permute-start | bytes 1228808 | tf_op jit(solution)/shard_map/ppermute | solution.py:252
  57.6 32.3 %collective-permute-start.11 = (bf16[800,256]{1,0:T(8,128)(2,1)S(1)}, bf16[800,256]{1,0:T(8,128)(2,1)S(1)}, u32[]{:S(2)}, u32[]{:S(2)}) collective-permute-start(bf16[800,256]{1,0:T(8,128)(2,1)S(1)} %add_convert_fusion.1), channel_id=1, source_target_pairs={{0,66},{1,67},{2,64},{3,65},{4,70},{5,71},{6,68},{7,69},{8,74},{9,... | collective-permute-start | bytes 1228808 | tf_op jit(solution)/shard_map/ppermute | solution.py:252
  62.7 27.2 %collective-permute-start.12 = (bf16[800,256]{1,0:T(8,128)(2,1)S(1)}, bf16[800,256]{1,0:T(8,128)(2,1)S(1)}, u32[]{:S(2)}, u32[]{:S(2)}) collective-permute-start(bf16[800,256]{1,0:T(8,128)(2,1)S(1)} %get-tuple-element.41), channel_id=1, source_target_pairs={{0,1},{1,0},{2,3},{3,2},{4,5},{5,4},{6,7},{7,6},{8,9},{9,8},{10,11... | collective-permute-start | bytes 1228808 | tf_op jit(solution)/shard_map/ppermute | solution.py:252
  79.4 13.0 %collective-permute-start.9 = (bf16[800,256]{1,0:T(8,128)(2,1)S(1)}, bf16[800,256]{1,0:T(8,128)(2,1)S(1)}, u32[]{:S(2)}, u32[]{:S(2)}) collective-permute-start(bf16[800,256]{1,0:T(8,128)(2,1)S(1)} %get-tuple-element.32), channel_id=1, source_target_pairs={{0,1},{1,0},{2,3},{3,2},{4,5},{5,4},{6,7},{7,6},{8,9},{9,8},{10,11... | collective-permute-start | bytes 1228808 | tf_op jit(solution)/shard_map/ppermute | solution.py:252
  90.0 12.8 %collective-permute-start.13 = (bf16[800,256]{1,0:T(8,128)(2,1)S(1)}, bf16[800,256]{1,0:T(8,128)(2,1)}, u32[]{:S(2)}, u32[]{:S(2)}) collective-permute-start(bf16[800,256]{1,0:T(8,128)(2,1)S(1)} %add_convert_fusion), channel_id=1, source_target_pairs={{0,64},{1,65},{2,66},{3,67},{4,68},{5,69},{6,70},{7,71},{8,72},{9,... | collective-permute-start | bytes 1228808 | tf_op jit(solution)/shard_map/ppermute | solution.py:252
  92.4 14.6 %all-to-all-start.1 = ((bf16[16,2,32,256]{3,2,1,0:T(8,128)(2,1)}), bf16[16,2,32,256]{3,2,1,0:T(8,128)(2,1)S(1)}, u32[]{:S(2)}, u32[]{:S(2)}) async-start(bf16[16,2,32,256]{3,2,1,0:T(8,128)(2,1)} %bitcast.3), calls=%async_computation.1 | async-start | bytes 1048576 | tf_op jit(solution)/shard_map/all_to_all | solution.py:303
